TPU v7x, 32 devices: a whole 2x2x4 slice. The times are simulated.
32 devices in a mesh: img: 4 (over y, core), tile: 8 (over z, x).
Axes of the slice: x: 2, y: 2, z: 4, core: 2. Of those that a mesh axis runs over, the one named last changes fastest.
Arguments:
- features: bfloat16 [8, 64, 160, 256], P('img', 'tile'), may hold values from -6 to 6
- conv_weight: float32 [2560, 256], replicated, may hold values from -0.21875 to 0.21875
- conv_first: float32 [2560, 256], replicated, may hold values from -0.0029296875 to 0.0029296875
- conv_second: float32 [2560, 256], replicated, may hold values from 3.6621093e-09 to 1.4648437e-08
- head_weight: float32 [3, 1024, 85], replicated, may hold values from -0.375 to 0.375
- head_first: float32 [3, 1024, 85], replicated, may hold values from -0.0048828125 to 0.0048828125
- head_second: float32 [3, 1024, 85], replicated, may hold values from 1.0986328e-08 to 4.3945313e-08
- bias_vector: float32 [6911], replicated, may hold values from -0.3 to 0.3
- bias_first: float32 [6911], replicated, may hold values from -0.0048828125 to 0.0048828125
- bias_second: float32 [6911], replicated, may hold values from 1.0986328e-08 to 4.3945313e-08
- block_master: float32 [1280, 32, 1024], P(('img', 'tile')), may hold values from -0.109375 to 0.109375
- block_first: float32 [1280, 32, 1024], P(('img', 'tile')), may hold values from -0.0017089844 to 0.0017089844
- block_second: float32 [1280, 32, 1024], P(('img', 'tile')), may hold values from 1.2207031e-09 to 4.8828124e-09
- slot_block: int32 [1280], replicated, may hold values from -1 to 1271, as said below
- roi_image: int32 [8192], P(('img', 'tile')), may hold values from 0 to 1
- corner_index: int32 [3, 49, 8192], P(None, None, ('img', 'tile')), may hold values from 0 to 1758, as said below
- corner_frac: float32 [3, 2, 49, 8192], P(None, None, None, ('img', 'tile')), may hold values from 0 to 1
- labels: int32 [3, 8192], P(None, ('img', 'tile')), may hold values from 0 to 80
- valid: int32 [8192], P(('img', 'tile')), may hold values from 0 to 1, as said below
- box_deltas: float32 [3, 4, 8192], P(None, None, ('img', 'tile')), may hold values from -0.6 to 0.6
Outputs:
- loss: float32 [1], replicated
- conv_new: float32 [2560, 256], replicated
- conv_first_new: float32 [2560, 256], replicated
- conv_second_new: float32 [2560, 256], replicated
- head_new: float32 [3, 1024, 85], replicated
- head_first_new: float32 [3, 1024, 85], replicated
- head_second_new: float32 [3, 1024, 85], replicated
- bias_new: float32 [6911], replicated
- bias_first_new: float32 [6911], replicated
- bias_second_new: float32 [6911], replicated
- block_new: float32 [1280, 32, 1024], P(('img', 'tile'))
- block_first_new: float32 [1280, 32, 1024], P(('img', 'tile'))
- block_second_new: float32 [1280, 32, 1024], P(('img', 'tile'))
Inputs may be any that keep to these rules, and one draw needn't show every extreme that they name: `slot_block`: each of the 1272 blocks is held by exactly one slot; every other slot holds -1. `corner_index`: flat index y * 160 + x into the device's 8 + 2 * 2 padded rows of the image; x <= 158 and y <= 10; no sample point reads a row outside the image. On each device the valid slots come first; a device has 256, 128 or 64 of them, and some device has 256.
All inputs are finite; a program needn't handle non-finite values.
Results may differ from a plain program's by a relative error of at most 0.011.
Values may be sent and summed in bfloat16 or wider, within the bound.
A program may use at most 832 MiB of HBM per device.

v0:
```python
import jax
import jax.numpy as jnp
from jax import lax
from jax.sharding import PartitionSpec as P

HR = 2
STEP = 5
BINS = 49


BETA_ONE = 0.9
BETA_TWO = 0.999
RATE = 0.025
DECAY = 0.01
EPSILON = 1e-08


def padded_2(cells, sides, width):
    for axis, dim in sides:
        count = lax.axis_size(axis)
        ends = count - 1
        head = lax.slice_in_dim(cells, 0, width, axis=dim)
        tail = lax.slice_in_dim(cells, cells.shape[dim] - width, cells.shape[dim], axis=dim)
        cells = jnp.concatenate(
            [
                lax.ppermute(tail, axis, [(i, (i + 1) % count) for i in range(ends)]),
                cells,
                lax.ppermute(head, axis, [((i + 1) % count, i) for i in range(ends)]),
            ],
            axis=dim,
        )
    return cells


def adamw(master, first, second, grad, step):
    first_new = BETA_ONE * first + (1.0 - BETA_ONE) * grad
    second_new = BETA_TWO * second + (1.0 - BETA_TWO) * grad * grad
    first_hat = first_new / (1.0 - BETA_ONE**step)
    second_hat = second_new / (1.0 - BETA_TWO**step)
    master_new = master - RATE * (first_hat / (jnp.sqrt(second_hat) + EPSILON) + DECAY * master)
    return (master_new, first_new, second_new)


def silu_slope(value):
    sigmoid = jax.nn.sigmoid(value)
    return sigmoid * (1.0 + value * (1.0 - sigmoid))


def convolve(padded, kernel_taps, height, breadth):
    summed = None
    for kernel_pos in range(9):
        row_shift = kernel_pos // 3
        col_shift = kernel_pos % 3
        window = padded[:, row_shift : row_shift + height, col_shift : col_shift + breadth]
        contrib = jnp.einsum(
            "ihwc,cd->ihwd", window, kernel_taps[kernel_pos], preferred_element_type=jnp.float32
        )
        summed = contrib if summed is None else summed + contrib
    return summed


def convolve_back(grad_padded, lateral_padded, grad_low, kernel_taps, height, breadth):
    grad_input = None
    tap_grads = []
    for kernel_pos in range(9):
        row_shift = kernel_pos // 3
        col_shift = kernel_pos % 3
        window = lateral_padded[:, row_shift : row_shift + height, col_shift : col_shift + breadth]
        tap_grads.append(
            jnp.einsum("ihwc,ihwd->cd", window, grad_low, preferred_element_type=jnp.float32)
        )
        source = grad_padded[
            :, 2 - row_shift : 2 - row_shift + height, 2 - col_shift : 2 - col_shift + breadth
        ]
        contrib = jnp.einsum(
            "ihwd,cd->ihwc", source, kernel_taps[kernel_pos], preferred_element_type=jnp.float32
        )
        grad_input = contrib if grad_input is None else grad_input + contrib
    return (jnp.concatenate(tap_grads, axis=0), grad_input)


def on_device(
    features,
    conv_weight,
    conv_first,
    conv_second,
    head_weight,
    head_first,
    head_second,
    bias_vector,
    bias_first,
    bias_second,
    block_master,
    block_first,
    block_second,
    slot_block,
    roi_image,
    corner_index,
    corner_frac,
    labels,
    valid,
    box_deltas,
):
    images, height, breadth, in_channels = features.shape
    channels = conv_weight.shape[1]
    section_count, hidden, out_width = head_weight.shape
    classes = out_width - 4
    slots, block_rows, _ = block_master.shape
    all_slots = slot_block.shape[0]
    region_count = roi_image.shape[0]
    rim = HR
    first_rows = BINS * channels
    section_rows = first_rows + hidden
    section_blocks = section_rows // block_rows
    block_total = section_count * section_blocks
    gathered = lax.all_gather(
        block_master.astype(jnp.bfloat16), ("img", "tile"), axis=0, tiled=True
    )
    position = jnp.arange(all_slots, dtype=jnp.int32)
    owner_slot = (
        jnp.zeros((block_total,), jnp.int32)
        .at[jnp.where(slot_block >= 0, slot_block, block_total)]
        .set(position, mode="drop")
    )
    stacked = gathered[owner_slot].reshape(section_count, section_rows, hidden)
    valid_float = valid.astype(jnp.float32)
    valid_sum = lax.psum(jnp.sum(valid_float), ("img", "tile"))
    conv_low = conv_weight.astype(jnp.bfloat16)
    lateral_w = conv_low[:in_channels]
    kernel_taps = conv_low[in_channels:].reshape(9, channels, channels)
    head_all = head_weight.astype(jnp.bfloat16)
    lateral_bias = bias_vector[:channels]
    conv_bias = bias_vector[channels : 2 * channels]
    lateral = (
        jnp.einsum("ihwc,cd->ihwd", features, lateral_w, preferred_element_type=jnp.float32)
        + lateral_bias
    ).astype(jnp.bfloat16)
    column_pad = ((0, 0), (0, 0), (1, 1), (0, 0))
    lateral_padded = jnp.pad(padded_2(lateral, (("tile", 1),), 1), column_pad)
    feature_map = (convolve(lateral_padded, kernel_taps, height, breadth) + conv_bias).astype(
        jnp.bfloat16
    )
    map_padded = padded_2(feature_map, (("tile", 1),), rim)
    padded_rows = height + 2 * rim
    flat_map = map_padded.reshape(images * padded_rows * breadth, channels)
    corner_shifts = (0, 1, breadth, breadth + 1)
    grad_flat = jnp.zeros((images * padded_rows * breadth, channels), jnp.float32)
    loss_part = jnp.zeros((), jnp.float32)
    weight_each = valid_float / valid_sum
    head_grads = []
    section_bias_grads = []
    block_term = jnp.zeros((all_slots, block_rows, hidden), jnp.float32)
    for section in range(section_count):
        first_matrix = stacked[section, :first_rows]
        second_matrix = stacked[section, first_rows:]
        head_low = head_all[section]
        offset = 2 * channels + section * (2 * hidden + out_width)
        first_bias = bias_vector[offset : offset + hidden]
        second_bias = bias_vector[offset + hidden : offset + 2 * hidden]
        head_bias = bias_vector[offset + 2 * hidden : offset + 2 * hidden + out_width]
        corner_base = roi_image[:, None] * (padded_rows * breadth) + corner_index[section].T
        frac_row = corner_frac[section, 0].T
        frac_col = corner_frac[section, 1].T
        corner_weights = (
            (1.0 - frac_row) * (1.0 - frac_col),
            (1.0 - frac_row) * frac_col,
            frac_row * (1.0 - frac_col),
            frac_row * frac_col,
        )
        pooled = None
        for corner in range(4):
            contrib = corner_weights[corner][:, :, None] * flat_map[
                corner_base + corner_shifts[corner]
            ].astype(jnp.float32)
            pooled = contrib if pooled is None else pooled + contrib
        roi_feats = pooled.reshape(region_count, first_rows).astype(jnp.bfloat16)
        first_pre = (
            jnp.dot(roi_feats, first_matrix, preferred_element_type=jnp.float32) + first_bias
        )
        first_act = jax.nn.silu(first_pre).astype(jnp.bfloat16)
        second_pre = (
            jnp.dot(first_act, second_matrix, preferred_element_type=jnp.float32) + second_bias
        )
        second_act = jax.nn.silu(second_pre).astype(jnp.bfloat16)
        outputs = jnp.dot(second_act, head_low, preferred_element_type=jnp.float32) + head_bias
        logits = outputs[:, :classes]
        shifted = logits - jnp.max(logits, axis=1, keepdims=True)
        log_total = jnp.log(jnp.sum(jnp.exp(shifted), axis=1, keepdims=True))
        one_hot = (
            labels[section][:, None] == jnp.arange(classes, dtype=jnp.int32)[None, :]
        ).astype(jnp.float32)
        cross = log_total[:, 0] - jnp.sum(shifted * one_hot, axis=1)
        foreground = (labels[section] > 0).astype(jnp.float32)
        target = box_deltas[section].T * (
            jnp.array([10.0, 10.0, 5.0, 5.0], jnp.float32) * (section + 1)
        )
        differ = outputs[:, classes:] - target
        magnitude = jnp.abs(differ)
        smooth = jnp.where(magnitude < 1.0, 0.5 * differ * differ, magnitude - 0.5)
        loss_part = loss_part + jnp.sum(
            valid_float * (cross + foreground * jnp.sum(smooth, axis=1))
        )
        probs = jnp.exp(shifted - log_total)
        grad_logits = weight_each[:, None] * (probs - one_hot)
        grad_box = (weight_each * foreground)[:, None] * jnp.clip(differ, -1.0, 1.0)
        grad_out = jnp.concatenate([grad_logits, grad_box], axis=1).astype(jnp.bfloat16)
        head_grads.append(
            jnp.einsum("rk,rf->kf", second_act, grad_out, preferred_element_type=jnp.float32)
        )
        grad_head_bias = jnp.sum(grad_out.astype(jnp.float32), axis=0)
        grad_second = (
            jnp.einsum("rf,kf->rk", grad_out, head_low, preferred_element_type=jnp.float32)
            * silu_slope(second_pre)
        ).astype(jnp.bfloat16)
        grad_second_bias = jnp.sum(grad_second.astype(jnp.float32), axis=0)
        grad_first = (
            jnp.einsum("rf,kf->rk", grad_second, second_matrix, preferred_element_type=jnp.float32)
            * silu_slope(first_pre)
        ).astype(jnp.bfloat16)
        grad_first_bias = jnp.sum(grad_first.astype(jnp.float32), axis=0)
        section_bias_grads.extend([grad_first_bias, grad_second_bias, grad_head_bias])
        grad_pooled = jnp.einsum(
            "rf,kf->rk", grad_first, first_matrix, preferred_element_type=jnp.float32
        )
        grad_pooled = grad_pooled.reshape(region_count, BINS, channels)
        for corner in range(4):
            grad_flat = grad_flat.at[corner_base + corner_shifts[corner]].add(
                corner_weights[corner][:, :, None] * grad_pooled
            )
        dense_first = jnp.einsum(
            "rk,rf->kf", roi_feats, grad_first, preferred_element_type=jnp.float32
        )
        dense_second = jnp.einsum(
            "rk,rf->kf", first_act, grad_second, preferred_element_type=jnp.float32
        )
        dense_section = jnp.concatenate([dense_first, dense_second], axis=0).reshape(
            section_blocks, block_rows, hidden
        )
        targets = lax.dynamic_slice_in_dim(owner_slot, section * section_blocks, section_blocks)
        block_term = block_term.at[targets].set(dense_section)
    grad_padded_map = grad_flat.reshape(images, padded_rows, breadth, channels)
    outer_rims = jnp.concatenate(
        [grad_padded_map[:, :rim], grad_padded_map[:, rim + height :]], axis=1
    )
    returned = padded_2(outer_rims, (("tile", 1),), rim)
    grad_own = grad_padded_map[:, rim : rim + height]
    grad_own = (
        grad_own.at[:, :rim]
        .add(returned[:, :rim])
        .at[:, height - rim :]
        .add(returned[:, 3 * rim :])
    )
    grad_map = grad_own.astype(jnp.bfloat16)
    grad_conv_bias = jnp.sum(grad_map.astype(jnp.float32), axis=(0, 1, 2))
    grad_map_padded = jnp.pad(padded_2(grad_map, (("tile", 1),), 1), column_pad)
    grad_taps, grad_lateral_full = convolve_back(
        grad_map_padded, lateral_padded, grad_map, kernel_taps, height, breadth
    )
    grad_lateral = grad_lateral_full.astype(jnp.bfloat16)
    grad_lateral_w = jnp.einsum(
        "ihwc,ihwd->cd", features, grad_lateral, preferred_element_type=jnp.float32
    )
    grad_lateral_bias = jnp.sum(grad_lateral.astype(jnp.float32), axis=(0, 1, 2))
    grad_conv = jnp.concatenate([grad_lateral_w, grad_taps], axis=0)
    grad_head = jnp.stack(head_grads)
    grad_bias = jnp.concatenate([grad_lateral_bias, grad_conv_bias] + section_bias_grads)
    conv_sum, head_sum, bias_sum, loss_total = lax.psum(
        (grad_conv, grad_head, grad_bias, loss_part), ("img", "tile")
    )
    block_grad = lax.psum_scatter(block_term, ("img", "tile"), scatter_dimension=0, tiled=True)
    step = float(STEP)
    conv_new, conv_first_new, conv_second_new = adamw(
        conv_weight, conv_first, conv_second, conv_sum, step
    )
    head_new, head_first_new, head_second_new = adamw(
        head_weight, head_first, head_second, head_sum, step
    )
    bias_new, bias_first_new, bias_second_new = adamw(
        bias_vector, bias_first, bias_second, bias_sum, step
    )
    block_new, block_first_new, block_second_new = adamw(
        block_master, block_first, block_second, block_grad, step
    )
    loss = (loss_total / valid_sum).reshape(1)
    return (
        loss,
        conv_new,
        conv_first_new,
        conv_second_new,
        head_new,
        head_first_new,
        head_second_new,
        bias_new,
        bias_first_new,
        bias_second_new,
        block_new,
        block_first_new,
        block_second_new,
    )


def solution(mesh):
    return jax.shard_map(
        on_device,
        mesh=mesh,
        in_specs=(
            P("img", "tile", None, None),
            P(),
            P(),
            P(),
            P(),
            P(),
            P(),
            P(),
            P(),
            P(),
            P(("img", "tile"), None, None),
            P(("img", "tile"), None, None),
            P(("img", "tile"), None, None),
            P(),
            P(("img", "tile")),
            P(None, None, ("img", "tile")),
            P(None, None, None, ("img", "tile")),
            P(None, ("img", "tile")),
            P(("img", "tile")),
            P(None, None, ("img", "tile")),
        ),
        out_specs=(
            P(),
            P(),
            P(),
            P(),
            P(),
            P(),
            P(),
            P(),
            P(),
            P(),
            P(("img", "tile"), None, None),
            P(("img", "tile"), None, None),
            P(("img", "tile"), None, None),
        ),
        check_vma=False,
    )
```

profile of v0, /device:TPU:0, one launch (start us, length us, event | category | flops | bytes accessed | tf_op | source)
XLA Modules:
  0.0 6458.2 jit_solution(1268085500871575329)
XLA Ops:
  93.8 35.3 gather_fusion.12
  139.8 35.3 gather_fusion.11
  185.7 35.3 gather_fusion.10
  232.5 35.3 gather_fusion.9
  278.5 32.3 fusion.7
  320.2 35.3 gather_fusion.3
  366.2 35.3 gather_fusion.2
  412.1 35.7 gather_fusion.1
  458.7 35.3 gather_fusion
  504.8 32.2 fusion.15
  546.3 35.3 gather_fusion.8
  592.3 35.3 gather_fusion.7
  638.2 35.3 gather_fusion.6
  684.2 35.3 gather_fusion.5
  730.2 32.4 fusion.11
  772.0 54.7 gather_fusion.4
  826.7 51.3 fusion.245
  897.6 14.8 fusion.93
  937.1 41.6 psum.36
  996.2 22.6 fusion.256
  1018.9 26.7 broadcast_multiply_fusion.8
  1045.6 17.4 copy.159
  1077.5 17.4 copy.160
  1094.9 14.6 reshape.473
  1109.5 17.4 copy.161
  1126.8 14.8 reshape.481
  1141.7 17.4 copy.162
  1173.4 22.6 fusion.257
  1196.1 26.5 broadcast_multiply_fusion.4
  1222.5 17.4 copy.163
  1239.9 14.6 reshape.497
  1254.5 17.4 copy.164
  1271.9 14.7 reshape.505
  1286.7 17.4 copy.165
  1318.6 17.4 copy.166
  1357.0 22.8 fusion.258
  1379.8 26.5 broadcast_multiply_fusion
  1406.3 17.4 copy.167
  1423.7 14.8 reshape.529
  1438.6 17.4 copy.168
  1470.5 17.4 copy.169
  1487.9 14.6 reshape.545
  1502.5 17.4 copy.170
  1534.3 65.4 %scatter_custom_fusion.1 = f32[3840,256]{1,0:T(8,128)} fusion(s32[12544]{0:T(1024)} %reshape.351, f32[12544,256]{1,0:T(8,128)} %reshape.465, f32[]{:T(128)} %constant.169.clone.1), kind=kCustom, calls=%fused_computation.94 | custom fusion | flops 3211264 | bytes 3932672 | tf_op jit(solution)/shard_map/scatter-add | solution.py:227
  1599.7 73.9 %scatter_fusion = f32[3840,256]{1,0:T(8,128)} fusion(f32[3840,256]{1,0:T(8,128)} %scatter_custom_fusion.1, s32[12544]{0:T(1024)S(1)} %copy-done.50, f32[12544,256]{1,0:T(8,128)} %reshape.473), kind=kCustom, calls=%fused_computation.15 | custom fusion | flops 3211264 | bytes 38585344 | tf_op jit(solution)/shard_map/scatter-add | solution.py:227
  1673.6 73.5 %scatter_fusion.1 = f32[3840,256]{1,0:T(8,128)} fusion(f32[3840,256]{1,0:T(8,128)} %scatter_fusion, s32[12544]{0:T(1024)S(1)} %copy-done.46, f32[12544,256]{1,0:T(8,128)} %reshape.481), kind=kCustom, calls=%fused_computation.16 | custom fusion | flops 3211264 | bytes 38585344 | tf_op jit(solution)/shard_map/scatter-add | solution.py:227
  1747.1 73.5 %scatter_fusion.2 = f32[3840,256]{1,0:T(8,128)} fusion(f32[3840,256]{1,0:T(8,128)} %scatter_fusion.1, s32[12544]{0:T(1024)S(1)} %copy-done.42, f32[12544,256]{1,0:T(8,128)} %reshape.489), kind=kCustom, calls=%fused_computation.17 | custom fusion | flops 3211264 | bytes 38585344 | tf_op jit(solution)/shard_map/scatter-add | solution.py:227
  1820.7 73.7 %scatter_fusion.3 = f32[3840,256]{1,0:T(8,128)} fusion(f32[3840,256]{1,0:T(8,128)} %scatter_fusion.2, s32[12544]{0:T(1024)S(1)} %copy-done.54, f32[12544,256]{1,0:T(8,128)} %reshape.497), kind=kCustom, calls=%fused_computation.18 | custom fusion | flops 3211264 | bytes 38585344 | tf_op jit(solution)/shard_map/scatter-add | solution.py:227
  1894.4 73.9 %scatter_fusion.4 = f32[3840,256]{1,0:T(8,128)} fusion(f32[3840,256]{1,0:T(8,128)} %scatter_fusion.3, s32[12544]{0:T(1024)S(1)} %copy-done.52, f32[12544,256]{1,0:T(8,128)} %reshape.505), kind=kCustom, calls=%fused_computation.19 | custom fusion | flops 3211264 | bytes 38585344 | tf_op jit(solution)/shard_map/scatter-add | solution.py:227
  1968.3 73.7 %scatter_fusion.5 = f32[3840,256]{1,0:T(8,128)} fusion(f32[3840,256]{1,0:T(8,128)} %scatter_fusion.4, s32[12544]{0:T(1024)S(1)} %copy-done.48, f32[12544,256]{1,0:T(8,128)} %reshape.513), kind=kCustom, calls=%fused_computation.20 | custom fusion | flops 3211264 | bytes 38585344 | tf_op jit(solution)/shard_map/scatter-add | solution.py:227
  2042.1 73.7 %scatter_fusion.6 = f32[3840,256]{1,0:T(8,128)} fusion(f32[3840,256]{1,0:T(8,128)} %scatter_fusion.5, s32[12544]{0:T(1024)S(1)} %copy-done.44, f32[12544,256]{1,0:T(8,128)} %reshape.521), kind=kCustom, calls=%fused_computation.21 | custom fusion | flops 3211264 | bytes 38585344 | tf_op jit(solution)/shard_map/scatter-add | solution.py:227
  2115.8 73.8 %scatter_fusion.7 = f32[3840,256]{1,0:T(8,128)} fusion(f32[3840,256]{1,0:T(8,128)} %scatter_fusion.6, s32[12544]{0:T(1024)S(1)} %copy-done.40, f32[12544,256]{1,0:T(8,128)} %reshape.529), kind=kCustom, calls=%fused_computation.22 | custom fusion | flops 3211264 | bytes 38585344 | tf_op jit(solution)/shard_map/scatter-add | solution.py:227
  2189.6 74.0 %scatter_fusion.8 = f32[3840,256]{1,0:T(8,128)} fusion(f32[3840,256]{1,0:T(8,128)} %scatter_fusion.7, s32[12544]{0:T(1024)S(1)} %copy-done.38, f32[12544,256]{1,0:T(8,128)} %reshape.537), kind=kCustom, calls=%fused_computation.23 | custom fusion | flops 3211264 | bytes 38585344 | tf_op jit(solution)/shard_map/scatter-add | solution.py:227
  2263.6 73.8 %scatter_fusion.9 = f32[3840,256]{1,0:T(8,128)} fusion(f32[3840,256]{1,0:T(8,128)} %scatter_fusion.8, s32[12544]{0:T(1024)S(1)} %copy-done.36, f32[12544,256]{1,0:T(8,128)} %reshape.545), kind=kCustom, calls=%fused_computation.24 | custom fusion | flops 3211264 | bytes 38585344 | tf_op jit(solution)/shard_map/scatter-add | solution.py:227
  2337.4 73.8 %scatter_fusion.10 = f32[3840,256]{1,0:T(8,128)} fusion(f32[3840,256]{1,0:T(8,128)} %scatter_fusion.9, s32[12544]{0:T(1024)S(1)} %copy-done.34, f32[12544,256]{1,0:T(8,128)} %reshape.553), kind=kCustom, calls=%fused_computation.25 | custom fusion | flops 3211264 | bytes 38585344 | tf_op jit(solution)/shard_map/scatter-add | solution.py:227
  2420.6 37.3 pad_maximum_fusion
  2458.0 35.9 pad_maximum_fusion.1
  2498.5 51.4 broadcast_in_dim.58
  2549.9 105.2 %scatter_fusion.11 = f32[1280,32,1024]{2,1,0:T(8,128)} fusion(f32[1280,32,1024]{2,1,0:T(8,128)} %broadcast_in_dim.58, s32[424]{0:T(512)S(1)} %copy-done.114, f32[424,32,1024]{2,1,0:T(8,128)} %bitcast.496), kind=kCustom, calls=%fused_computation.26 | custom fusion | bytes 166725280 | tf_op jit(solution)/shard_map/scatter | solution.py:240
  2655.1 104.9 %scatter_fusion.12 = f32[1280,32,1024]{2,1,0:T(8,128)} fusion(f32[1280,32,1024]{2,1,0:T(8,128)} %scatter_fusion.11, s32[424]{0:T(512)S(1)} %copy-done.113, f32[424,32,1024]{2,1,0:T(8,128)} %bitcast.495), kind=kCustom, calls=%fused_computation.27 | custom fusion | bytes 166725280 | tf_op jit(solution)/shard_map/scatter | solution.py:240
  2798.2 37.6 pad_maximum_fusion.2
  2835.8 106.5 %scatter_fusion.13 = f32[1280,32,1024]{2,1,0:T(8,128)} fusion(f32[1280,32,1024]{2,1,0:T(8,128)} %scatter_fusion.12, s32[424]{0:T(512)S(1)} %copy-done.112, f32[424,32,1024]{2,1,0:T(8,128)} %bitcast.497), kind=kCustom, calls=%fused_computation.28 | custom fusion | bytes 166725280 | tf_op jit(solution)/shard_map/scatter | solution.py:240
  2948.2 61.7 all-reduce.2
  3024.1 3412.6 %reduce-scatter.2.cloned.1.call-done = f32[40,32,1024]{2,1,0:T(8,128)} async-done(((f32[1280,32,1024]{2,1,0:T(8,128)}), f32[40,32,1024]{2,1,0:T(8,128)}) %reduce-scatter.2.cloned.1.call-update) | async-done | bytes 5242896 | tf_op jit(solution)/shard_map/reduce_scatter | solution.py:270
  (463 shorter events, 481.0 us)
Async XLA Ops:
  7.2 764.8 %all-gather.2.cloned.1.call-start = ((), (), s32[]{:S(2)}) async-start(), calls=%async_computation.1 | async-start | bytes 86507520 | tf_op jit(solution)/shard_map/all_gather | solution.py:116
  11.8 3000.9 %all-reduce.6.cloned.1.call-start = ((), (), s32[]{:S(2)}) async-start(), calls=%async_computation.3 | async-start | bytes 7405568 | tf_op jit(solution)/shard_map/psum | solution.py:267
  15.3 65.3 %copy-start.2 = (bf16[2,8,160,256]{3,2,1,0:T(8,128)(2,1)}, bf16[2,8,160,256]{3,2,1,0:T(8,128)(2,1)S(1)}, u32[]{:S(2)}) copy-start(bf16[2,8,160,256]{3,2,1,0:T(8,128)(2,1)S(1)} %add_convert_fusion.2) | copy-start | bytes 3932164
  16.1 51.7 collective-permute-start.1
  17.4 50.9 collective-permute-start
  22.9 20.5 copy-start.111
  24.0 36.1 copy-start.33
  25.2 37.6 copy-start.35
  25.5 37.3 copy-start.37
  25.8 37.7 copy-start.39
  26.1 38.2 copy-start.41
  27.3 37.0 copy-start.45
  30.0 34.8 copy-start.49
  36.0 28.8 copy-start.43
  38.8 26.1 copy-start.47
  41.5 23.4 copy-start.51
  43.4 21.5 copy-start.53
  73.6 12.6 collective-permute-start.3
  74.9 18.7 collective-permute-start.2
  826.7 51.3 copy-start.120
  892.0 25.8 slice-start
  996.2 22.6 copy-start.76
  996.2 22.6 copy-start.78
  996.2 22.6 copy-start.80
  996.2 22.6 copy-start.82
  1173.4 22.6 copy-start.68
  1173.4 22.6 copy-start.70
  1173.4 22.6 copy-start.72
  1173.4 22.6 copy-start.74
  1357.0 22.8 copy-start.84
  1357.0 22.8 copy-start.86
  1357.0 22.8 copy-start.88
  1357.0 22.8 copy-start.90
  1534.3 65.5 %copy-start.50 = (s32[12544]{0:T(1024)S(1)}, s32[12544]{0:T(1024)}, u32[]{:S(2)}) copy-start(s32[12544]{0:T(1024)} %copy-done.49) | copy-start | bytes 150532
  1599.7 73.9 %copy-start.46 = (s32[12544]{0:T(1024)S(1)}, s32[12544]{0:T(1024)}, u32[]{:S(2)}) copy-start(s32[12544]{0:T(1024)} %copy-done.45) | copy-start | bytes 150532
  1673.6 73.5 %copy-start.42 = (s32[12544]{0:T(1024)S(1)}, s32[12544]{0:T(1024)}, u32[]{:S(2)}) copy-start(s32[12544]{0:T(1024)} %copy-done.41) | copy-start | bytes 150532
  1747.1 73.5 %copy-start.54 = (s32[12544]{0:T(1024)S(1)}, s32[12544]{0:T(1024)}, u32[]{:S(2)}) copy-start(s32[12544]{0:T(1024)} %copy-done.53) | copy-start | bytes 150532
  1820.7 73.7 %copy-start.52 = (s32[12544]{0:T(1024)S(1)}, s32[12544]{0:T(1024)}, u32[]{:S(2)}) copy-start(s32[12544]{0:T(1024)} %copy-done.51) | copy-start | bytes 150532
  1894.4 73.9 %copy-start.48 = (s32[12544]{0:T(1024)S(1)}, s32[12544]{0:T(1024)}, u32[]{:S(2)}) copy-start(s32[12544]{0:T(1024)} %copy-done.47) | copy-start | bytes 150532
  1968.3 73.7 %copy-start.44 = (s32[12544]{0:T(1024)S(1)}, s32[12544]{0:T(1024)}, u32[]{:S(2)}) copy-start(s32[12544]{0:T(1024)} %copy-done.43) | copy-start | bytes 150532
  2042.1 73.7 %copy-start.40 = (s32[12544]{0:T(1024)S(1)}, s32[12544]{0:T(1024)}, u32[]{:S(2)}) copy-start(s32[12544]{0:T(1024)} %copy-done.39) | copy-start | bytes 150532
  2115.8 73.8 %copy-start.38 = (s32[12544]{0:T(1024)S(1)}, s32[12544]{0:T(1024)}, u32[]{:S(2)}) copy-start(s32[12544]{0:T(1024)} %copy-done.37) | copy-start | bytes 150532
  2189.6 74.0 %copy-start.36 = (s32[12544]{0:T(1024)S(1)}, s32[12544]{0:T(1024)}, u32[]{:S(2)}) copy-start(s32[12544]{0:T(1024)} %copy-done.35) | copy-start | bytes 150532
  2263.6 73.8 %copy-start.34 = (s32[12544]{0:T(1024)S(1)}, s32[12544]{0:T(1024)}, u32[]{:S(2)}) copy-start(s32[12544]{0:T(1024)} %copy-done.33) | copy-start | bytes 150532
  2413.7 349.2 %collective-permute-start.4 = (f32[2,2,160,256]{3,2,1,0:T(8,128)}, f32[2,2,160,256]{3,2,1,0:T(8,128)}, u32[]{:S(2)}, u32[]{:S(2)}) collective-permute-start(f32[2,2,160,256]{3,2,1,0:T(8,128)} %get-tuple-element.86), channel_id=1, source_target_pairs={{0,1},{1,2},{2,3},{3,4},{4,5},{5,6},{6,7},{8,9},{9,10},{10,11},{11... | collective-permute-start | bytes 1966088 | tf_op jit(solution)/shard_map/ppermute | solution.py:26
  2419.3 345.0 %collective-permute-start.5 = (f32[2,2,160,256]{3,2,1,0:T(8,128)}, f32[2,2,160,256]{3,2,1,0:T(8,128)}, u32[]{:S(2)}, u32[]{:S(2)}) collective-permute-start(f32[2,2,160,256]{3,2,1,0:T(8,128)} %get-tuple-element.85), channel_id=1, source_target_pairs={{1,0},{2,1},{3,2},{4,3},{5,4},{6,5},{7,6},{9,8},{10,9},{11,10},{12... | collective-permute-start | bytes 1966088 | tf_op jit(solution)/shard_map/ppermute | solution.py:28
  2420.6 37.4 copy-start.11
  2458.0 35.9 copy-start.15
  2458.0 35.9 copy-start.94
  2458.0 35.9 copy-start.107
  2458.0 36.2 copy-start.17
  2458.0 36.2 copy-start.96
  2458.0 36.2 copy-start.110
  2498.5 51.4 copy-start.114
  2549.9 105.2 %copy-start.113 = (s32[424]{0:T(512)S(1)}, s32[424]{0:T(512)}, u32[]{:S(2)}) copy-start(s32[424]{0:T(512)} %get-tuple-element.147) | copy-start | bytes 5092
  2655.1 104.9 %copy-start.130 = (f32[256,1024]{1,0:T(8,128)S(1)}, f32[256,1024]{1,0:T(8,128)}, u32[]{:S(2)}) copy-start(f32[256,1024]{1,0:T(8,128)} %fusion.93) | copy-start | bytes 3145732
  2655.1 104.9 %copy-start.135 = (bf16[256,1024]{1,0:T(8,128)(2,1)S(1)}, bf16[256,1024]{1,0:T(8,128)(2,1)}, u32[]{:S(2)}) copy-start(bf16[256,1024]{1,0:T(8,128)(2,1)} %copy-done.134) | copy-start | bytes 1572868
  2766.6 8.0 collective-permute-start.7
  2767.9 10.4 collective-permute-start.6
  2798.0 37.8 copy-start.112
  2798.0 3638.8 %reduce-scatter.2.cloned.1.call-start = ((), (), s32[]{:S(2)}) async-start(), calls=%async_computation.2 | async-start | bytes 173015040 | tf_op jit(solution)/shard_map/reduce_scatter | solution.py:270
  2942.3 69.0 %copy-start.98 = (f32[6911]{0:T(1024)S(1)}, f32[6911]{0:T(1024)}, u32[]{:S(2)}) copy-start(f32[6911]{0:T(1024)} %param.34) | copy-start | bytes 82936
  2942.3 70.4 %copy-start.10 = (f32[3,1024,85]{1,2,0:T(8,128)S(1)}, f32[3,1024,85]{1,2,0:T(8,128)}, u32[]{:S(2)}) copy-start(f32[3,1024,85]{1,2,0:T(8,128)} %param.31) | copy-start | bytes 3133444
  2942.3 70.4 %copy-start.32 = (f32[3,1024,85]{1,2,0:T(8,128)S(1)}, f32[3,1024,85]{1,2,0:T(8,128)}, u32[]{:S(2)}) copy-start(f32[3,1024,85]{1,2,0:T(8,128)} %param.32) | copy-start | bytes 3133444
  (87 other events, 599.2 us)
Sparse Core Ops, SparseCore 0:
  11.9 443.3 all-gather.1
  2798.1 140.4 all-reduce.5
  2942.4 3494.2 reduce-scatter.1
where the time goes:
time: 6480 us; the launch traced here: 6460 us
  waiting for transfers between devices  3420 us (53%)
  local copies, waits for them, and re-layouts  1490 us (23%)
  other arithmetic  1150 us (18%)
  matrix products  251 us (4%)
  blocking collectives  103 us (2%)
    reduce_scatter x1, waiting for transfers between devices, on_device(): lax.psum_scatter(block_term, ('img', 'tile'), scatter_dimension=0, tiled=...  3410 us
    scatter-add x12, other arithmetic, on_device(): grad_flat.at[corner_base + corner_shifts[corner]]  877 us
    gather x12, local copies, waits for them, and re-layouts, on_device(): flat_map[corner_base + corner_shifts[corner]].astype(jnp.float32)  424 us
    mul x24, local copies, waits for them, and re-layouts, on_device(): corner_weights[corner][:, :, None] * grad_pooled  384 us
    scatter x3, local copies, waits for them, and re-layouts, on_device(): block_term = block_term.at[targets].set(dense_section)  317 us
  transfers between devices with their start and end apart: 11, of which 4 were waited for; matrix products, arithmetic and copies ran while one was open for 19% of the time, Pallas kernels for 0%

commit v1 on v0

--- a/solution.py
+++ b/solution.py
@@ -1,18 +1,23 @@
 import jax
 import jax.numpy as jnp
 from jax import lax
+from jax.experimental import pallas as pl
+from jax.experimental.pallas import tpu as pltpu
 from jax.sharding import PartitionSpec as P
 
 HR = 2
 STEP = 5
 BINS = 49
-
+POOL = 7
 
 BETA_ONE = 0.9
 BETA_TWO = 0.999
 RATE = 0.025
 DECAY = 0.01
 EPSILON = 1e-08
+
+VMEM_LIMIT = 56 * 1024 * 1024
+AXES = ("img", "tile")
 
 
 def padded_2(cells, sides, width):
@@ -77,6 +82,377 @@
         )
         grad_input = contrib if grad_input is None else grad_input + contrib
     return (jnp.concatenate(tap_grads, axis=0), grad_input)
+
+
+def column_weights(column, frac, breadth):
+    regions = column.shape[1]
+    away = lax.broadcasted_iota(jnp.int32, (breadth, regions), 0) - column
+    return jnp.where(away == 0, 1.0 - frac, jnp.where(away == 1, frac, 0.0))
+
+
+def row_weight(row, frac, at):
+    away = at - row
+    return jnp.where(away == 0, 1.0 - frac, jnp.where(away == 1, frac, 0.0))
+
+
+def pool_regions(map_t, rows, cols, fracs_row, fracs_col, breadth):
+    section_count, bins, regions = rows.shape
+    channels, cells = map_t.shape
+    lines = cells // breadth
+    group = POOL
+    chunk = 8
+
+    def body(map_ref, row_ref, col_ref, fr_ref, fc_ref, out_ref):
+        turn = pl.program_id(1)
+
+        def one_bin(b, carry):
+            p = turn * group + b
+            row = row_ref[0, pl.ds(p, 1), :]
+            col = col_ref[0, pl.ds(p, 1), :]
+            frow = fr_ref[0, pl.ds(p, 1), :]
+            fcol = fc_ref[0, pl.ds(p, 1), :]
+            across = column_weights(col, fcol, breadth)
+            total = None
+            for first in range(0, lines, chunk):
+                weights = jnp.concatenate(
+                    [
+                        (across * row_weight(row, frow, line)).astype(jnp.bfloat16)
+                        for line in range(first, first + chunk)
+                    ],
+                    axis=0,
+                )
+                part = jnp.dot(
+                    map_ref[:, first * breadth : (first + chunk) * breadth],
+                    weights,
+                    preferred_element_type=jnp.float32,
+                )
+                total = part if total is None else total + part
+            out_ref[0, b] = total.astype(jnp.bfloat16)
+            return carry
+
+        lax.fori_loop(0, group, one_bin, 0)
+
+    samples = pl.BlockSpec((1, bins, regions), lambda u, t: (u, 0, 0))
+    return pl.pallas_call(
+        body,
+        grid=(section_count, bins // group),
+        in_specs=[pl.BlockSpec((channels, cells), lambda u, t: (0, 0))] + [samples] * 4,
+        out_specs=pl.BlockSpec((1, group, channels, regions), lambda u, t: (u, t, 0, 0)),
+        out_shape=jax.ShapeDtypeStruct((section_count, bins, channels, regions), jnp.bfloat16),
+        compiler_params=pltpu.CompilerParams(vmem_limit_bytes=VMEM_LIMIT),
+        cost_estimate=pl.CostEstimate(
+            flops=2 * section_count * bins * regions * cells * channels,
+            bytes_accessed=section_count * bins * regions * channels * 2,
+            transcendentals=0,
+        ),
+        name="pool_regions",
+    )(map_t, rows, cols, fracs_row, fracs_col)
+
+
+def fetch_blocks(table, blocks_ref, buffer, sem, base, slot, count, block_rows):
+    def one(b, carry):
+        pltpu.make_async_copy(
+            blocks_ref.at[table[base + b]],
+            buffer.at[slot, pl.ds(pl.multiple_of(b * block_rows, block_rows), block_rows)],
+            sem.at[slot],
+        ).start()
+        return carry
+
+    lax.fori_loop(0, count, one, 0, unroll=8)
+
+
+def first_layer(table, blocks, feats_t, section_blocks):
+    section_count, bins, channels, regions = feats_t.shape
+    _, block_rows, hidden = blocks.shape
+    group = POOL
+    turns = bins // group
+    per_bin = channels // block_rows
+    count = group * per_bin
+
+    def body(table_ref, blocks_ref, x_ref, out_ref, buffer, sem):
+        u, t = pl.program_id(0), pl.program_id(1)
+        step = u * turns + t
+        slot = lax.rem(step, 2)
+
+        def fetch(at, into):
+            base = (at // turns) * section_blocks + lax.rem(at, turns) * count
+            fetch_blocks(table_ref, blocks_ref, buffer, sem, base, into, count, block_rows)
+
+        @pl.when(step == 0)
+        def _():
+            fetch(step, slot)
+
+        @pl.when(step + 1 < section_count * turns)
+        def _():
+            fetch(step + 1, 1 - slot)
+
+        pltpu.make_async_copy(buffer.at[slot], buffer.at[slot], sem.at[slot]).wait()
+
+        @pl.when(t == 0)
+        def _():
+            out_ref[...] = jnp.zeros_like(out_ref)
+
+        def one_bin(b, carry):
+            at = pl.ds(pl.multiple_of(b * channels, channels), channels)
+            out_ref[0] += lax.dot_general(
+                x_ref[0, b],
+                buffer[slot, at],
+                (((0,), (0,)), ((), ())),
+                preferred_element_type=jnp.float32,
+            )
+            return carry
+
+        lax.fori_loop(0, group, one_bin, 0)
+
+    return pl.pallas_call(
+        body,
+        grid_spec=pltpu.PrefetchScalarGridSpec(
+            num_scalar_prefetch=1,
+            grid=(section_count, turns),
+            in_specs=[
+                pl.BlockSpec(memory_space=pl.ANY),
+                pl.BlockSpec((1, group, channels, regions), lambda u, t, _: (u, t, 0, 0)),
+            ],
+            out_specs=pl.BlockSpec((1, regions, hidden), lambda u, t, _: (u, 0, 0)),
+            scratch_shapes=[
+                pltpu.VMEM((2, count * block_rows, hidden), jnp.bfloat16),
+                pltpu.SemaphoreType.DMA((2,)),
+            ],
+        ),
+        out_shape=jax.ShapeDtypeStruct((section_count, regions, hidden), jnp.float32),
+        compiler_params=pltpu.CompilerParams(vmem_limit_bytes=VMEM_LIMIT),
+        cost_estimate=pl.CostEstimate(
+            flops=2 * section_count * bins * regions * channels * hidden,
+            bytes_accessed=section_count * bins * channels * (regions + hidden) * 2,
+            transcendentals=0,
+        ),
+        name="first_layer",
+    )(table, blocks, feats_t)
+
+
+def weight_grads(order, place, offsets, feats_t, acts_t, grads_first, grads_second, sizes):
+    section_count, bins, channels, regions = feats_t.shape
+    hidden = grads_first.shape[2]
+    block_rows = sizes[0][1]
+    group = POOL
+    turns = bins // group + 1
+    rows = group * channels
+    wide = acts_t.shape[1]
+    steps = section_count * turns
+    kinds = len(sizes)
+
+    def body(order_ref, place_ref, offset_ref, x_ref, a_ref, gf_ref, gs_ref, *rest):
+        outs, (buffer, sem) = rest[:kinds], rest[kinds:]
+        u, t = pl.program_id(0), pl.program_id(1)
+        step = u * turns + t
+        slot = lax.rem(step, 2)
+
+        def drain(at, into):
+            last = lax.rem(at, turns) == turns - 1
+
+            @pl.when(last)
+            def _():
+                half = buffer.at[into, pl.ds(0, wide)]
+                pltpu.make_async_copy(half, half, sem.at[into]).wait()
+
+            @pl.when(jnp.logical_not(last))
+            def _():
+                pltpu.make_async_copy(buffer.at[into], buffer.at[into], sem.at[into]).wait()
+
+        @pl.when(step >= 2)
+        def _():
+            drain(step - 2, slot)
+
+        @pl.when(t < turns - 1)
+        def _():
+            def one_bin(b, carry):
+                at = pl.ds(pl.multiple_of(b * channels, channels), channels)
+                buffer[slot, at] = jnp.dot(
+                    x_ref[0, b], gf_ref[0], preferred_element_type=jnp.float32
+                ).astype(jnp.bfloat16)
+                return carry
+
+            lax.fori_loop(0, group, one_bin, 0)
+
+        @pl.when(t == turns - 1)
+        def _():
+            def one_part(b, carry):
+                at = pl.ds(pl.multiple_of(b * channels, channels), channels)
+                buffer[slot, at] = jnp.dot(
+                    a_ref[0, at], gs_ref[0], preferred_element_type=jnp.float32
+                ).astype(jnp.bfloat16)
+                return carry
+
+            lax.fori_loop(0, wide // channels, one_part, 0)
+
+        for kind in range(kinds):
+
+            def one(i, carry, kind=kind):
+                at = pl.ds(pl.multiple_of(order_ref[i] * block_rows, block_rows), block_rows)
+                pltpu.make_async_copy(
+                    buffer.at[slot, at], outs[kind].at[place_ref[i]], sem.at[slot]
+                ).start()
+                return carry
+
+            lax.fori_loop(
+                offset_ref[step * kinds + kind], offset_ref[step * kinds + kind + 1], one, 0
+            )
+
+        @pl.when(step == steps - 1)
+        def _():
+            drain(step - 1, 1 - slot)
+            drain(step, slot)
+
+    return pl.pallas_call(
+        body,
+        grid_spec=pltpu.PrefetchScalarGridSpec(
+            num_scalar_prefetch=3,
+            grid=(section_count, turns),
+            in_specs=[
+                pl.BlockSpec(
+                    (1, group, channels, regions),
+                    lambda u, t, *_: (u, jnp.minimum(t, turns - 2), 0, 0),
+                ),
+                pl.BlockSpec((1, wide, regions), lambda u, t, *_: (u, 0, 0)),
+                pl.BlockSpec((1, regions, hidden), lambda u, t, *_: (u, 0, 0)),
+                pl.BlockSpec((1, regions, hidden), lambda u, t, *_: (u, 0, 0)),
+            ],
+            out_specs=[pl.BlockSpec(memory_space=pl.ANY)] * kinds,
+            scratch_shapes=[
+                pltpu.VMEM((2, rows, hidden), jnp.bfloat16),
+                pltpu.SemaphoreType.DMA((2,)),
+            ],
+        ),
+        out_shape=[jax.ShapeDtypeStruct(size, jnp.bfloat16) for size in sizes],
+        compiler_params=pltpu.CompilerParams(vmem_limit_bytes=VMEM_LIMIT),
+        cost_estimate=pl.CostEstimate(
+            flops=2 * section_count * regions * (bins * channels + wide) * hidden,
+            bytes_accessed=section_count * (bins * channels + wide) * (regions + hidden) * 2,
+            transcendentals=0,
+        ),
+        name="weight_grads",
+    )(order, place, offsets, feats_t, acts_t, grads_first, grads_second)
+
+
+def map_grads(table, blocks, grads_first, rows, cols, fracs_row, fracs_col, section_blocks, lines, breadth, channels):
+    section_count, bins, regions = rows.shape
+    _, block_rows, hidden = blocks.shape
+    group = POOL
+    turns = bins // group
+    count = group * channels // block_rows
+    cells = lines * breadth
+
+    def body(table_ref, blocks_ref, g_ref, row_ref, col_ref, fr_ref, fc_ref, out_ref, buffer, sem):
+        u, t = pl.program_id(0), pl.program_id(1)
+        step = u * turns + t
+        slot = lax.rem(step, 2)
+
+        def fetch(at, into):
+            base = (at // turns) * section_blocks + lax.rem(at, turns) * count
+            fetch_blocks(table_ref, blocks_ref, buffer, sem, base, into, count, block_rows)
+
+        @pl.when(step == 0)
+        def _():
+            out_ref[...] = jnp.zeros_like(out_ref)
+            fetch(step, slot)
+
+        @pl.when(step + 1 < section_count * turns)
+        def _():
+            fetch(step + 1, 1 - slot)
+
+        pltpu.make_async_copy(buffer.at[slot], buffer.at[slot], sem.at[slot]).wait()
+
+        def one_bin(b, carry):
+            p = t * group + b
+            at = pl.ds(pl.multiple_of(b * channels, channels), channels)
+            pooled = lax.dot_general(
+                g_ref[0],
+                buffer[slot, at],
+                (((1,), (1,)), ((), ())),
+                preferred_element_type=jnp.float32,
+            ).astype(jnp.bfloat16)
+            row = row_ref[0, pl.ds(p, 1), :]
+            frow = fr_ref[0, pl.ds(p, 1), :]
+            across = column_weights(
+                col_ref[0, pl.ds(p, 1), :], fc_ref[0, pl.ds(p, 1), :], breadth
+            )
+            for line in range(lines):
+                weights = (across * row_weight(row, frow, line)).astype(jnp.bfloat16)
+                out_ref[line * breadth : (line + 1) * breadth] += jnp.dot(
+                    weights, pooled, preferred_element_type=jnp.float32
+                )
+            return carry
+
+        lax.fori_loop(0, group, one_bin, 0)
+
+    samples = pl.BlockSpec((1, bins, regions), lambda u, t, _: (u, 0, 0))
+    return pl.pallas_call(
+        body,
+        grid_spec=pltpu.PrefetchScalarGridSpec(
+            num_scalar_prefetch=1,
+            grid=(section_count, turns),
+            in_specs=[
+                pl.BlockSpec(memory_space=pl.ANY),
+                pl.BlockSpec((1, regions, hidden), lambda u, t, _: (u, 0, 0)),
+            ]
+            + [samples] * 4,
+            out_specs=pl.BlockSpec((cells, channels), lambda u, t, _: (0, 0)),
+            scratch_shapes=[
+                pltpu.VMEM((2, count * block_rows, hidden), jnp.bfloat16),
+                pltpu.SemaphoreType.DMA((2,)),
+            ],
+        ),
+        out_shape=jax.ShapeDtypeStruct((cells, channels), jnp.float32),
+        compiler_params=pltpu.CompilerParams(vmem_limit_bytes=VMEM_LIMIT),
+        cost_estimate=pl.CostEstimate(
+            flops=2 * section_count * bins * regions * channels * (hidden + cells),
+            bytes_accessed=section_count * bins * channels * hidden * 2,
+            transcendentals=0,
+        ),
+        name="map_grads",
+    )(table, blocks, grads_first, rows, cols, fracs_row, fracs_col)
+
+
+def bits_of(count):
+    return list(range(count.bit_length() - 1))
+
+
+def part_orders(n_img, n_tile):
+    low = [("tile", b) for b in bits_of(n_tile)[:1]]
+    high = [("tile", b) for b in bits_of(n_tile)[1:]]
+    side = [("img", b) for b in bits_of(n_img)[1:]]
+    return [low + side + high, side + high + low, high + low + side]
+
+
+def part_sizes(slots):
+    first = (3 * slots + 7) // 8
+    second = (slots - first + 1) * 5 // 9
+    return [first, second, slots - first - second]
+
+
+def swap(values, axis, bit):
+    count = lax.axis_size(axis)
+    return lax.ppermute(values, axis, [(i, i ^ (1 << bit)) for i in range(count)])
+
+
+def add_low(a, b):
+    return (a.astype(jnp.float32) + b.astype(jnp.float32)).astype(jnp.bfloat16)
+
+
+def sum_parts(kept, sent, orders):
+    received = [swap(s, "img", 0) for s in sent]
+    results = [None] * len(kept)
+    pairs = [(k, r) for k, r in zip(kept, received)]
+    for stage in range(len(orders[0])):
+        for i, order in enumerate(orders):
+            mine, theirs = pairs[i]
+            half = mine.shape[0] // 2
+            away = add_low(mine[half:], theirs[half:])
+            stay = add_low(mine[:half], theirs[:half])
+            pairs[i] = (stay, swap(away, *order[stage]))
+    for i, (mine, theirs) in enumerate(pairs):
+        results[i] = mine.astype(jnp.float32) + theirs.astype(jnp.float32)
+    return results
 
 
 def on_device(
@@ -107,24 +483,53 @@
     classes = out_width - 4
     slots, block_rows, _ = block_master.shape
     all_slots = slot_block.shape[0]
-    region_count = roi_image.shape[0]
     rim = HR
     first_rows = BINS * channels
     section_rows = first_rows + hidden
     section_blocks = section_rows // block_rows
+    first_blocks = first_rows // block_rows
     block_total = section_count * section_blocks
-    gathered = lax.all_gather(
-        block_master.astype(jnp.bfloat16), ("img", "tile"), axis=0, tiled=True
-    )
+    n_img, n_tile = lax.axis_size("img"), lax.axis_size("tile")
+    at_img, at_tile = lax.axis_index("img"), lax.axis_index("tile")
+
+    gathered = lax.all_gather(block_master.astype(jnp.bfloat16), AXES, axis=0, tiled=True)
     position = jnp.arange(all_slots, dtype=jnp.int32)
     owner_slot = (
         jnp.zeros((block_total,), jnp.int32)
         .at[jnp.where(slot_block >= 0, slot_block, block_total)]
         .set(position, mode="drop")
     )
-    stacked = gathered[owner_slot].reshape(section_count, section_rows, hidden)
+
+    orders = part_orders(n_img, n_tile)
+    shares = part_sizes(slots)
+    groups = n_img * n_tile // 2
+    owner = owner_slot // slots
+    within = owner_slot % slots
+    relative = {"img": (owner // n_tile) ^ at_img, "tile": (owner % n_tile) ^ at_tile}
+    kind = jnp.zeros((block_total,), jnp.int32)
+    place = jnp.zeros((block_total,), jnp.int32)
+    start = 0
+    for i, (order, share) in enumerate(zip(orders, shares)):
+        rank = jnp.zeros((block_total,), jnp.int32)
+        for axis, bit in order:
+            rank = rank * 2 + ((relative[axis] >> bit) & 1)
+        inside = (within >= start) & (within < start + share)
+        kind = jnp.where(inside, 2 * i + (relative["img"] & 1), kind)
+        place = jnp.where(inside, rank * share + within - start, place)
+        start += share
+    kinds = 2 * len(orders)
+    block_id = jnp.arange(block_total, dtype=jnp.int32)
+    per_turn = POOL * channels // block_rows
+    turn = (block_id // section_blocks) * (POOL + 1) + (block_id % section_blocks) // per_turn
+    bucket = turn * kinds + kind
+    buckets = section_count * (POOL + 1) * kinds
+    within_turn = (block_id % section_blocks) % per_turn
+    _, order_list, place_list = lax.sort((bucket, within_turn, place), num_keys=1)
+    offsets = jnp.sum(
+        (bucket[None, :] < jnp.arange(buckets + 1, dtype=jnp.int32)[:, None]).astype(jnp.int32), axis=1
+    )
+
     valid_float = valid.astype(jnp.float32)
-    valid_sum = lax.psum(jnp.sum(valid_float), ("img", "tile"))
     conv_low = conv_weight.astype(jnp.bfloat16)
     lateral_w = conv_low[:in_channels]
     kernel_taps = conv_low[in_channels:].reshape(9, channels, channels)
@@ -142,42 +547,32 @@
     )
     map_padded = padded_2(feature_map, (("tile", 1),), rim)
     padded_rows = height + 2 * rim
-    flat_map = map_padded.reshape(images * padded_rows * breadth, channels)
-    corner_shifts = (0, 1, breadth, breadth + 1)
-    grad_flat = jnp.zeros((images * padded_rows * breadth, channels), jnp.float32)
+    lines = images * padded_rows
+    map_t = map_padded.reshape(lines * breadth, channels).T
+    sample_rows = roi_image * padded_rows + corner_index // breadth
+    sample_cols = corner_index % breadth
+    fracs_row = corner_frac[:, 0]
+    fracs_col = corner_frac[:, 1]
+    feats_t = pool_regions(map_t, sample_rows, sample_cols, fracs_row, fracs_col, breadth)
+    first_pres = first_layer(owner_slot, gathered, feats_t, section_blocks)
+
     loss_part = jnp.zeros((), jnp.float32)
-    weight_each = valid_float / valid_sum
     head_grads = []
     section_bias_grads = []
-    block_term = jnp.zeros((all_slots, block_rows, hidden), jnp.float32)
+    acts_t, grads_first, grads_second = [], [], []
     for section in range(section_count):
-        first_matrix = stacked[section, :first_rows]
-        second_matrix = stacked[section, first_rows:]
+        second_slots = lax.slice_in_dim(
+            owner_slot, section * section_blocks + first_blocks, (section + 1) * section_blocks
+        )
+        second_matrix = gathered[second_slots].reshape(hidden, hidden)
         head_low = head_all[section]
         offset = 2 * channels + section * (2 * hidden + out_width)
         first_bias = bias_vector[offset : offset + hidden]
         second_bias = bias_vector[offset + hidden : offset + 2 * hidden]
         head_bias = bias_vector[offset + 2 * hidden : offset + 2 * hidden + out_width]
-        corner_base = roi_image[:, None] * (padded_rows * breadth) + corner_index[section].T
-        frac_row = corner_frac[section, 0].T
-        frac_col = corner_frac[section, 1].T
-        corner_weights = (
-            (1.0 - frac_row) * (1.0 - frac_col),
-            (1.0 - frac_row) * frac_col,
-            frac_row * (1.0 - frac_col),
-            frac_row * frac_col,
-        )
-        pooled = None
-        for corner in range(4):
-            contrib = corner_weights[corner][:, :, None] * flat_map[
-                corner_base + corner_shifts[corner]
-            ].astype(jnp.float32)
-            pooled = contrib if pooled is None else pooled + contrib
-        roi_feats = pooled.reshape(region_count, first_rows).astype(jnp.bfloat16)
-        first_pre = (
-            jnp.dot(roi_feats, first_matrix, preferred_element_type=jnp.float32) + first_bias
-        )
+        first_pre = first_pres[section] + first_bias
         first_act = jax.nn.silu(first_pre).astype(jnp.bfloat16)
+        acts_t.append(first_act.T)
         second_pre = (
             jnp.dot(first_act, second_matrix, preferred_element_type=jnp.float32) + second_bias
         )
@@ -201,8 +596,8 @@
             valid_float * (cross + foreground * jnp.sum(smooth, axis=1))
         )
         probs = jnp.exp(shifted - log_total)
-        grad_logits = weight_each[:, None] * (probs - one_hot)
-        grad_box = (weight_each * foreground)[:, None] * jnp.clip(differ, -1.0, 1.0)
+        grad_logits = valid_float[:, None] * (probs - one_hot)
+        grad_box = (valid_float * foreground)[:, None] * jnp.clip(differ, -1.0, 1.0)
         grad_out = jnp.concatenate([grad_logits, grad_box], axis=1).astype(jnp.bfloat16)
         head_grads.append(
             jnp.einsum("rk,rf->kf", second_act, grad_out, preferred_element_type=jnp.float32)
@@ -219,25 +614,24 @@
         ).astype(jnp.bfloat16)
         grad_first_bias = jnp.sum(grad_first.astype(jnp.float32), axis=0)
         section_bias_grads.extend([grad_first_bias, grad_second_bias, grad_head_bias])
-        grad_pooled = jnp.einsum(
-            "rf,kf->rk", grad_first, first_matrix, preferred_element_type=jnp.float32
-        )
-        grad_pooled = grad_pooled.reshape(region_count, BINS, channels)
-        for corner in range(4):
-            grad_flat = grad_flat.at[corner_base + corner_shifts[corner]].add(
-                corner_weights[corner][:, :, None] * grad_pooled
-            )
-        dense_first = jnp.einsum(
-            "rk,rf->kf", roi_feats, grad_first, preferred_element_type=jnp.float32
-        )
-        dense_second = jnp.einsum(
-            "rk,rf->kf", first_act, grad_second, preferred_element_type=jnp.float32
-        )
-        dense_section = jnp.concatenate([dense_first, dense_second], axis=0).reshape(
-            section_blocks, block_rows, hidden
-        )
-        targets = lax.dynamic_slice_in_dim(owner_slot, section * section_blocks, section_blocks)
-        block_term = block_term.at[targets].set(dense_section)
+        grads_first.append(grad_first)
+        grads_second.append(grad_second)
+    acts_t = jnp.stack(acts_t)
+    grads_first = jnp.stack(grads_first)
+    grads_second = jnp.stack(grads_second)
+
+    sizes = []
+    for share in shares:
+        sizes += [(groups * share, block_rows, hidden)] * 2
+    parts = weight_grads(
+        order_list, place_list, offsets, feats_t, acts_t, grads_first, grads_second, sizes
+    )
+    block_parts = sum_parts(parts[0::2], parts[1::2], orders)
+
+    grad_flat = map_grads(
+        owner_slot, gathered, grads_first, sample_rows, sample_cols, fracs_row, fracs_col,
+        section_blocks, lines, breadth, channels,
+    )
     grad_padded_map = grad_flat.reshape(images, padded_rows, breadth, channels)
     outer_rims = jnp.concatenate(
         [grad_padded_map[:, :rim], grad_padded_map[:, rim + height :]], axis=1
@@ -264,24 +658,28 @@
     grad_conv = jnp.concatenate([grad_lateral_w, grad_taps], axis=0)
     grad_head = jnp.stack(head_grads)
     grad_bias = jnp.concatenate([grad_lateral_bias, grad_conv_bias] + section_bias_grads)
-    conv_sum, head_sum, bias_sum, loss_total = lax.psum(
-        (grad_conv, grad_head, grad_bias, loss_part), ("img", "tile")
-    )
-    block_grad = lax.psum_scatter(block_term, ("img", "tile"), scatter_dimension=0, tiled=True)
+    conv_sum, head_sum, bias_sum, loss_total, valid_sum = lax.psum(
+        (grad_conv, grad_head, grad_bias, loss_part, jnp.sum(valid_float)), AXES
+    )
+    scale = 1.0 / valid_sum
+    mine = lax.dynamic_slice_in_dim(slot_block, (at_img * n_tile + at_tile) * slots, slots)
+    block_grad = jnp.where(
+        (mine >= 0)[:, None, None], jnp.concatenate(block_parts, axis=0) * scale, 0.0
+    )
     step = float(STEP)
     conv_new, conv_first_new, conv_second_new = adamw(
-        conv_weight, conv_first, conv_second, conv_sum, step
+        conv_weight, conv_first, conv_second, conv_sum * scale, step
     )
     head_new, head_first_new, head_second_new = adamw(
-        head_weight, head_first, head_second, head_sum, step
+        head_weight, head_first, head_second, head_sum * scale, step
     )
     bias_new, bias_first_new, bias_second_new = adamw(
-        bias_vector, bias_first, bias_second, bias_sum, step
+        bias_vector, bias_first, bias_second, bias_sum * scale, step
     )
     block_new, block_first_new, block_second_new = adamw(
         block_master, block_first, block_second, block_grad, step
     )
-    loss = (loss_total / valid_sum).reshape(1)
+    loss = (loss_total * scale).reshape(1)
     return (
         loss,
         conv_new,
@@ -300,45 +698,22 @@
 
 
 def solution(mesh):
+    split = P(AXES, None, None)
     return jax.shard_map(
         on_device,
         mesh=mesh,
         in_specs=(
             P("img", "tile", None, None),
+            P(), P(), P(), P(), P(), P(), P(), P(), P(),
+            split, split, split,
             P(),
-            P(),
-            P(),
-            P(),
-            P(),
-            P(),
-            P(),
-            P(),
-            P(),
-            P(("img", "tile"), None, None),
-            P(("img", "tile"), None, None),
-            P(("img", "tile"), None, None),
-            P(),
-            P(("img", "tile")),
-            P(None, None, ("img", "tile")),
-            P(None, None, None, ("img", "tile")),
-            P(None, ("img", "tile")),
-            P(("img", "tile")),
-            P(None, None, ("img", "tile")),
+            P(AXES),
+            P(None, None, AXES),
+            P(None, None, None, AXES),
+            P(None, AXES),
+            P(AXES),
+            P(None, None, AXES),
         ),
-        out_specs=(
-            P(),
-            P(),
-            P(),
-            P(),
-            P(),
-            P(),
-            P(),
-            P(),
-            P(),
-            P(),
-            P(("img", "tile"), None, None),
-            P(("img", "tile"), None, None),
-            P(("img", "tile"), None, None),
-        ),
+        out_specs=(P(),) * 10 + (split,) * 3,
         check_vma=False,
     )

time: 6480 us -> 1600 us (0.25)
  waiting for transfers between devices: 3420 us -> 690 us
  local copies, waits for them, and re-layouts: 1490 us -> 36.8 us
  other arithmetic: 1150 us -> 147 us
  Pallas kernels: 0 us -> 431 us
  matrix products: 251 us -> 71.5 us
    reduce_scatter x1 -> x0, waiting for transfers between devices: 3410 us -> none  [on_device(): lax.psum_scatter(block_term, ('img', 'tile'), scatter_dimension=0, tiled=...]
    scatter-add x12 -> x0, other arithmetic: 877 us -> none  [on_device(): grad_flat.at[corner_base + corner_shifts[corner]]]
    gather x13 -> x3, local copies, waits for them, and re-layouts: 478 us -> 10.6 us  [on_device(): second_matrix = gathered[second_slots].reshape(hidden, hidden)]
    pallas_call x0 -> x4, Pallas kernels: none -> 431 us  [the longest x1 198 us: map_grads(): pl.pallas_call(body, grid_spec=pltpu.PrefetchScalarGridSpec(num_scalar_pr...]
    mul x24 -> x0, local copies, waits for them, and re-layouts: 384 us -> none  [on_device(): corner_weights[corner][:, :, None] * grad_pooled]
    scatter x3 -> x0, local copies, waits for them, and re-layouts: 317 us -> none  [on_device(): block_term = block_term.at[targets].set(dense_section)]
    all_gather x1, waiting for transfers between devices: 0.01 us -> 281 us  [on_device(): lax.all_gather(block_master.astype(jnp.bfloat16), AXES, axis=0, tiled=True)]
    dot_general x12 -> x0, matrix products: 198 us -> none  [the longest x3 79.7 us: on_device(): jnp.einsum('rf,kf->rk', grad_first, first_matrix, preferred_element_type=...]
  transfers between devices with their start and end apart: 11 -> 25, of which waited for: 4 -> 9; matrix products, arithmetic and copies ran while one was open for 19% -> 12% of each run, Pallas kernels for 0% -> 19%
where the time goes in v1:
time: 1600 us; the launch traced here: 1590 us
  waiting for transfers between devices  690 us (43%)
  Pallas kernels  431 us (27%)
  blocking collectives  158 us (10%)
  other arithmetic  147 us (9%)
  matrix products  71.5 us (4%)
  starting transfers between devices  40.4 us (3%)
  local copies, waits for them, and re-layouts  36.8 us (2%)
  between operations  20.3 us (1%)
    all_gather x1, waiting for transfers between devices, on_device(): lax.all_gather(block_master.astype(jnp.bfloat16), AXES, axis=0, tiled=True)  281 us
    pallas_call x1, Pallas kernels, map_grads(): pl.pallas_call(body, grid_spec=pltpu.PrefetchScalarGridSpec(num_scalar_pr...  198 us
    ppermute x4, waiting for transfers between devices, padded_2(): lax.ppermute(head, axis, [((i + 1) % count, i) for i in range(ends)])  183 us
    psum x1, blocking collectives, on_device(): lax.psum((grad_conv, grad_head, grad_bias, loss_part, jnp.sum(valid_float...  158 us
    ppermute x15, waiting for transfers between devices, swap(): return lax.ppermute(values, axis, [(i, i ^ 1 << bit) for i in range(count)])  114 us
    pallas_call x1, Pallas kernels, pool_regions(): pl.pallas_call(body, grid=(section_count, bins // group), in_specs=[pl.Bl...  109 us
    psum x1, waiting for transfers between devices, on_device(): lax.psum((grad_conv, grad_head, grad_bias, loss_part, jnp.sum(valid_float...  108 us
    convert_element_type x12, other arithmetic, add_low(): return (a.astype(jnp.float32) + b.astype(jnp.float32)).astype(jnp.bfloat16)  89.6 us
  transfers between devices with their start and end apart: 25, of which 9 were waited for; matrix products, arithmetic and copies ran while one was open for 12% of the time, Pallas kernels for 19%

profile of v1, /device:TPU:0, one launch (start us, length us, event | category | flops | bytes accessed | tf_op | source)
XLA Modules:
  0.0 1594.6 jit_solution(3683626875609853764)
XLA Ops:
  7.2 4.5 convert_element_type.364
  11.8 1.9 convert_element_type.365
  17.4 5.5 collective-permute-start
  22.9 5.2 scatter_custom_fusion.table_ref
  32.6 3.0 fusion.144
  36.5 5.2 sort.31
  52.0 5.7 collective-permute-start.2
  58.5 4.2 collective-permute-done.3
  62.6 4.1 collective-permute-done.2
  67.0 2.3 copy.108
  69.2 108.7 %pool_regions.1.x_ref = bf16[3,49,256,256]{3,2,1,0:T(8,128)(2,1)} custom-call(bf16[256,3840]{1,0:T(8,128)(2,1)} %bitcast.292, s32[3,49,256]{2,1,0:T(8,128)} %get-tuple-element.128.row_ref, s32[3,49,256]{2,1,0:T(8,128)} %get-tuple-element.127.col_ref, f32[3,49,256]{2,1,0:T(8,128)} %get-tuple-element.183.fr_ref, f32[3,49,256]{2,1,0:T(8,128)} %get-tuple-element.182.fc_ref), custom_call_target="tpu_custom_call" | custom-call | flops 73987522560 | bytes 19267584 | tf_op jit(solution)/shard_map/pool_regions/pallas_call | solution.py:136
  177.9 281.1 %all-gather.2.cloned.1.call-done.blocks_ref = bf16[1280,32,1024]{2,1,0:T(8,128)(2,1)} async-done(((bf16[40,32,1024]{2,1,0:T(8,128)(2,1)}), bf16[1280,32,1024]{2,1,0:T(8,128)(2,1)}) %all-gather.2.cloned.1.call-update) | async-done | bytes 83886096 | tf_op jit(solution)/shard_map/all_gather | solution.py:495
  459.0 58.0 %first_layer.1 = f32[3,256,1024]{2,1,0:T(8,128)} custom-call(s32[1272]{0:T(1024)} %copy-done.62, bf16[1280,32,1024]{2,1,0:T(8,128)(2,1)} %all-gather.2.cloned.1.call-done.blocks_ref, bf16[3,49,256,256]{3,2,1,0:T(8,128)(2,1)} %pool_regions.1.x_ref), custom_call_target="tpu_custom_call" | custom-call | flops 19730006016 | bytes 96337920 | tf_op jit(solution)/shard_map/first_layer/pallas_call | solution.py:207
  517.0 3.6 gather_fusion
  520.6 3.7 multiply_convert_fusion.7
  525.6 3.6 gather_fusion.1
  529.2 3.8 multiply_convert_fusion.5
  534.2 1.8 fusion.135
  536.0 3.5 gather_fusion.2
  539.7 2.8 multiply_convert_fusion.3
  546.7 2.4 convert_reduce_fusion.3
  550.7 2.4 convert_reduce_fusion.5
  554.6 2.4 convert_reduce_fusion.7
  558.8 2.6 pad_maximum_fusion.1.g_ref.gf_ref
  562.8 66.3 %weight_grads.1 = (bf16[240,32,1024]{2,1,0:T(8,128)(2,1)}, bf16[240,32,1024]{2,1,0:T(8,128)(2,1)}, bf16[224,32,1024]{2,1,0:T(8,128)(2,1)}, bf16[224,32,1024]{2,1...) custom-call(s32[1272]{0:T(1024)} %get-tuple-element.48.order_ref, ...), custom_call_target="tpu_custom_call" | custom-call | flops 21340618752 | bytes 104202240 | tf_op jit(solution)/shard_map/weight_grads/pallas_call | solution.py:306
  629.6 4.0 fusion.214
  633.8 197.8 %map_grads.1 = f32[3840,256]{1,0:T(8,128)} custom-call(s32[1272]{0:T(1024)} %copy-done.62, bf16[1280,32,1024]{2,1,0:T(8,128)(2,1)} %all-gather.2.cloned.1.call-done.blocks_ref, bf16[3,256,1024]{2,1,0:T(8,128)(2,1)} %pad_maximum_fusion.1.g_ref.gf_ref, s32[3,49,256]{2,1,0:T(8,128)} %get-tuple-element.128.row_ref, s32[3,49,256]{2,1,0:T(8,128)} %get-tuple-element.127.col_ref, ...), custom_call_target="tpu_custom_call" | custom-call | flops 93717528576 | bytes 77070336 | tf_op jit(solution)/shard_map/map_grads/pallas_call | solution.py:389
  833.0 3.4 collective-permute-start.4
  836.4 15.1 add_convert_fusion.3
  852.1 16.1 %add_convert_fusion.1 = (bf16[120,32,1024]{2,1,0:T(8,128)(2,1)S(1)}, bf16[120,32,1024]{2,1,0:T(8,128)(2,1)}) fusion(bf16[240,32,1024]{2,1,0:T(8,128)(2,1)} %collective-permute-done.8, bf16[240,32,1024]{2,1,0:T(8,128)(2,1)} %get-tuple-element.50), kind=kLoop, calls=%fused_computation.5 | loop fusion | flops 31457280 | bytes 47185920 | tf_op jit(solution)/shard_map/convert_element_type | solution.py:439
  874.8 178.4 %collective-permute-done.5 = f32[2,2,160,256]{3,2,1,0:T(8,128)S(1)} collective-permute-done((f32[2,2,160,256]{3,2,1,0:T(8,128)S(1)}, f32[2,2,160,256]{3,2,1,0:T(8,128)S(1)}, u32[]{:S(2)}, u32[]{:S(2)}) %collective-permute-start.5) | collective-permute-done | bytes 655392 | tf_op jit(solution)/shard_map/ppermute | solution.py:33
  1055.2 4.6 collective-permute-start.6
  1059.8 13.7 add_convert_fusion.5
  1074.7 2.0 fusion.143
  1076.7 2.0 fusion.17
  1078.8 2.0 fusion.13
  1081.7 2.0 fusion.25
  1083.7 2.0 fusion.27
  1085.7 2.0 fusion.29
  1087.8 2.0 fusion.31
  1089.8 2.1 fusion.33
  1091.9 9.4 convert_reduce_fusion.1
  1101.3 2.7 fusion.67
  1105.3 7.7 add_convert_fusion.9
  1113.9 8.4 add_convert_fusion.7
  1123.7 77.4 %collective-permute-done.19 = bf16[88,32,1024]{2,1,0:T(8,128)(2,1)} collective-permute-done((bf16[88,32,1024]{2,1,0:T(8,128)(2,1)}, bf16[88,32,1024]{2,1,0:T(8,128)(2,1)}, u32[]{:S(2)}, u32[]{:S(2)}) %collective-permute-start.19) | collective-permute-done | bytes 5767200 | tf_op jit(solution)/shard_map/ppermute | solution.py:435
  1201.0 6.4 add_convert_fusion.11
  1222.5 157.9 %all-reduce.2 = (f32[]{:T(128)}, f32[]{:T(128)}, f32[6911]{0:T(1024)S(1)}) all-reduce(f32[]{:T(128)S(6)} %add.550, f32[]{:T(128)} %get-tuple-element.65, f32[6911]{0:T(1024)S(1)} %concatenate.57), channel_id=1, replica_groups=mesh['img'=4,'tile'=8] {'img','tile'}, use_global_device_ids=true, to_apply=%region_16.17 | all-reduce | flops 6913 | bytes 55304 | tf_op jit(solution)/shard_map/psum | solution.py:661
  1381.8 6.1 add_convert_fusion.17
  1387.9 2.3 collective-permute-start.21
  1390.2 5.9 add_convert_fusion.15
  1396.1 2.2 collective-permute-start.16
  1398.4 5.5 add_convert_fusion.13
  1405.2 108.4 %all-reduce.6.cloned.1.call-done = (f32[2560,256]{1,0:T(8,128)}, f32[3,1024,85]{1,2,0:T(8,128)}) async-done(((f32[2560,256]{1,0:T(8,128)}, f32[3,1024,85]{1,2,0:T(8,128)}), (f32[2560,256]{1,0:T(8,128)}, f32[3,1024,85]{1,2,0:T(8,128)})) %all-reduce.6.cloned.1.call-update) | async-done | bytes 3665936 | tf_op jit(solution)/shard_map/psum | solution.py:661
  1513.5 8.7 multiply_subtract_fusion.1
  1525.1 1.7 add_convert_fusion.23
  1529.2 1.8 collective-permute-start.12
  1531.0 2.3 multiply_subtract_fusion.2
  1533.3 6.6 collective-permute-done.22
  1541.4 5.9 collective-permute-done.17
  1547.2 1.7 convert_add_fusion.1
  1548.9 24.1 %collective-permute-done.12 = bf16[15,32,1024]{2,1,0:T(8,128)(2,1)S(1)} collective-permute-done((bf16[15,32,1024]{2,1,0:T(8,128)(2,1)S(1)}, bf16[15,32,1024]{2,1,0:T(8,128)(2,1)S(1)}, u32[]{:S(2)}, u32[]{:S(2)}) %collective-permute-start.12) | collective-permute-done | bytes 983072 | tf_op jit(solution)/shard_map/ppermute | solution.py:435
  1573.0 1.7 convert_add_fusion
  1574.8 11.3 multiply_subtract_fusion
  (343 shorter events, 70.8 us)
Async XLA Ops:
  7.2 7.6 copy-start
  7.2 451.8 %all-gather.2.cloned.1.call-start = ((), (), s32[]{:S(2)}) async-start(), calls=%async_computation | async-start | bytes 86507520 | tf_op jit(solution)/shard_map/all_gather | solution.py:495
  11.8 1501.7 %all-reduce.6.cloned.1.call-start = ((), (), s32[]{:S(2)}) async-start(), calls=%async_computation.1 | async-start | bytes 7405568 | tf_op jit(solution)/shard_map/psum | solution.py:661
  13.7 9.2 copy-start.87
  13.7 14.5 copy-start.105
  13.7 15.7 copy-start.100
  13.8 15.7 copy-start.85
  13.8 17.6 %copy-start.59 = (s32[3,49,256]{2,1,0:T(8,128)S(1)}, s32[3,49,256]{2,1,0:T(8,128)}, u32[]{:S(2)}) copy-start(s32[3,49,256]{2,1,0:T(8,128)} %param.42) | copy-start | bytes 451588
  13.8 18.5 %copy-start.58 = (f32[3,2,49,256]{3,1,2,0:T(2,128)S(1)}, f32[3,2,49,256]{3,1,2,0:T(2,128)}, u32[]{:S(2)}) copy-start(f32[3,2,49,256]{3,1,2,0:T(2,128)} %param.43) | copy-start | bytes 903172
  15.3 29.2 %copy-start.3 = (bf16[2,8,160,256]{3,2,1,0:T(8,128)(2,1)}, bf16[2,8,160,256]{3,2,1,0:T(8,128)(2,1)S(1)}, u32[]{:S(2)}) copy-start(bf16[2,8,160,256]{3,2,1,0:T(8,128)(2,1)S(1)} %add_convert_fusion.20) | copy-start | bytes 3932164
  16.1 26.3 %collective-permute-start.1 = (bf16[2,1,160,256]{3,2,1,0:T(8,128)(2,1)}, bf16[2,1,160,256]{3,2,1,0:T(8,128)(2,1)S(1)}, u32[]{:S(2)}, u32[]{:S(2)}) collective-permute-start(bf16[2,1,160,256]{3,2,1,0:T(8,128)(2,1)} %get-tuple-element.124), channel_id=1, source_target_pairs={{1,0},{2,1},{3,2},{4,3},{5,4},{6,5},{7,6},{9,8},{10,9},{11,10},{12... | collective-permute-start | bytes 491528 | tf_op jit(solution)/shard_map/ppermute | solution.py:33
  17.4 26.5 %collective-permute-start = (bf16[2,1,160,256]{3,2,1,0:T(8,128)(2,1)}, bf16[2,1,160,256]{3,2,1,0:T(8,128)(2,1)S(1)}, u32[]{:S(2)}, u32[]{:S(2)}) collective-permute-start(bf16[2,1,160,256]{3,2,1,0:T(8,128)(2,1)} %get-tuple-element.123), channel_id=1, source_target_pairs={{0,1},{1,2},{2,3},{3,4},{4,5},{5,6},{6,7},{8,9},{9,10},{10,11},{11... | collective-permute-start | bytes 491528 | tf_op jit(solution)/shard_map/ppermute | solution.py:31
  49.3 8.4 copy-start.101
  50.7 12.0 collective-permute-start.3
  52.0 14.7 collective-permute-start.2
  520.6 4.5 copy-start.18
  520.6 4.5 copy-start.104
  520.6 4.9 copy-start.71
  529.1 4.7 copy-start.103
  529.1 5.0 copy-start.73
  529.1 5.1 copy-start.7
  529.1 5.0 copy-start.82
  543.1 6.0 copy-start.76
  543.1 10.0 copy-start.78
  543.9 5.2 copy-start.54
  543.9 9.2 copy-start.56
  545.1 4.0 copy-start.45
  562.8 66.9 %copy-start.2 = (bf16[2,10,162,256]{3,2,1,0:T(8,128)(2,1)S(1)}, bf16[2,10,162,256]{3,2,1,0:T(8,128)(2,1)}, u32[]{:S(2)}) copy-start(bf16[2,10,162,256]{3,2,1,0:T(8,128)(2,1)} %copy-done.1) | copy-start | bytes 4976644
  629.1 207.4 %collective-permute-start.13 = (bf16[224,32,1024]{2,1,0:T(8,128)(2,1)}, bf16[224,32,1024]{2,1,0:T(8,128)(2,1)}, u32[]{:S(2)}, u32[]{:S(2)}) collective-permute-start(bf16[224,32,1024]{2,1,0:T(8,128)(2,1)} %get-tuple-element.53), channel_id=1, source_target_pairs={{0,8},{8,0},{16,24},{24,16},{1,9},{9,1},{17,25},{25,17},{2,10},{10... | collective-permute-start | bytes 44040200 | tf_op jit(solution)/shard_map/ppermute | solution.py:435
  629.3 222.8 %collective-permute-start.8 = (bf16[240,32,1024]{2,1,0:T(8,128)(2,1)}, bf16[240,32,1024]{2,1,0:T(8,128)(2,1)}, u32[]{:S(2)}, u32[]{:S(2)}) collective-permute-start(bf16[240,32,1024]{2,1,0:T(8,128)(2,1)} %get-tuple-element.51), channel_id=1, source_target_pairs={{0,8},{8,0},{16,24},{24,16},{1,9},{9,1},{17,25},{25,17},{2,10},{10... | collective-permute-start | bytes 47185928 | tf_op jit(solution)/shard_map/ppermute | solution.py:435
  633.7 426.1 %collective-permute-start.18 = (bf16[176,32,1024]{2,1,0:T(8,128)(2,1)}, bf16[176,32,1024]{2,1,0:T(8,128)(2,1)}, u32[]{:S(2)}, u32[]{:S(2)}) collective-permute-start(bf16[176,32,1024]{2,1,0:T(8,128)(2,1)} %get-tuple-element.55), channel_id=1, source_target_pairs={{0,8},{8,0},{16,24},{24,16},{1,9},{9,1},{17,25},{25,17},{2,10},{10... | collective-permute-start | bytes 34603016 | tf_op jit(solution)/shard_map/ppermute | solution.py:435
  833.0 41.7 %collective-permute-start.4 = (f32[2,2,160,256]{3,2,1,0:T(8,128)S(1)}, f32[2,2,160,256]{3,2,1,0:T(8,128)S(1)}, u32[]{:S(2)}, u32[]{:S(2)}) collective-permute-start(f32[2,2,160,256]{3,2,1,0:T(8,128)S(1)} %get-tuple-element.107), channel_id=1, source_target_pairs={{0,1},{1,2},{2,3},{3,4},{4,5},{5,6},{6,7},{8,9},{9,10},{10,11},{11... | collective-permute-start | bytes 1966088 | tf_op jit(solution)/shard_map/ppermute | solution.py:31
  851.5 253.8 %collective-permute-start.14 = (bf16[112,32,1024]{2,1,0:T(8,128)(2,1)}, bf16[112,32,1024]{2,1,0:T(8,128)(2,1)}, u32[]{:S(2)}, u32[]{:S(2)}) collective-permute-start(bf16[112,32,1024]{2,1,0:T(8,128)(2,1)} %get-tuple-element.91), channel_id=1, source_target_pairs={{0,16},{8,24},{16,0},{24,8},{1,17},{9,25},{17,1},{25,9},{2,18},{10... | collective-permute-start | bytes 22020104 | tf_op jit(solution)/shard_map/ppermute | solution.py:435
  852.1 16.7 %copy-start.4 = (bf16[2,8,160,256]{3,2,1,0:T(8,128)(2,1)S(1)}, bf16[2,8,160,256]{3,2,1,0:T(8,128)(2,1)}, u32[]{:S(2)}) copy-start(bf16[2,8,160,256]{3,2,1,0:T(8,128)(2,1)} %copy-done.3) | copy-start | bytes 3932164
  852.1 16.7 %copy-start.31 = (bf16[2,1,160,256]{3,2,1,0:T(8,128)(2,1)S(1)}, bf16[2,1,160,256]{3,2,1,0:T(8,128)(2,1)}, u32[]{:S(2)}) copy-start(bf16[2,1,160,256]{3,2,1,0:T(8,128)(2,1)} %copy-done.30) | copy-start | bytes 491524
  852.1 16.7 %copy-start.33 = (bf16[2,1,160,256]{3,2,1,0:T(8,128)(2,1)S(1)}, bf16[2,1,160,256]{3,2,1,0:T(8,128)(2,1)}, u32[]{:S(2)}) copy-start(bf16[2,1,160,256]{3,2,1,0:T(8,128)(2,1)} %copy-done.32) | copy-start | bytes 491524
  868.2 245.7 %collective-permute-start.9 = (bf16[120,32,1024]{2,1,0:T(8,128)(2,1)}, bf16[120,32,1024]{2,1,0:T(8,128)(2,1)}, u32[]{:S(2)}, u32[]{:S(2)}) collective-permute-start(bf16[120,32,1024]{2,1,0:T(8,128)(2,1)} %get-tuple-element.89), channel_id=1, source_target_pairs={{0,1},{1,0},{2,3},{3,2},{4,5},{5,4},{6,7},{7,6},{8,9},{9,8},{10,11... | collective-permute-start | bytes 23592968 | tf_op jit(solution)/shard_map/ppermute | solution.py:435
  871.5 181.8 %collective-permute-start.5 = (f32[2,2,160,256]{3,2,1,0:T(8,128)S(1)}, f32[2,2,160,256]{3,2,1,0:T(8,128)S(1)}, u32[]{:S(2)}, u32[]{:S(2)}) collective-permute-start(f32[2,2,160,256]{3,2,1,0:T(8,128)S(1)} %get-tuple-element.106), channel_id=1, source_target_pairs={{1,0},{2,1},{3,2},{4,3},{5,4},{6,5},{7,6},{9,8},{10,9},{11,10},{12... | collective-permute-start | bytes 1966088 | tf_op jit(solution)/shard_map/ppermute | solution.py:33
  1053.9 24.9 %collective-permute-start.7 = (bf16[2,1,160,256]{3,2,1,0:T(8,128)(2,1)S(1)}, bf16[2,1,160,256]{3,2,1,0:T(8,128)(2,1)S(1)}, u32[]{:S(2)}, u32[]{:S(2)}) collective-permute-start(bf16[2,1,160,256]{3,2,1,0:T(8,128)(2,1)S(1)} %get-tuple-element.119), channel_id=1, source_target_pairs={{1,0},{2,1},{3,2},{4,3},{5,4},{6,5},{7,6},{9,8},{10,9},{11,10},{12... | collective-permute-start | bytes 491528 | tf_op jit(solution)/shard_map/ppermute | solution.py:33
  1055.2 21.5 %collective-permute-start.6 = (bf16[2,1,160,256]{3,2,1,0:T(8,128)(2,1)S(1)}, bf16[2,1,160,256]{3,2,1,0:T(8,128)(2,1)S(1)}, u32[]{:S(2)}, u32[]{:S(2)}) collective-permute-start(bf16[2,1,160,256]{3,2,1,0:T(8,128)(2,1)S(1)} %get-tuple-element.120), channel_id=1, source_target_pairs={{0,1},{1,2},{2,3},{3,4},{4,5},{5,6},{6,7},{8,9},{9,10},{10,11},{11... | collective-permute-start | bytes 491528 | tf_op jit(solution)/shard_map/ppermute | solution.py:31
  1059.8 14.9 copy-start.11
  1073.5 127.5 %collective-permute-start.19 = (bf16[88,32,1024]{2,1,0:T(8,128)(2,1)}, bf16[88,32,1024]{2,1,0:T(8,128)(2,1)}, u32[]{:S(2)}, u32[]{:S(2)}) collective-permute-start(bf16[88,32,1024]{2,1,0:T(8,128)(2,1)} %get-tuple-element.93), channel_id=1, source_target_pairs={{0,2},{1,3},{2,0},{3,1},{4,6},{5,7},{6,4},{7,5},{8,10},{9,11},{10,... | collective-permute-start | bytes 17301512 | tf_op jit(solution)/shard_map/ppermute | solution.py:435
  1113.1 277.1 %collective-permute-start.15 = (bf16[56,32,1024]{2,1,0:T(8,128)(2,1)}, bf16[56,32,1024]{2,1,0:T(8,128)(2,1)}, u32[]{:S(2)}, u32[]{:S(2)}) collective-permute-start(bf16[56,32,1024]{2,1,0:T(8,128)(2,1)} %get-tuple-element.97), channel_id=1, source_target_pairs={{0,2},{1,3},{2,0},{3,1},{4,6},{5,7},{6,4},{7,5},{8,10},{9,11},{10,... | collective-permute-start | bytes 11010056 | tf_op jit(solution)/shard_map/ppermute | solution.py:435
  1122.3 276.1 %collective-permute-start.10 = (bf16[60,32,1024]{2,1,0:T(8,128)(2,1)}, bf16[60,32,1024]{2,1,0:T(8,128)(2,1)}, u32[]{:S(2)}, u32[]{:S(2)}) collective-permute-start(bf16[60,32,1024]{2,1,0:T(8,128)(2,1)} %get-tuple-element.95), channel_id=1, source_target_pairs={{0,16},{8,24},{16,0},{24,8},{1,17},{9,25},{17,1},{25,9},{2,18},{10... | collective-permute-start | bytes 11796488 | tf_op jit(solution)/shard_map/ppermute | solution.py:435
  1201.0 7.8 copy-start.35
  1207.4 174.4 %collective-permute-start.20 = (bf16[44,32,1024]{2,1,0:T(8,128)(2,1)}, bf16[44,32,1024]{2,1,0:T(8,128)(2,1)}, u32[]{:S(2)}, u32[]{:S(2)}) collective-permute-start(bf16[44,32,1024]{2,1,0:T(8,128)(2,1)} %get-tuple-element.99), channel_id=1, source_target_pairs={{0,4},{1,5},{2,6},{3,7},{4,0},{5,1},{6,2},{7,3},{8,12},{9,13},{10,... | collective-permute-start | bytes 8650760 | tf_op jit(solution)/shard_map/ppermute | solution.py:435
  1381.8 8.4 copy-start.6
  1387.9 134.3 %collective-permute-start.21 = (bf16[22,32,1024]{2,1,0:T(8,128)(2,1)}, bf16[22,32,1024]{2,1,0:T(8,128)(2,1)}, u32[]{:S(2)}, u32[]{:S(2)}) collective-permute-start(bf16[22,32,1024]{2,1,0:T(8,128)(2,1)} %get-tuple-element.105), channel_id=1, source_target_pairs={{0,1},{1,0},{2,3},{3,2},{4,5},{5,4},{6,7},{7,6},{8,9},{9,8},{10,11... | collective-permute-start | bytes 4325384 | tf_op jit(solution)/shard_map/ppermute | solution.py:435
  1390.2 8.2 copy-start.5
  1396.1 128.9 %collective-permute-start.16 = (bf16[28,32,1024]{2,1,0:T(8,128)(2,1)}, bf16[28,32,1024]{2,1,0:T(8,128)(2,1)}, u32[]{:S(2)}, u32[]{:S(2)}) collective-permute-start(bf16[28,32,1024]{2,1,0:T(8,128)(2,1)} %get-tuple-element.103), channel_id=1, source_target_pairs={{0,4},{1,5},{2,6},{3,7},{4,0},{5,1},{6,2},{7,3},{8,12},{9,13},{10,... | collective-permute-start | bytes 5505032 | tf_op jit(solution)/shard_map/ppermute | solution.py:435
  1398.4 6.1 copy-start.61
  1398.4 6.1 copy-start.66
  1398.4 6.1 copy-start.67
  1403.9 123.8 %collective-permute-start.11 = (bf16[30,32,1024]{2,1,0:T(8,128)(2,1)}, bf16[30,32,1024]{2,1,0:T(8,128)(2,1)}, u32[]{:S(2)}, u32[]{:S(2)}) collective-permute-start(bf16[30,32,1024]{2,1,0:T(8,128)(2,1)} %get-tuple-element.101), channel_id=1, source_target_pairs={{0,2},{1,3},{2,0},{3,1},{4,6},{5,7},{6,4},{7,5},{8,10},{9,11},{10,... | collective-permute-start | bytes 5898248 | tf_op jit(solution)/shard_map/ppermute | solution.py:435
  1513.5 8.7 copy-start.14
  1523.7 16.2 %collective-permute-start.22 = (bf16[11,32,1024]{2,1,0:T(8,128)(2,1)S(1)}, bf16[11,32,1024]{2,1,0:T(8,128)(2,1)S(1)}, u32[]{:S(2)}, u32[]{:S(2)}) collective-permute-start(bf16[11,32,1024]{2,1,0:T(8,128)(2,1)S(1)} %add_convert_fusion.25), channel_id=1, source_target_pairs={{0,16},{8,24},{16,0},{24,8},{1,17},{9,25},{17,1},{25,9},{2,18},{10... | collective-permute-start | bytes 2162696 | tf_op jit(solution)/shard_map/ppermute | solution.py:435
  1525.1 5.9 copy-start.43
  1525.1 5.9 copy-start.44
  1526.8 4.2 copy-start.17
  1526.8 4.2 copy-start.42
  1526.8 20.4 %collective-permute-start.17 = (bf16[14,32,1024]{2,1,0:T(8,128)(2,1)S(1)}, bf16[14,32,1024]{2,1,0:T(8,128)(2,1)S(1)}, u32[]{:S(2)}, u32[]{:S(2)}) collective-permute-start(bf16[14,32,1024]{2,1,0:T(8,128)(2,1)S(1)} %add_convert_fusion.23), channel_id=1, source_target_pairs={{0,1},{1,0},{2,3},{3,2},{4,5},{5,4},{6,7},{7,6},{8,9},{9,8},{10,11... | collective-permute-start | bytes 2752520 | tf_op jit(solution)/shard_map/ppermute | solution.py:435
  1529.2 43.8 %collective-permute-start.12 = (bf16[15,32,1024]{2,1,0:T(8,128)(2,1)S(1)}, bf16[15,32,1024]{2,1,0:T(8,128)(2,1)S(1)}, u32[]{:S(2)}, u32[]{:S(2)}) collective-permute-start(bf16[15,32,1024]{2,1,0:T(8,128)(2,1)S(1)} %add_convert_fusion.21), channel_id=1, source_target_pairs={{0,4},{1,5},{2,6},{3,7},{4,0},{5,1},{6,2},{7,3},{8,12},{9,13},{10,... | collective-permute-start | bytes 2949128 | tf_op jit(solution)/shard_map/ppermute | solution.py:435
  1531.0 43.8 %slice-start = ((s8[5242880]{0:T(1024)(128)(4,1)}), s8[4194304]{0:T(1024)(128)(4,1)S(1)}, s32[]{:S(2)}) async-start(s8[5242880]{0:T(1024)(128)(4,1)} %bitcast.280), calls=%async_computation.2 | async-start | bytes 8388608
  1533.3 41.5 %slice-start.1 = ((s8[5242880]{0:T(1024)(128)(4,1)}), s8[1048576]{0:T(1024)(128)(4,1)S(1)}, s32[]{:S(2)}) async-start(s8[5242880]{0:T(1024)(128)(4,1)} %bitcast.280), calls=%async_computation.3 | async-start | bytes 2097152
  (74 other events, 179.5 us)
Sparse Core Ops, SparseCore 0:
  11.9 447.0 all-gather.1
  1219.4 294.0 all-reduce.5

commit v2 on v1

--- a/solution.py
+++ b/solution.py
@@ -334,29 +334,32 @@
     )(order, place, offsets, feats_t, acts_t, grads_first, grads_second)
 
 
-def map_grads(table, blocks, grads_first, rows, cols, fracs_row, fracs_col, section_blocks, lines, breadth, channels):
+def map_grads(before, span, table, blocks, grads_first, rows, cols, fracs_row, fracs_col, section_blocks, lines, breadth, after):
     section_count, bins, regions = rows.shape
     _, block_rows, hidden = blocks.shape
+    cells, channels = before.shape
     group = POOL
+    chunk = 8
     turns = bins // group
     count = group * channels // block_rows
-    cells = lines * breadth
-
-    def body(table_ref, blocks_ref, g_ref, row_ref, col_ref, fr_ref, fc_ref, out_ref, buffer, sem):
-        u, t = pl.program_id(0), pl.program_id(1)
-        step = u * turns + t
+    start, stop = span
+
+    def body(table_ref, blocks_ref, g_ref, row_ref, col_ref, fr_ref, fc_ref, old_ref, after_ref, out_ref, buffer, sem, pooled, across, down, weights_a, weights_b):
+        del after_ref
+        step = start + pl.program_id(0)
         slot = lax.rem(step, 2)
+        t = lax.rem(step, turns)
 
         def fetch(at, into):
             base = (at // turns) * section_blocks + lax.rem(at, turns) * count
             fetch_blocks(table_ref, blocks_ref, buffer, sem, base, into, count, block_rows)
 
-        @pl.when(step == 0)
+        @pl.when(step == start)
         def _():
-            out_ref[...] = jnp.zeros_like(out_ref)
             fetch(step, slot)
-
-        @pl.when(step + 1 < section_count * turns)
+            out_ref[...] = old_ref[...]
+
+        @pl.when(step + 1 < stop)
         def _():
             fetch(step + 1, 1 - slot)
 
@@ -365,69 +368,132 @@
         def one_bin(b, carry):
             p = t * group + b
             at = pl.ds(pl.multiple_of(b * channels, channels), channels)
-            pooled = lax.dot_general(
+            pooled[at] = lax.dot_general(
                 g_ref[0],
                 buffer[slot, at],
                 (((1,), (1,)), ((), ())),
                 preferred_element_type=jnp.float32,
             ).astype(jnp.bfloat16)
+            here = pl.ds(pl.multiple_of(b * regions, regions), regions)
+            across[:, here] = column_weights(
+                col_ref[0, pl.ds(p, 1), :], fc_ref[0, pl.ds(p, 1), :], breadth
+            ).astype(jnp.bfloat16)
             row = row_ref[0, pl.ds(p, 1), :]
             frow = fr_ref[0, pl.ds(p, 1), :]
-            across = column_weights(
-                col_ref[0, pl.ds(p, 1), :], fc_ref[0, pl.ds(p, 1), :], breadth
+            at_line = lax.broadcasted_iota(jnp.int32, (lines, regions), 0)
+            down[:, here] = row_weight(row, frow, at_line)
+            return carry
+
+        lax.fori_loop(0, group, one_bin, 0)
+
+        def build(first, into):
+            for i in range(chunk):
+                into[i * breadth : (i + 1) * breadth] = across[...] * down[
+                    first + i : first + i + 1, :
+                ].astype(jnp.bfloat16)
+
+        stores = (weights_a, weights_b)
+        build(0, stores[0])
+        for turn in range(lines // chunk):
+            if turn + 1 < lines // chunk:
+                build((turn + 1) * chunk, stores[(turn + 1) % 2])
+            at = slice(turn * chunk * breadth, (turn + 1) * chunk * breadth)
+            out_ref[at] += jnp.dot(
+                stores[turn % 2][...], pooled[...], preferred_element_type=jnp.float32
             )
-            for line in range(lines):
-                weights = (across * row_weight(row, frow, line)).astype(jnp.bfloat16)
-                out_ref[line * breadth : (line + 1) * breadth] += jnp.dot(
-                    weights, pooled, preferred_element_type=jnp.float32
-                )
-            return carry
-
-        lax.fori_loop(0, group, one_bin, 0)
-
-    samples = pl.BlockSpec((1, bins, regions), lambda u, t, _: (u, 0, 0))
+
+    samples = pl.BlockSpec((1, bins, regions), lambda i, _: ((start + i) // turns, 0, 0))
+    whole = pl.BlockSpec((cells, channels), lambda i, _: (0, 0))
     return pl.pallas_call(
         body,
         grid_spec=pltpu.PrefetchScalarGridSpec(
             num_scalar_prefetch=1,
-            grid=(section_count, turns),
+            grid=(stop - start,),
             in_specs=[
                 pl.BlockSpec(memory_space=pl.ANY),
-                pl.BlockSpec((1, regions, hidden), lambda u, t, _: (u, 0, 0)),
+                pl.BlockSpec((1, regions, hidden), lambda i, _: ((start + i) // turns, 0, 0)),
             ]
-            + [samples] * 4,
-            out_specs=pl.BlockSpec((cells, channels), lambda u, t, _: (0, 0)),
+            + [samples] * 4
+            + [whole, pl.BlockSpec(memory_space=pl.ANY)],
+            out_specs=whole,
             scratch_shapes=[
                 pltpu.VMEM((2, count * block_rows, hidden), jnp.bfloat16),
                 pltpu.SemaphoreType.DMA((2,)),
+                pltpu.VMEM((group * channels, channels), jnp.bfloat16),
+                pltpu.VMEM((breadth, group * regions), jnp.bfloat16),
+                pltpu.VMEM((lines, group * regions), jnp.float32),
+                pltpu.VMEM((chunk * breadth, group * regions), jnp.bfloat16),
+                pltpu.VMEM((chunk * breadth, group * regions), jnp.bfloat16),
             ],
         ),
         out_shape=jax.ShapeDtypeStruct((cells, channels), jnp.float32),
         compiler_params=pltpu.CompilerParams(vmem_limit_bytes=VMEM_LIMIT),
         cost_estimate=pl.CostEstimate(
-            flops=2 * section_count * bins * regions * channels * (hidden + cells),
-            bytes_accessed=section_count * bins * channels * hidden * 2,
+            flops=2 * (stop - start) * group * regions * channels * (hidden + cells),
+            bytes_accessed=(stop - start) * count * block_rows * hidden * 2,
             transcendentals=0,
         ),
         name="map_grads",
-    )(table, blocks, grads_first, rows, cols, fracs_row, fracs_col)
+    )(table, blocks, grads_first, rows, cols, fracs_row, fracs_col, before, after)
+
+
+def sum_blocks(terms, half, after):
+    _, block_rows, hidden = terms[0].shape
+    batch = max(b for b in range(1, 17) if half % b == 0)
+    count = len(terms)
+
+    def body(*refs):
+        total = None
+        for ref in refs[:count]:
+            value = ref[...].astype(jnp.float32)
+            total = value if total is None else total + value
+        refs[-1][...] = total.astype(jnp.bfloat16)
+
+    return pl.pallas_call(
+        body,
+        grid=(half // batch,),
+        in_specs=[
+            pl.BlockSpec((batch, block_rows, hidden), lambda i: (i + half // batch, 0, 0))
+        ] * count
+        + [pl.BlockSpec(memory_space=pl.ANY)],
+        out_specs=pl.BlockSpec((batch, block_rows, hidden), lambda i: (i, 0, 0)),
+        out_shape=jax.ShapeDtypeStruct((half, block_rows, hidden), jnp.bfloat16),
+        compiler_params=pltpu.CompilerParams(vmem_limit_bytes=VMEM_LIMIT),
+        cost_estimate=pl.CostEstimate(
+            flops=half * block_rows * hidden * count,
+            bytes_accessed=half * block_rows * hidden * 2 * (count + 1),
+            transcendentals=0,
+        ),
+        name="sum_blocks",
+    )(*terms, after)
 
 
 def bits_of(count):
     return list(range(count.bit_length() - 1))
 
 
+PARTS = ((7, "zwxy"), (7, "yxzw"), (10, "xzyw"), (10, "yxzw"), (6, "zwxy"))
+TURNS_AT = {0: 5, 5: 6, 7: 3, 8: 2, 10: 5}
+REST_AT = 15
+
+
 def part_orders(n_img, n_tile):
-    low = [("tile", b) for b in bits_of(n_tile)[:1]]
-    high = [("tile", b) for b in bits_of(n_tile)[1:]]
-    side = [("img", b) for b in bits_of(n_img)[1:]]
-    return [low + side + high, side + high + low, high + low + side]
+    bits = {
+        "x": [("tile", b) for b in bits_of(n_tile)[:1]],
+        "y": [("img", b) for b in bits_of(n_img)[1:]],
+        "z": [("tile", b) for b in bits_of(n_tile)[1:2]],
+        "w": [("tile", b) for b in bits_of(n_tile)[2:]],
+    }
+    return [[place for letter in order for place in bits[letter]] for _, order in PARTS]
 
 
 def part_sizes(slots):
-    first = (3 * slots + 7) // 8
-    second = (slots - first + 1) * 5 // 9
-    return [first, second, slots - first - second]
+    total = sum(share for share, _ in PARTS)
+    ends, done = [0], 0
+    for share, _ in PARTS:
+        done += share
+        ends.append((done * slots + total // 2) // total)
+    return [b - a for a, b in zip(ends, ends[1:])]
 
 
 def swap(values, axis, bit):
@@ -435,23 +501,160 @@
     return lax.ppermute(values, axis, [(i, i ^ (1 << bit)) for i in range(count)])
 
 
-def add_low(a, b):
-    return (a.astype(jnp.float32) + b.astype(jnp.float32)).astype(jnp.bfloat16)
-
-
-def sum_parts(kept, sent, orders):
-    received = [swap(s, "img", 0) for s in sent]
-    results = [None] * len(kept)
-    pairs = [(k, r) for k, r in zip(kept, received)]
-    for stage in range(len(orders[0])):
-        for i, order in enumerate(orders):
-            mine, theirs = pairs[i]
-            half = mine.shape[0] // 2
-            away = add_low(mine[half:], theirs[half:])
-            stay = add_low(mine[:half], theirs[:half])
-            pairs[i] = (stay, swap(away, *order[stage]))
-    for i, (mine, theirs) in enumerate(pairs):
-        results[i] = mine.astype(jnp.float32) + theirs.astype(jnp.float32)
+def sum_parts(kept, sent, orders, events):
+    terms = [[k, swap(s, "img", 0)] for k, s in zip(kept, sent)]
+    sums = [(stage, i) for stage in range(len(orders[0])) for i in range(len(orders))]
+    last = kept[0]
+    for at, (stage, i) in enumerate(sums):
+        if at in events:
+            last = events[at](last)
+        half = terms[i][-1].shape[0] // 2
+        last = sum_blocks(terms[i], half, last)
+        terms[i].append(swap(last, *orders[i][stage]))
+    results = []
+    for part in terms:
+        size = part[-1].shape[0]
+        results.append(sum(term[:size].astype(jnp.float32) for term in part))
+    return results
+
+
+def sum_everywhere(wide, narrow, after, n_img, n_tile):
+    x = [("tile", 1)]
+    y = [("img", 1 << b) for b in bits_of(n_img)[1:]]
+    z = [("tile", 1 << b) for b in bits_of(n_tile)[1:]]
+    pair = [("img", 1)]
+    orders = [pair + x + y + z, pair + y + z + x, pair + z + x + y]
+    stages = len(orders[0])
+    streams = len(orders)
+    lanes = 128
+    placed, rows = [], 0
+    for i, array in enumerate(wide):
+        for half in range(2):
+            placed.append((i, half, rows, array.shape[0], lanes))
+            rows += array.shape[0]
+    for i, array in enumerate(narrow):
+        placed.append((len(wide) + i, 0, rows, array.shape[0], array.shape[1]))
+        rows += array.shape[0]
+    unit = 8 * n_img * n_tile
+    size = -(-rows // (streams * unit)) * unit
+    operands = list(wide) + list(narrow)
+    number = len(operands)
+
+    def body(*refs):
+        inputs = refs[:number]
+        out_ref, total, landing, send, recv, send_back, recv_back = refs[number + 1 :]
+        place = {"img": lax.axis_index("img"), "tile": lax.axis_index("tile")}
+
+        def partner(axis, step):
+            here = place[axis]
+            bit = (here // step) % 2
+            there = dict(place)
+            there[axis] = here + step - 2 * step * bit
+            return bit, (there["img"], there["tile"])
+
+        barrier = pltpu.get_barrier_semaphore()
+        for axis, step in orders[0]:
+            _, there = partner(axis, step)
+            pl.semaphore_signal(
+                barrier, inc=1, device_id=there, device_id_type=pl.DeviceIdType.MESH
+            )
+        pl.semaphore_wait(barrier, stages)
+
+        for i, half, first, count, columns in placed:
+            if columns < lanes:
+                total[first : first + count] = jnp.zeros((count, lanes), jnp.float32)
+            total[first : first + count, :columns] = inputs[i][
+                :, half * lanes : half * lanes + columns
+            ]
+        if rows < streams * size:
+            total[rows:] = jnp.zeros((streams * size - rows, lanes), jnp.float32)
+
+        start = [s * size for s in range(streams)]
+        copies = {}
+
+        def rows_at(first, count):
+            return pl.ds(pl.multiple_of(first, 8), count)
+
+        def send_half(s, k):
+            half = size >> (k + 1)
+            bit, there = partner(*orders[s][k])
+            copy = pltpu.make_async_remote_copy(
+                src_ref=total.at[rows_at(start[s] + (1 - bit) * half, half)],
+                dst_ref=landing.at[pl.ds(s * size + size - 2 * half, half)],
+                send_sem=send.at[s, k],
+                recv_sem=recv.at[s, k],
+                device_id=there,
+                device_id_type=pl.DeviceIdType.MESH,
+            )
+            copy.start()
+            copies[s, k] = copy
+
+        for s in range(streams):
+            send_half(s, 0)
+        for k in range(stages):
+            for s in range(streams):
+                half = size >> (k + 1)
+                bit, _ = partner(*orders[s][k])
+                copies[s, k].wait()
+                keep = rows_at(start[s] + bit * half, half)
+                target = out_ref if k == stages - 1 else total
+                target[keep] = total[keep] + landing[pl.ds(s * size + size - 2 * half, half)]
+                start[s] = start[s] + bit * half
+                if k + 1 < stages:
+                    send_half(s, k + 1)
+
+        def send_back_half(s, k):
+            half = size >> (k + 1)
+            _, there = partner(*orders[s][k])
+            at = rows_at(start[s], half)
+            copy = pltpu.make_async_remote_copy(
+                src_ref=out_ref.at[at],
+                dst_ref=out_ref.at[at],
+                send_sem=send_back.at[s, k],
+                recv_sem=recv_back.at[s, k],
+                device_id=there,
+                device_id_type=pl.DeviceIdType.MESH,
+            )
+            copy.start()
+            copies[s, k] = copy
+
+        for s in range(streams):
+            send_back_half(s, stages - 1)
+        for k in reversed(range(stages)):
+            for s in range(streams):
+                half = size >> (k + 1)
+                bit, _ = partner(*orders[s][k])
+                copies[s, k].wait()
+                start[s] = start[s] - bit * half
+                if k > 0:
+                    send_back_half(s, k - 1)
+
+    whole = pl.BlockSpec(memory_space=pltpu.VMEM)
+    result = pl.pallas_call(
+        body,
+        in_specs=[whole] * number + [pl.BlockSpec(memory_space=pl.ANY)],
+        out_specs=whole,
+        out_shape=jax.ShapeDtypeStruct((streams * size, lanes), jnp.float32),
+        scratch_shapes=[
+            pltpu.VMEM((streams * size, lanes), jnp.float32),
+            pltpu.VMEM((streams * size, lanes), jnp.float32),
+        ]
+        + [pltpu.SemaphoreType.DMA((streams, stages))] * 4,
+        compiler_params=pltpu.CompilerParams(
+            collective_id=0, has_side_effects=True, vmem_limit_bytes=VMEM_LIMIT
+        ),
+        name="sum_everywhere",
+    )(*operands, after)
+    results, at = [], 0
+    for array in wide:
+        count = array.shape[0]
+        results.append(
+            jnp.concatenate([result[at : at + count], result[at + count : at + 2 * count]], axis=1)
+        )
+        at += 2 * count
+    for array in narrow:
+        results.append(result[at : at + array.shape[0], : array.shape[1]])
+        at += array.shape[0]
     return results
 
 
@@ -626,41 +829,69 @@
     parts = weight_grads(
         order_list, place_list, offsets, feats_t, acts_t, grads_first, grads_second, sizes
     )
-    block_parts = sum_parts(parts[0::2], parts[1::2], orders)
-
-    grad_flat = map_grads(
-        owner_slot, gathered, grads_first, sample_rows, sample_cols, fracs_row, fracs_col,
-        section_blocks, lines, breadth, channels,
-    )
-    grad_padded_map = grad_flat.reshape(images, padded_rows, breadth, channels)
-    outer_rims = jnp.concatenate(
-        [grad_padded_map[:, :rim], grad_padded_map[:, rim + height :]], axis=1
-    )
-    returned = padded_2(outer_rims, (("tile", 1),), rim)
-    grad_own = grad_padded_map[:, rim : rim + height]
-    grad_own = (
-        grad_own.at[:, :rim]
-        .add(returned[:, :rim])
-        .at[:, height - rim :]
-        .add(returned[:, 3 * rim :])
-    )
-    grad_map = grad_own.astype(jnp.bfloat16)
-    grad_conv_bias = jnp.sum(grad_map.astype(jnp.float32), axis=(0, 1, 2))
-    grad_map_padded = jnp.pad(padded_2(grad_map, (("tile", 1),), 1), column_pad)
-    grad_taps, grad_lateral_full = convolve_back(
-        grad_map_padded, lateral_padded, grad_map, kernel_taps, height, breadth
-    )
-    grad_lateral = grad_lateral_full.astype(jnp.bfloat16)
-    grad_lateral_w = jnp.einsum(
-        "ihwc,ihwd->cd", features, grad_lateral, preferred_element_type=jnp.float32
-    )
-    grad_lateral_bias = jnp.sum(grad_lateral.astype(jnp.float32), axis=(0, 1, 2))
-    grad_conv = jnp.concatenate([grad_lateral_w, grad_taps], axis=0)
-    grad_head = jnp.stack(head_grads)
-    grad_bias = jnp.concatenate([grad_lateral_bias, grad_conv_bias] + section_bias_grads)
-    conv_sum, head_sum, bias_sum, loss_total, valid_sum = lax.psum(
-        (grad_conv, grad_head, grad_bias, loss_part, jnp.sum(valid_float)), AXES
-    )
+
+    found = {"map": jnp.zeros((lines * breadth, channels), jnp.float32)}
+
+    def turns_of(start, stop):
+        def work(after):
+            found["map"] = map_grads(
+                found["map"], (start, stop), owner_slot, gathered, grads_first, sample_rows,
+                sample_cols, fracs_row, fracs_col, section_blocks, lines, breadth, after,
+            )
+            return found["map"]
+
+        return work
+
+    def rest(after):
+        grad_flat = found["map"]
+        grad_padded_map = grad_flat.reshape(images, padded_rows, breadth, channels)
+        outer_rims = jnp.concatenate(
+            [grad_padded_map[:, :rim], grad_padded_map[:, rim + height :]], axis=1
+        )
+        returned = padded_2(outer_rims, (("tile", 1),), rim)
+        grad_own = grad_padded_map[:, rim : rim + height]
+        grad_own = (
+            grad_own.at[:, :rim]
+            .add(returned[:, :rim])
+            .at[:, height - rim :]
+            .add(returned[:, 3 * rim :])
+        )
+        grad_map = grad_own.astype(jnp.bfloat16)
+        grad_conv_bias = jnp.sum(grad_map.astype(jnp.float32), axis=(0, 1, 2))
+        grad_map_padded = jnp.pad(padded_2(grad_map, (("tile", 1),), 1), column_pad)
+        grad_taps, grad_lateral_full = convolve_back(
+            grad_map_padded, lateral_padded, grad_map, kernel_taps, height, breadth
+        )
+        grad_lateral = grad_lateral_full.astype(jnp.bfloat16)
+        grad_lateral_w = jnp.einsum(
+            "ihwc,ihwd->cd", features, grad_lateral, preferred_element_type=jnp.float32
+        )
+        grad_lateral_bias = jnp.sum(grad_lateral.astype(jnp.float32), axis=(0, 1, 2))
+        misc = jnp.concatenate(
+            [grad_lateral_bias, grad_conv_bias]
+            + section_bias_grads
+            + [loss_part[None], jnp.sum(valid_float)[None]]
+        )
+        filled = -(-misc.size // 1024) * 1024
+        misc = jnp.pad(misc, (0, filled - misc.size)).reshape(-1, 128)
+        heads = jnp.stack(head_grads).reshape(-1, out_width)
+        found["sums"] = sum_everywhere(
+            [grad_lateral_w, grad_taps], [heads, misc], after, n_img, n_tile
+        )
+        return found["sums"][-1]
+
+    events, start = {}, 0
+    for at, count in TURNS_AT.items():
+        events[at] = turns_of(start, start + count)
+        start += count
+    events[REST_AT] = rest
+    block_parts = sum_parts(parts[0::2], parts[1::2], orders, events)
+
+    conv_sum = jnp.concatenate(found["sums"][:2], axis=0)
+    head_sum = found["sums"][2].reshape(section_count, hidden, out_width)
+    misc_sum = found["sums"][3].reshape(-1)
+    biases = bias_vector.shape[0]
+    bias_sum, loss_total, valid_sum = misc_sum[:biases], misc_sum[biases], misc_sum[biases + 1]
     scale = 1.0 / valid_sum
     mine = lax.dynamic_slice_in_dim(slot_block, (at_img * n_tile + at_tile) * slots, slots)
     block_grad = jnp.where(

time: 1600 us -> 1290 us (0.81)
  waiting for transfers between devices: 690 us -> 408 us
  blocking collectives: 158 us -> 0 us
  Pallas kernels: 431 us -> 572 us
  other arithmetic: 147 us -> 67.9 us
  starting transfers between devices: 40.4 us -> 108 us
  matrix products: 71.5 us -> 46 us
  local copies, waits for them, and re-layouts: 36.8 us -> 58.5 us
    ppermute x4, waiting for transfers between devices: 183 us -> 8.85 us  [padded_2(): lax.ppermute(head, axis, [((i + 1) % count, i) for i in range(ends)])]
    pallas_call x0 -> x21, Pallas kernels: none -> 166 us  [the longest x20 86.7 us: sum_blocks(): pl.pallas_call(body, grid=(half // batch,), in_specs=[pl.BlockSpec((batch...]
    psum x1 -> x0, blocking collectives: 158 us -> none  [on_device(): lax.psum((grad_conv, grad_head, grad_bias, loss_part, jnp.sum(valid_float...]
    psum x1 -> x0, waiting for transfers between devices: 108 us -> none  [on_device(): lax.psum((grad_conv, grad_head, grad_bias, loss_part, jnp.sum(valid_float...]
    convert_element_type x12 -> x0, other arithmetic: 89.6 us -> none  [add_low(): return (a.astype(jnp.float32) + b.astype(jnp.float32)).astype(jnp.bfloat16)]
    ppermute x15 -> x25, starting transfers between devices: 15.9 us -> 59.7 us  [swap(): return lax.ppermute(values, axis, [(i, i ^ 1 << bit) for i in range(count)])]
    pallas_call x1 -> x5, Pallas kernels: 198 us -> 172 us  [map_grads(): pl.pallas_call(body, grid_spec=pltpu.PrefetchScalarGridSpec(num_scalar_pr...]
    ppermute x4, starting transfers between devices: 19.1 us -> 43 us  [padded_2(): lax.ppermute(tail, axis, [(i, (i + 1) % count) for i in range(ends)])]
  transfers between devices with their start and end apart: 25 -> 34, of which waited for: 9 -> 11; matrix products, arithmetic and copies ran while one was open for 12% -> 8% of each run, Pallas kernels for 19% -> 35%
where the time goes in v2:
time: 1290 us; the launch traced here: 1280 us
  Pallas kernels  572 us (44%)
  waiting for transfers between devices  408 us (32%)
  starting transfers between devices  108 us (8%)
  other arithmetic  67.9 us (5%)
  local copies, waits for them, and re-layouts  58.5 us (5%)
  matrix products  46 us (4%)
  between operations  19.9 us (2%)
    all_gather x1, waiting for transfers between devices, on_device(): lax.all_gather(block_master.astype(jnp.bfloat16), AXES, axis=0, tiled=True)  281 us
    pallas_call x5, Pallas kernels, map_grads(): pl.pallas_call(body, grid_spec=pltpu.PrefetchScalarGridSpec(num_scalar_pr...  172 us
    ppermute x25, waiting for transfers between devices, swap(): return lax.ppermute(values, axis, [(i, i ^ 1 << bit) for i in range(count)])  110 us
    pallas_call x1, Pallas kernels, pool_regions(): pl.pallas_call(body, grid=(section_count, bins // group), in_specs=[pl.Bl...  109 us
    pallas_call x20, Pallas kernels, sum_blocks(): pl.pallas_call(body, grid=(half // batch,), in_specs=[pl.BlockSpec((batch...  86.7 us
    pallas_call x1, Pallas kernels, sum_everywhere(): pl.pallas_call(body, in_specs=[whole] * number + [pl.BlockSpec(memory_spa...  79.4 us
    pallas_call x1, Pallas kernels, weight_grads(): pl.pallas_call(body, grid_spec=pltpu.PrefetchScalarGridSpec(num_scalar_pr...  66.5 us
    ppermute x25, starting transfers between devices, swap(): return lax.ppermute(values, axis, [(i, i ^ 1 << bit) for i in range(count)])  59.7 us
  transfers between devices with their start and end apart: 34, of which 11 were waited for; matrix products, arithmetic and copies ran while one was open for 8% of the time, Pallas kernels for 35%

profile of v2, /device:TPU:0, one launch (start us, length us, event | category | flops | bytes accessed | tf_op | source)
XLA Modules:
  0.0 1279.9 jit_solution(283644783307139587)
XLA Ops:
  7.2 4.5 convert_element_type.221
  16.0 4.8 collective-permute-start
  22.2 5.2 scatter_custom_fusion.table_ref
  31.7 3.0 fusion.142
  36.1 5.2 sort.31
  50.4 4.6 collective-permute-start.2
  57.1 5.0 collective-permute-done.2
  62.1 4.1 collective-permute-done.3
  68.9 108.7 %pool_regions.1.x_ref = bf16[3,49,256,256]{3,2,1,0:T(8,128)(2,1)} custom-call(bf16[256,3840]{1,0:T(8,128)(2,1)} %bitcast.300, s32[3,49,256]{2,1,0:T(8,128)} %get-tuple-element.119.row_ref, s32[3,49,256]{2,1,0:T(8,128)} %get-tuple-element.118.col_ref, f32[3,49,256]{2,1,0:T(8,128)} %get-tuple-element.174.fr_ref, f32[3,49,256]{2,1,0:T(8,128)} %get-tuple-element.173.fc_ref), custom_call_target="tpu_custom_call" | custom-call | flops 73987522560 | bytes 19267584 | tf_op jit(solution)/shard_map/pool_regions/pallas_call | solution.py:136
  177.6 280.7 %all-gather.2.cloned.1.call-done.blocks_ref = bf16[1280,32,1024]{2,1,0:T(8,128)(2,1)} async-done(((bf16[40,32,1024]{2,1,0:T(8,128)(2,1)}), bf16[1280,32,1024]{2,1,0:T(8,128)(2,1)}) %all-gather.2.cloned.1.call-update) | async-done | bytes 83886096 | tf_op jit(solution)/shard_map/all_gather | solution.py:698
  458.3 58.1 %first_layer.1 = f32[3,256,1024]{2,1,0:T(8,128)} custom-call(s32[1272]{0:T(1024)} %copy-done.45, bf16[1280,32,1024]{2,1,0:T(8,128)(2,1)} %all-gather.2.cloned.1.call-done.blocks_ref, bf16[3,49,256,256]{3,2,1,0:T(8,128)(2,1)} %pool_regions.1.x_ref), custom_call_target="tpu_custom_call" | custom-call | flops 19730006016 | bytes 96337920 | tf_op jit(solution)/shard_map/first_layer/pallas_call | solution.py:207
  516.3 3.6 gather_fusion.2
  519.9 3.7 multiply_convert_fusion.3
  525.4 3.5 gather_fusion.1
  528.9 3.8 multiply_convert_fusion.5
  536.9 3.5 gather_fusion
  540.4 3.8 multiply_convert_fusion.7
  563.8 66.5 %weight_grads.1 = (bf16[112,32,1024]{2,1,0:T(8,128)(2,1)}, bf16[112,32,1024]{2,1,0:T(8,128)(2,1)}, bf16[112,32,1024]{2,1,0:T(8,128)(2,1)}, bf16[112,32,1024]{2,1...) custom-call(s32[1272]{0:T(1024)} %get-tuple-element.52.order_ref, ...), custom_call_target="tpu_custom_call" | custom-call | flops 21340618752 | bytes 104202240 | tf_op jit(solution)/shard_map/weight_grads/pallas_call | solution.py:306
  633.9 39.8 %map_grads.5.refs_2_.old_ref = f32[3840,256]{1,0:T(8,128)} custom-call(s32[1272]{0:T(1024)} %copy-done.45, bf16[1280,32,1024]{2,1,0:T(8,128)(2,1)} %all-gather.2.cloned.1.call-done.blocks_ref, bf16[3,256,1024]{2,1,0:T(8,128)(2,1)} %pad_maximum_fusion.1.gf_ref.g_ref, s32[3,49,256]{2,1,0:T(8,128)} %get-tuple-element.119.row_ref, ...), custom_call_target="tpu_custom_call" | custom-call | flops 22313697280 | bytes 18350080 | tf_op jit(solution)/shard_map/map_grads/pallas_call | solution.py:407
  673.7 5.6 sum_blocks.20.refs_2_
  679.2 3.7 collective-permute-done.7.refs_1_
  682.9 5.6 sum_blocks.21.refs_2_
  688.5 8.0 sum_blocks.22.refs_2_
  698.7 8.2 sum_blocks.23.refs_2_
  709.5 4.1 fusion.215
  713.6 5.4 sum_blocks.24.after_ref
  721.0 46.3 %map_grads.6.refs_3_.old_ref = f32[3840,256]{1,0:T(8,128)} custom-call(s32[1272]{0:T(1024)} %copy-done.45, bf16[1280,32,1024]{2,1,0:T(8,128)(2,1)} %all-gather.2.cloned.1.call-done.blocks_ref, bf16[3,256,1024]{2,1,0:T(8,128)(2,1)} %pad_maximum_fusion.1.gf_ref.g_ref, s32[3,49,256]{2,1,0:T(8,128)} %get-tuple-element.119.row_ref, ...), custom_call_target="tpu_custom_call" | custom-call | flops 26776436736 | bytes 22020096 | tf_op jit(solution)/shard_map/map_grads/pallas_call | solution.py:407
  767.4 13.1 %collective-permute-done.10.refs_2_ = bf16[56,32,1024]{2,1,0:T(8,128)(2,1)} collective-permute-done((bf16[56,32,1024]{2,1,0:T(8,128)(2,1)}, bf16[56,32,1024]{2,1,0:T(8,128)(2,1)}, u32[]{:S(2)}, u32[]{:S(2)}) %collective-permute-start.10) | collective-permute-done | bytes 3670048 | tf_op jit(solution)/shard_map/ppermute | solution.py:501
  780.5 3.8 sum_blocks.25.refs_3_
  785.9 4.0 sum_blocks.26.after_ref
  790.4 26.5 %map_grads.7.refs_3_.old_ref = f32[3840,256]{1,0:T(8,128)} custom-call(s32[1272]{0:T(1024)} %copy-done.45, bf16[1280,32,1024]{2,1,0:T(8,128)(2,1)} %all-gather.2.cloned.1.call-done.blocks_ref, bf16[3,256,1024]{2,1,0:T(8,128)(2,1)} %pad_maximum_fusion.1.gf_ref.g_ref, s32[3,49,256]{2,1,0:T(8,128)} %get-tuple-element.119.row_ref, ...), custom_call_target="tpu_custom_call" | custom-call | flops 13388218368 | bytes 11010048 | tf_op jit(solution)/shard_map/map_grads/pallas_call | solution.py:407
  816.9 5.5 sum_blocks.27.after_ref
  822.4 19.9 %map_grads.8.refs_3_.old_ref = f32[3840,256]{1,0:T(8,128)} custom-call(s32[1272]{0:T(1024)} %copy-done.45, bf16[1280,32,1024]{2,1,0:T(8,128)(2,1)} %all-gather.2.cloned.1.call-done.blocks_ref, bf16[3,256,1024]{2,1,0:T(8,128)(2,1)} %pad_maximum_fusion.1.gf_ref.g_ref, s32[3,49,256]{2,1,0:T(8,128)} %get-tuple-element.119.row_ref, ...), custom_call_target="tpu_custom_call" | custom-call | flops 8925478912 | bytes 7340032 | tf_op jit(solution)/shard_map/map_grads/pallas_call | solution.py:407
  842.3 49.6 %collective-permute-done.13.refs_2_ = bf16[80,32,1024]{2,1,0:T(8,128)(2,1)} collective-permute-done((bf16[80,32,1024]{2,1,0:T(8,128)(2,1)}, bf16[80,32,1024]{2,1,0:T(8,128)(2,1)}, u32[]{:S(2)}, u32[]{:S(2)}) %collective-permute-start.13) | collective-permute-done | bytes 5242912 | tf_op jit(solution)/shard_map/ppermute | solution.py:501
  891.9 5.5 sum_blocks.28.refs_3_
  899.0 3.5 sum_blocks.29.after_ref
  902.5 40.0 %map_grads.9.refs_4_ = f32[3840,256]{1,0:T(8,128)} custom-call(s32[1272]{0:T(1024)} %copy-done.45, bf16[1280,32,1024]{2,1,0:T(8,128)(2,1)} %all-gather.2.cloned.1.call-done.blocks_ref, bf16[3,256,1024]{2,1,0:T(8,128)(2,1)} %pad_maximum_fusion.1.gf_ref.g_ref, s32[3,49,256]{2,1,0:T(8,128)} %get-tuple-element.119.row_ref, ...), custom_call_target="tpu_custom_call" | custom-call | flops 22313697280 | bytes 18350080 | tf_op jit(solution)/shard_map/map_grads/pallas_call | solution.py:407
  944.9 3.5 collective-permute-start.14
  953.3 2.9 copy.148
  958.5 3.9 collective-permute-start.20
  964.4 3.4 sum_blocks.30.refs_4_
  969.8 3.4 sum_blocks.31.refs_4_
  973.2 3.2 collective-permute-done.14
  982.1 30.1 %collective-permute-start.16 = (bf16[2,1,160,256]{3,2,1,0:T(8,128)(2,1)S(1)}, bf16[2,1,160,256]{3,2,1,0:T(8,128)(2,1)S(1)}, u32[]{:S(2)}, u32[]{:S(2)}) collective-permute-start(bf16[2,1,160,256]{3,2,1,0:T(8,128)(2,1)S(1)} %get-tuple-element.111), channel_id=1, source_target_pairs={{0,1},{1,2},{2,3},{3,4},{4,5},{5,6},{6,7},{8,9},{9,10},{10,11},{11... | collective-permute-start | bytes 491528 | tf_op jit(solution)/shard_map/ppermute | solution.py:31
  1022.6 4.8 collective-permute-done.17
  1027.4 36.1 %collective-permute-start.23 = (bf16[14,32,1024]{2,1,0:T(8,128)(2,1)S(1)}, bf16[14,32,1024]{2,1,0:T(8,128)(2,1)}, u32[]{:S(2)}, u32[]{:S(2)}) collective-permute-start(bf16[14,32,1024]{2,1,0:T(8,128)(2,1)S(1)} %copy-done.15), channel_id=1, source_target_pairs={{0,1},{1,0},{2,3},{3,2},{4,5},{5,4},{6,7},{7,6},{8,9},{9,8},{10,11... | collective-permute-start | bytes 2752520 | tf_op jit(solution)/shard_map/ppermute | solution.py:501
  1072.1 2.6 fusion.65.refs_0_
  1074.7 3.8 sum_blocks.32.refs_4_
  1079.2 3.7 sum_blocks.33.refs_4_
  1084.8 3.1 sum_blocks.34.refs_4_
  1088.0 79.4 %sum_everywhere.1 = f32[8448,128]{1,0:T(8,128)} custom-call(f32[256,256]{1,0:T(8,128)} %fusion.65.refs_0_, f32[2304,256]{1,0:T(8,128)} %copy-done.17, f32[3072,85]{1,0:T(8,128)} %bitcast.292, f32[56,128]{1,0:T(8,128)} %pad_bitcast_fusion.refs_3_, bf16[12,32,1024]{2,1,0:T(8,128)(2,1)} %sum_blocks.34.refs_4_), custom_call_target="tpu_custom_call" | custom-call | tf_op jit(solution)/shard_map/sum_everywhere/pallas_call | solution.py:633
  1168.8 2.8 sum_blocks.35.refs_5_
  1175.0 2.8 sum_blocks.36.refs_5_
  1179.4 6.1 multiply_subtract_fusion.1
  1187.1 4.6 multiply_subtract_fusion.2
  1191.7 3.1 sum_blocks.37.refs_5_
  1194.8 2.6 collective-permute-start.28
  1201.0 3.1 sum_blocks.38.refs_5_
  1204.4 24.7 %collective-permute-done.26 = bf16[7,32,1024]{2,1,0:T(8,128)(2,1)} collective-permute-done((bf16[7,32,1024]{2,1,0:T(8,128)(2,1)}, bf16[7,32,1024]{2,1,0:T(8,128)(2,1)}, u32[]{:S(2)}, u32[]{:S(2)}) %collective-permute-start.26) | collective-permute-done | bytes 458784 | tf_op jit(solution)/shard_map/ppermute | solution.py:501
  1235.4 7.7 collective-permute-done.28
  1243.1 2.8 add_dynamic-update-slice_fusion.1
  1245.9 11.1 collective-permute-done.30
  1257.0 2.6 add_dynamic-update-slice_fusion
  1261.6 10.1 multiply_subtract_fusion
  (323 shorter events, 121.7 us)
Async XLA Ops:
  7.2 7.6 copy-start
  7.2 451.1 %all-gather.2.cloned.1.call-start = ((), (), s32[]{:S(2)}) async-start(), calls=%async_computation | async-start | bytes 86507520 | tf_op jit(solution)/shard_map/all_gather | solution.py:698
  13.7 8.5 copy-start.65
  14.7 12.7 copy-start.77
  14.7 13.4 %copy-start.73 = (s32[3,256]{1,0:T(4,128)S(1)}, s32[3,256]{1,0:T(4,128)}, u32[]{:S(2)}) copy-start(s32[3,256]{1,0:T(4,128)} %param.44) | copy-start | bytes 9220
  14.7 13.4 %copy-start.64 = (s32[256]{0:T(256)S(1)}, s32[256]{0:T(256)}, u32[]{:S(2)}) copy-start(s32[256]{0:T(256)} %param.45) | copy-start | bytes 3076
  14.7 14.7 %copy-start.52 = (s32[3,49,256]{2,1,0:T(8,128)S(1)}, s32[3,49,256]{2,1,0:T(8,128)}, u32[]{:S(2)}) copy-start(s32[3,49,256]{2,1,0:T(8,128)} %param.42) | copy-start | bytes 451588
  15.3 28.9 %copy-start.3 = (bf16[2,8,160,256]{3,2,1,0:T(8,128)(2,1)}, bf16[2,8,160,256]{3,2,1,0:T(8,128)(2,1)S(1)}, u32[]{:S(2)}) copy-start(bf16[2,8,160,256]{3,2,1,0:T(8,128)(2,1)S(1)} %add_convert_fusion.2) | copy-start | bytes 3932164
  16.0 26.1 %collective-permute-start = (bf16[2,1,160,256]{3,2,1,0:T(8,128)(2,1)}, bf16[2,1,160,256]{3,2,1,0:T(8,128)(2,1)S(1)}, u32[]{:S(2)}, u32[]{:S(2)}) collective-permute-start(bf16[2,1,160,256]{3,2,1,0:T(8,128)(2,1)} %get-tuple-element.114), channel_id=1, source_target_pairs={{0,1},{1,2},{2,3},{3,4},{4,5},{5,6},{6,7},{8,9},{9,10},{10,11},{11... | collective-permute-start | bytes 491528 | tf_op jit(solution)/shard_map/ppermute | solution.py:31
  20.9 22.7 %collective-permute-start.1 = (bf16[2,1,160,256]{3,2,1,0:T(8,128)(2,1)S(1)}, bf16[2,1,160,256]{3,2,1,0:T(8,128)(2,1)S(1)}, u32[]{:S(2)}, u32[]{:S(2)}) collective-permute-start(bf16[2,1,160,256]{3,2,1,0:T(8,128)(2,1)S(1)} %get-tuple-element.115), channel_id=1, source_target_pairs={{1,0},{2,1},{3,2},{4,3},{5,4},{6,5},{7,6},{9,8},{10,9},{11,10},{12... | collective-permute-start | bytes 491528 | tf_op jit(solution)/shard_map/ppermute | solution.py:33
  27.5 7.2 copy-start.45
  50.4 11.7 collective-permute-start.2
  55.0 11.2 collective-permute-start.3
  528.9 6.2 copy-start.7
  547.9 7.0 copy-start.61
  547.9 10.1 copy-start.57
  550.4 7.7 copy-start.46
  630.4 58.2 %collective-permute-start.6 = (bf16[160,32,1024]{2,1,0:T(8,128)(2,1)}, bf16[160,32,1024]{2,1,0:T(8,128)(2,1)}, u32[]{:S(2)}, u32[]{:S(2)}) collective-permute-start(bf16[160,32,1024]{2,1,0:T(8,128)(2,1)} %get-tuple-element.60), channel_id=1, source_target_pairs={{0,8},{8,0},{16,24},{24,16},{1,9},{9,1},{17,25},{25,17},{2,10},{10... | collective-permute-start | bytes 31457288 | tf_op jit(solution)/shard_map/ppermute | solution.py:501
  630.7 68.0 %collective-permute-start.5 = (bf16[160,32,1024]{2,1,0:T(8,128)(2,1)}, bf16[160,32,1024]{2,1,0:T(8,128)(2,1)}, u32[]{:S(2)}, u32[]{:S(2)}) collective-permute-start(bf16[160,32,1024]{2,1,0:T(8,128)(2,1)} %get-tuple-element.58), channel_id=1, source_target_pairs={{0,8},{8,0},{16,24},{24,16},{1,9},{9,1},{17,25},{25,17},{2,10},{10... | collective-permute-start | bytes 31457288 | tf_op jit(solution)/shard_map/ppermute | solution.py:501
  630.9 42.7 %collective-permute-start.8 = (bf16[112,32,1024]{2,1,0:T(8,128)(2,1)}, bf16[112,32,1024]{2,1,0:T(8,128)(2,1)}, u32[]{:S(2)}, u32[]{:S(2)}) collective-permute-start(bf16[112,32,1024]{2,1,0:T(8,128)(2,1)} %get-tuple-element.63), channel_id=1, source_target_pairs={{0,8},{8,0},{16,24},{24,16},{1,9},{9,1},{17,25},{25,17},{2,10},{10... | collective-permute-start | bytes 22020104 | tf_op jit(solution)/shard_map/ppermute | solution.py:501
  631.2 51.7 %collective-permute-start.7 = (bf16[112,32,1024]{2,1,0:T(8,128)(2,1)}, bf16[112,32,1024]{2,1,0:T(8,128)(2,1)}, u32[]{:S(2)}, u32[]{:S(2)}) collective-permute-start(bf16[112,32,1024]{2,1,0:T(8,128)(2,1)} %get-tuple-element.62), channel_id=1, source_target_pairs={{0,8},{8,0},{16,24},{24,16},{1,9},{9,1},{17,25},{25,17},{2,10},{10... | collective-permute-start | bytes 22020104 | tf_op jit(solution)/shard_map/ppermute | solution.py:501
  631.5 82.1 %collective-permute-start.4 = (bf16[96,32,1024]{2,1,0:T(8,128)(2,1)}, bf16[96,32,1024]{2,1,0:T(8,128)(2,1)}, u32[]{:S(2)}, u32[]{:S(2)}) collective-permute-start(bf16[96,32,1024]{2,1,0:T(8,128)(2,1)} %get-tuple-element.56), channel_id=1, source_target_pairs={{0,8},{8,0},{16,24},{24,16},{1,9},{9,1},{17,25},{25,17},{2,10},{10... | collective-permute-start | bytes 18874376 | tf_op jit(solution)/shard_map/ppermute | solution.py:501
  696.6 120.3 %collective-permute-start.11 = (bf16[80,32,1024]{2,1,0:T(8,128)(2,1)}, bf16[80,32,1024]{2,1,0:T(8,128)(2,1)}, u32[]{:S(2)}, u32[]{:S(2)}) collective-permute-start(bf16[80,32,1024]{2,1,0:T(8,128)(2,1)} %sum_blocks.22.refs_2_), channel_id=1, source_target_pairs={{0,1},{1,0},{2,3},{3,2},{4,5},{5,4},{6,7},{7,6},{8,9},{9,8},{10,11... | collective-permute-start | bytes 15728648 | tf_op jit(solution)/shard_map/ppermute | solution.py:501
  698.0 82.5 %collective-permute-start.10 = (bf16[56,32,1024]{2,1,0:T(8,128)(2,1)}, bf16[56,32,1024]{2,1,0:T(8,128)(2,1)}, u32[]{:S(2)}, u32[]{:S(2)}) collective-permute-start(bf16[56,32,1024]{2,1,0:T(8,128)(2,1)} %sum_blocks.20.refs_2_), channel_id=1, source_target_pairs={{0,2},{1,3},{2,0},{3,1},{4,6},{5,7},{6,4},{7,5},{8,10},{9,11},{10,... | collective-permute-start | bytes 11010056 | tf_op jit(solution)/shard_map/ppermute | solution.py:501
  698.0 87.9 %collective-permute-start.9 = (bf16[56,32,1024]{2,1,0:T(8,128)(2,1)}, bf16[56,32,1024]{2,1,0:T(8,128)(2,1)}, u32[]{:S(2)}, u32[]{:S(2)}) collective-permute-start(bf16[56,32,1024]{2,1,0:T(8,128)(2,1)} %sum_blocks.21.refs_2_), channel_id=1, source_target_pairs={{0,16},{8,24},{16,0},{24,8},{1,17},{9,25},{17,1},{25,9},{2,18},{10... | collective-permute-start | bytes 11010056 | tf_op jit(solution)/shard_map/ppermute | solution.py:501
  698.7 10.8 copy-start.2
  706.9 185.0 %collective-permute-start.13 = (bf16[80,32,1024]{2,1,0:T(8,128)(2,1)}, bf16[80,32,1024]{2,1,0:T(8,128)(2,1)}, u32[]{:S(2)}, u32[]{:S(2)}) collective-permute-start(bf16[80,32,1024]{2,1,0:T(8,128)(2,1)} %sum_blocks.23.refs_2_), channel_id=1, source_target_pairs={{0,16},{8,24},{16,0},{24,8},{1,17},{9,25},{17,1},{25,9},{2,18},{10... | collective-permute-start | bytes 15728648 | tf_op jit(solution)/shard_map/ppermute | solution.py:501
  719.0 178.3 %collective-permute-start.12 = (bf16[48,32,1024]{2,1,0:T(8,128)(2,1)}, bf16[48,32,1024]{2,1,0:T(8,128)(2,1)S(1)}, u32[]{:S(2)}, u32[]{:S(2)}) collective-permute-start(bf16[48,32,1024]{2,1,0:T(8,128)(2,1)} %sum_blocks.24.after_ref), channel_id=1, source_target_pairs={{0,2},{1,3},{2,0},{3,1},{4,6},{5,7},{6,4},{7,5},{8,10},{9,11},{10,... | collective-permute-start | bytes 9437192 | tf_op jit(solution)/shard_map/ppermute | solution.py:501
  784.3 180.0 %collective-permute-start.22 = (bf16[28,32,1024]{2,1,0:T(8,128)(2,1)}, bf16[28,32,1024]{2,1,0:T(8,128)(2,1)}, u32[]{:S(2)}, u32[]{:S(2)}) collective-permute-start(bf16[28,32,1024]{2,1,0:T(8,128)(2,1)} %sum_blocks.25.refs_3_), channel_id=1, source_target_pairs={{0,4},{1,5},{2,6},{3,7},{4,0},{5,1},{6,2},{7,3},{8,12},{9,13},{10,... | collective-permute-start | bytes 5505032 | tf_op jit(solution)/shard_map/ppermute | solution.py:501
  789.8 177.9 %collective-permute-start.21 = (bf16[28,32,1024]{2,1,0:T(8,128)(2,1)}, bf16[28,32,1024]{2,1,0:T(8,128)(2,1)}, u32[]{:S(2)}, u32[]{:S(2)}) collective-permute-start(bf16[28,32,1024]{2,1,0:T(8,128)(2,1)} %sum_blocks.26.after_ref), channel_id=1, source_target_pairs={{0,1},{1,0},{2,3},{3,2},{4,5},{5,4},{6,7},{7,6},{8,9},{9,8},{10,11... | collective-permute-start | bytes 5505032 | tf_op jit(solution)/shard_map/ppermute | solution.py:501
  942.5 5.9 copy-start.4
  942.5 5.9 copy-start.34
  942.5 5.9 copy-start.36
  944.9 5.2 copy-start.51
  944.9 5.2 copy-start.62
  944.9 6.8 copy-start.24
  944.9 6.8 copy-start.49
  944.9 6.8 copy-start.60
  944.9 31.5 %collective-permute-start.14 = (f32[2,2,160,256]{3,2,1,0:T(8,128)}, f32[2,2,160,256]{3,2,1,0:T(8,128)}, u32[]{:S(2)}, u32[]{:S(2)}) collective-permute-start(f32[2,2,160,256]{3,2,1,0:T(8,128)} %get-tuple-element.98), channel_id=1, source_target_pairs={{0,1},{1,2},{2,3},{3,4},{4,5},{5,6},{6,7},{8,9},{9,10},{10,11},{11... | collective-permute-start | bytes 1966088 | tf_op jit(solution)/shard_map/ppermute | solution.py:31
  950.4 27.4 %collective-permute-start.15 = (f32[2,2,160,256]{3,2,1,0:T(8,128)S(1)}, f32[2,2,160,256]{3,2,1,0:T(8,128)}, u32[]{:S(2)}, u32[]{:S(2)}) collective-permute-start(f32[2,2,160,256]{3,2,1,0:T(8,128)S(1)} %get-tuple-element.97), channel_id=1, source_target_pairs={{1,0},{2,1},{3,2},{4,3},{5,4},{6,5},{7,6},{9,8},{10,9},{11,10},{12... | collective-permute-start | bytes 1966088 | tf_op jit(solution)/shard_map/ppermute | solution.py:33
  958.5 116.3 %collective-permute-start.20 = (bf16[40,32,1024]{2,1,0:T(8,128)(2,1)}, bf16[40,32,1024]{2,1,0:T(8,128)(2,1)}, u32[]{:S(2)}, u32[]{:S(2)}) collective-permute-start(bf16[40,32,1024]{2,1,0:T(8,128)(2,1)} %sum_blocks.27.after_ref), channel_id=1, source_target_pairs={{0,2},{1,3},{2,0},{3,1},{4,6},{5,7},{6,4},{7,5},{8,10},{9,11},{10,... | collective-permute-start | bytes 7864328 | tf_op jit(solution)/shard_map/ppermute | solution.py:501
  964.3 114.8 %collective-permute-start.19 = (bf16[40,32,1024]{2,1,0:T(8,128)(2,1)}, bf16[40,32,1024]{2,1,0:T(8,128)(2,1)}, u32[]{:S(2)}, u32[]{:S(2)}) collective-permute-start(bf16[40,32,1024]{2,1,0:T(8,128)(2,1)} %sum_blocks.28.refs_3_), channel_id=1, source_target_pairs={{0,1},{1,0},{2,3},{3,2},{4,5},{5,4},{6,7},{7,6},{8,9},{9,8},{10,11... | collective-permute-start | bytes 7864328 | tf_op jit(solution)/shard_map/ppermute | solution.py:501
  967.8 117.1 %collective-permute-start.18 = (bf16[24,32,1024]{2,1,0:T(8,128)(2,1)}, bf16[24,32,1024]{2,1,0:T(8,128)(2,1)}, u32[]{:S(2)}, u32[]{:S(2)}) collective-permute-start(bf16[24,32,1024]{2,1,0:T(8,128)(2,1)} %sum_blocks.29.after_ref), channel_id=1, source_target_pairs={{0,4},{1,5},{2,6},{3,7},{4,0},{5,1},{6,2},{7,3},{8,12},{9,13},{10,... | collective-permute-start | bytes 4718600 | tf_op jit(solution)/shard_map/ppermute | solution.py:501
  980.3 31.9 %copy-start.44 = (bf16[2,8,160,256]{3,2,1,0:T(8,128)(2,1)S(1)}, bf16[2,8,160,256]{3,2,1,0:T(8,128)(2,1)}, u32[]{:S(2)}) copy-start(bf16[2,8,160,256]{3,2,1,0:T(8,128)(2,1)} %get-tuple-element.107) | copy-start | bytes 3932164
  980.8 46.6 %collective-permute-start.17 = (bf16[2,1,160,256]{3,2,1,0:T(8,128)(2,1)S(1)}, bf16[2,1,160,256]{3,2,1,0:T(8,128)(2,1)S(1)}, u32[]{:S(2)}, u32[]{:S(2)}) collective-permute-start(bf16[2,1,160,256]{3,2,1,0:T(8,128)(2,1)S(1)} %get-tuple-element.110), channel_id=1, source_target_pairs={{1,0},{2,1},{3,2},{4,3},{5,4},{6,5},{7,6},{9,8},{10,9},{11,10},{12... | collective-permute-start | bytes 491528 | tf_op jit(solution)/shard_map/ppermute | solution.py:33
  982.1 81.4 %collective-permute-start.16 = (bf16[2,1,160,256]{3,2,1,0:T(8,128)(2,1)S(1)}, bf16[2,1,160,256]{3,2,1,0:T(8,128)(2,1)S(1)}, u32[]{:S(2)}, u32[]{:S(2)}) collective-permute-start(bf16[2,1,160,256]{3,2,1,0:T(8,128)(2,1)S(1)} %get-tuple-element.111), channel_id=1, source_target_pairs={{0,1},{1,2},{2,3},{3,4},{4,5},{5,6},{6,7},{8,9},{9,10},{10,11},{11... | collective-permute-start | bytes 491528 | tf_op jit(solution)/shard_map/ppermute | solution.py:31
  1022.0 5.4 copy-start.15
  1022.0 41.5 %copy-start.16 = (bf16[14,32,1024]{2,1,0:T(8,128)(2,1)S(1)}, bf16[14,32,1024]{2,1,0:T(8,128)(2,1)}, u32[]{:S(2)}) copy-start(bf16[14,32,1024]{2,1,0:T(8,128)(2,1)} %sum_blocks.31.refs_4_) | copy-start | bytes 2752516
  1022.6 40.9 %copy-start.17 = (f32[2304,256]{1,0:T(8,128)}, f32[2304,256]{1,0:T(8,128)S(1)}, u32[]{:S(2)}) copy-start(f32[2304,256]{1,0:T(8,128)S(1)} %fusion.121.refs_1_) | copy-start | bytes 7077892
  1027.4 141.4 %collective-permute-start.23 = (bf16[14,32,1024]{2,1,0:T(8,128)(2,1)S(1)}, bf16[14,32,1024]{2,1,0:T(8,128)(2,1)}, u32[]{:S(2)}, u32[]{:S(2)}) collective-permute-start(bf16[14,32,1024]{2,1,0:T(8,128)(2,1)S(1)} %copy-done.15), channel_id=1, source_target_pairs={{0,1},{1,0},{2,3},{3,2},{4,5},{5,4},{6,7},{7,6},{8,9},{9,8},{10,11... | collective-permute-start | bytes 2752520 | tf_op jit(solution)/shard_map/ppermute | solution.py:501
  1063.5 111.4 %collective-permute-start.25 = (bf16[14,32,1024]{2,1,0:T(8,128)(2,1)S(1)}, bf16[14,32,1024]{2,1,0:T(8,128)(2,1)}, u32[]{:S(2)}, u32[]{:S(2)}) collective-permute-start(bf16[14,32,1024]{2,1,0:T(8,128)(2,1)S(1)} %copy-done.16), channel_id=1, source_target_pairs={{0,2},{1,3},{2,0},{3,1},{4,6},{5,7},{6,4},{7,5},{8,10},{9,11},{10,... | collective-permute-start | bytes 2752520 | tf_op jit(solution)/shard_map/ppermute | solution.py:501
  1078.6 113.1 %collective-permute-start.27 = (bf16[20,32,1024]{2,1,0:T(8,128)(2,1)}, bf16[20,32,1024]{2,1,0:T(8,128)(2,1)}, u32[]{:S(2)}, u32[]{:S(2)}) collective-permute-start(bf16[20,32,1024]{2,1,0:T(8,128)(2,1)} %sum_blocks.32.refs_4_), channel_id=1, source_target_pairs={{0,16},{8,24},{16,0},{24,8},{1,17},{9,25},{17,1},{25,9},{2,18},{10... | collective-permute-start | bytes 3932168 | tf_op jit(solution)/shard_map/ppermute | solution.py:501
  1082.8 118.1 %collective-permute-start.29 = (bf16[20,32,1024]{2,1,0:T(8,128)(2,1)}, bf16[20,32,1024]{2,1,0:T(8,128)(2,1)}, u32[]{:S(2)}, u32[]{:S(2)}) collective-permute-start(bf16[20,32,1024]{2,1,0:T(8,128)(2,1)} %sum_blocks.33.refs_4_), channel_id=1, source_target_pairs={{0,2},{1,3},{2,0},{3,1},{4,6},{5,7},{6,4},{7,5},{8,10},{9,11},{10,... | collective-permute-start | bytes 3932168 | tf_op jit(solution)/shard_map/ppermute | solution.py:501
  1088.0 143.3 %collective-permute-start.31 = (bf16[12,32,1024]{2,1,0:T(8,128)(2,1)}, bf16[12,32,1024]{2,1,0:T(8,128)(2,1)}, u32[]{:S(2)}, u32[]{:S(2)}) collective-permute-start(bf16[12,32,1024]{2,1,0:T(8,128)(2,1)} %sum_blocks.34.refs_4_), channel_id=1, source_target_pairs={{0,1},{1,0},{2,3},{3,2},{4,5},{5,4},{6,7},{7,6},{8,9},{9,8},{10,11... | collective-permute-start | bytes 2359304 | tf_op jit(solution)/shard_map/ppermute | solution.py:501
  1171.6 27.2 %collective-permute-start.24 = (bf16[7,32,1024]{2,1,0:T(8,128)(2,1)}, bf16[7,32,1024]{2,1,0:T(8,128)(2,1)}, u32[]{:S(2)}, u32[]{:S(2)}) collective-permute-start(bf16[7,32,1024]{2,1,0:T(8,128)(2,1)} %sum_blocks.35.refs_5_), channel_id=1, source_target_pairs={{0,16},{8,24},{16,0},{24,8},{1,17},{9,25},{17,1},{25,9},{2,18},{10... | collective-permute-start | bytes 1376264 | tf_op jit(solution)/shard_map/ppermute | solution.py:501
  1177.7 51.4 %collective-permute-start.26 = (bf16[7,32,1024]{2,1,0:T(8,128)(2,1)}, bf16[7,32,1024]{2,1,0:T(8,128)(2,1)}, u32[]{:S(2)}, u32[]{:S(2)}) collective-permute-start(bf16[7,32,1024]{2,1,0:T(8,128)(2,1)} %sum_blocks.36.refs_5_), channel_id=1, source_target_pairs={{0,4},{1,5},{2,6},{3,7},{4,0},{5,1},{6,2},{7,3},{8,12},{9,13},{10,... | collective-permute-start | bytes 1376264 | tf_op jit(solution)/shard_map/ppermute | solution.py:501
  1191.7 5.7 copy-start.54
  1191.7 5.7 copy-start.55
  1191.7 5.7 copy-start.56
  1194.8 48.2 %collective-permute-start.28 = (bf16[10,32,1024]{2,1,0:T(8,128)(2,1)}, bf16[10,32,1024]{2,1,0:T(8,128)(2,1)S(1)}, u32[]{:S(2)}, u32[]{:S(2)}) collective-permute-start(bf16[10,32,1024]{2,1,0:T(8,128)(2,1)} %sum_blocks.37.refs_5_), channel_id=1, source_target_pairs={{0,4},{1,5},{2,6},{3,7},{4,0},{5,1},{6,2},{7,3},{8,12},{9,13},{10,... | collective-permute-start | bytes 1966088 | tf_op jit(solution)/shard_map/ppermute | solution.py:501
  1204.1 52.9 %collective-permute-start.30 = (bf16[10,32,1024]{2,1,0:T(8,128)(2,1)}, bf16[10,32,1024]{2,1,0:T(8,128)(2,1)S(1)}, u32[]{:S(2)}, u32[]{:S(2)}) collective-permute-start(bf16[10,32,1024]{2,1,0:T(8,128)(2,1)} %sum_blocks.38.refs_5_), channel_id=1, source_target_pairs={{0,4},{1,5},{2,6},{3,7},{4,0},{5,1},{6,2},{7,3},{8,12},{9,13},{10,... | collective-permute-start | bytes 1966088 | tf_op jit(solution)/shard_map/ppermute | solution.py:501
  1233.8 25.9 %collective-permute-start.32 = (bf16[6,32,1024]{2,1,0:T(8,128)(2,1)}, bf16[6,32,1024]{2,1,0:T(8,128)(2,1)S(1)}, u32[]{:S(2)}, u32[]{:S(2)}) collective-permute-start(bf16[6,32,1024]{2,1,0:T(8,128)(2,1)} %sum_blocks.39), channel_id=1, source_target_pairs={{0,16},{8,24},{16,0},{24,8},{1,17},{9,25},{17,1},{25,9},{2,18},{10... | collective-permute-start | bytes 1179656 | tf_op jit(solution)/shard_map/ppermute | solution.py:501
  1243.1 18.5 %slice-start = ((s8[5242880]{0:T(1024)(128)(4,1)}), s8[4194304]{0:T(1024)(128)(4,1)S(1)}, s32[]{:S(2)}) async-start(s8[5242880]{0:T(1024)(128)(4,1)} %bitcast.289), calls=%async_computation.1 | async-start | bytes 8388608
  1245.9 15.7 %slice-start.1 = ((s8[5242880]{0:T(1024)(128)(4,1)}), s8[1048576]{0:T(1024)(128)(4,1)S(1)}, s32[]{:S(2)}) async-start(s8[5242880]{0:T(1024)(128)(4,1)} %bitcast.289), calls=%async_computation.2 | async-start | bytes 2097152
  (53 other events, 128.0 us)
Sparse Core Ops, SparseCore 0:
  11.9 446.3 all-gather.1

commit v3 on v2

--- a/solution.py
+++ b/solution.py
@@ -192,17 +192,12 @@
         def _():
             out_ref[...] = jnp.zeros_like(out_ref)
 
-        def one_bin(b, carry):
-            at = pl.ds(pl.multiple_of(b * channels, channels), channels)
-            out_ref[0] += lax.dot_general(
-                x_ref[0, b],
-                buffer[slot, at],
-                (((0,), (0,)), ((), ())),
-                preferred_element_type=jnp.float32,
-            )
-            return carry
-
-        lax.fori_loop(0, group, one_bin, 0)
+        out_ref[0] += lax.dot_general(
+            x_ref[0].reshape(group * channels, regions),
+            buffer[slot],
+            (((0,), (0,)), ((), ())),
+            preferred_element_type=jnp.float32,
+        )
 
     return pl.pallas_call(
         body,
@@ -265,25 +260,15 @@
 
         @pl.when(t < turns - 1)
         def _():
-            def one_bin(b, carry):
-                at = pl.ds(pl.multiple_of(b * channels, channels), channels)
-                buffer[slot, at] = jnp.dot(
-                    x_ref[0, b], gf_ref[0], preferred_element_type=jnp.float32
-                ).astype(jnp.bfloat16)
-                return carry
-
-            lax.fori_loop(0, group, one_bin, 0)
+            buffer[slot] = jnp.dot(
+                x_ref[0].reshape(rows, regions), gf_ref[0], preferred_element_type=jnp.float32
+            ).astype(jnp.bfloat16)
 
         @pl.when(t == turns - 1)
         def _():
-            def one_part(b, carry):
-                at = pl.ds(pl.multiple_of(b * channels, channels), channels)
-                buffer[slot, at] = jnp.dot(
-                    a_ref[0, at], gs_ref[0], preferred_element_type=jnp.float32
-                ).astype(jnp.bfloat16)
-                return carry
-
-            lax.fori_loop(0, wide // channels, one_part, 0)
+            buffer[slot, 0:wide] = jnp.dot(
+                a_ref[0], gs_ref[0], preferred_element_type=jnp.float32
+            ).astype(jnp.bfloat16)
 
         for kind in range(kinds):
 
@@ -365,15 +350,16 @@
 
         pltpu.make_async_copy(buffer.at[slot], buffer.at[slot], sem.at[slot]).wait()
 
+        grads = lax.dot_general(
+            g_ref[0], buffer[slot], (((1,), (1,)), ((), ())), preferred_element_type=jnp.float32
+        )
+        for b in range(group):
+            pooled[b * regions : (b + 1) * regions] = grads[
+                :, b * channels : (b + 1) * channels
+            ].astype(jnp.bfloat16)
+
         def one_bin(b, carry):
             p = t * group + b
-            at = pl.ds(pl.multiple_of(b * channels, channels), channels)
-            pooled[at] = lax.dot_general(
-                g_ref[0],
-                buffer[slot, at],
-                (((1,), (1,)), ((), ())),
-                preferred_element_type=jnp.float32,
-            ).astype(jnp.bfloat16)
             here = pl.ds(pl.multiple_of(b * regions, regions), regions)
             across[:, here] = column_weights(
                 col_ref[0, pl.ds(p, 1), :], fc_ref[0, pl.ds(p, 1), :], breadth
@@ -419,7 +405,7 @@
             scratch_shapes=[
                 pltpu.VMEM((2, count * block_rows, hidden), jnp.bfloat16),
                 pltpu.SemaphoreType.DMA((2,)),
-                pltpu.VMEM((group * channels, channels), jnp.bfloat16),
+                pltpu.VMEM((group * regions, channels), jnp.bfloat16),
                 pltpu.VMEM((breadth, group * regions), jnp.bfloat16),
                 pltpu.VMEM((lines, group * regions), jnp.float32),
                 pltpu.VMEM((chunk * breadth, group * regions), jnp.bfloat16),
@@ -473,8 +459,9 @@
 
 
 PARTS = ((7, "zwxy"), (7, "yxzw"), (10, "xzyw"), (10, "yxzw"), (6, "zwxy"))
-TURNS_AT = {0: 5, 5: 6, 7: 3, 8: 2, 10: 5}
-REST_AT = 15
+TURNS_AT = {0: 5, 5: 7, 7: 3, 8: 6}
+EDGES_AT = 11
+REST_AT = 12
 
 
 def part_orders(n_img, n_tile):
@@ -511,21 +498,16 @@
         half = terms[i][-1].shape[0] // 2
         last = sum_blocks(terms[i], half, last)
         terms[i].append(swap(last, *orders[i][stage]))
-    results = []
-    for part in terms:
-        size = part[-1].shape[0]
-        results.append(sum(term[:size].astype(jnp.float32) for term in part))
-    return results
-
-
-def sum_everywhere(wide, narrow, after, n_img, n_tile):
+    return terms
+
+
+def sum_everywhere(wide, narrow, exact, after, n_img, n_tile):
     x = [("tile", 1)]
     y = [("img", 1 << b) for b in bits_of(n_img)[1:]]
     z = [("tile", 1 << b) for b in bits_of(n_tile)[1:]]
     pair = [("img", 1)]
     orders = [pair + x + y + z, pair + y + z + x, pair + z + x + y]
     stages = len(orders[0])
-    streams = len(orders)
     lanes = 128
     placed, rows = [], 0
     for i, array in enumerate(wide):
@@ -535,14 +517,27 @@
     for i, array in enumerate(narrow):
         placed.append((len(wide) + i, 0, rows, array.shape[0], array.shape[1]))
         rows += array.shape[0]
-    unit = 8 * n_img * n_tile
-    size = -(-rows // (streams * unit)) * unit
-    operands = list(wide) + list(narrow)
+    unit = 16 * n_img * n_tile
+    units = -(-rows // unit)
+    streams, first = [], 0
+    for i, order in enumerate(orders):
+        size = (units + len(orders) - 1 - i) // len(orders) * unit
+        if size:
+            streams.append((order, first, size, True))
+            first += size
+    filled = first
+    count = exact.shape[0]
+    small = -(-count // (8 * n_img * n_tile)) * 8 * n_img * n_tile
+    streams.append((orders[0], 0, small, False))
+    operands = list(wide) + list(narrow) + [exact]
     number = len(operands)
 
     def body(*refs):
         inputs = refs[:number]
-        out_ref, total, landing, send, recv, send_back, recv_back = refs[number + 1 :]
+        (out_low, out_exact, total, going, landing, total_exact, landing_exact) = refs[
+            number + 1 : number + 8
+        ]
+        send, recv, send_back, recv_back = refs[number + 8 :]
         place = {"img": lax.axis_index("img"), "tile": lax.axis_index("tile")}
 
         def partner(axis, step):
@@ -558,88 +553,109 @@
             pl.semaphore_signal(
                 barrier, inc=1, device_id=there, device_id_type=pl.DeviceIdType.MESH
             )
-        pl.semaphore_wait(barrier, stages)
-
-        for i, half, first, count, columns in placed:
+        for i, half, first, size, columns in placed:
             if columns < lanes:
-                total[first : first + count] = jnp.zeros((count, lanes), jnp.float32)
-            total[first : first + count, :columns] = inputs[i][
+                total[first : first + size] = jnp.zeros((size, lanes), jnp.float32)
+            total[first : first + size, :columns] = inputs[i][
                 :, half * lanes : half * lanes + columns
             ]
-        if rows < streams * size:
-            total[rows:] = jnp.zeros((streams * size - rows, lanes), jnp.float32)
-
-        start = [s * size for s in range(streams)]
+        if rows < filled:
+            total[rows:] = jnp.zeros((filled - rows, lanes), jnp.float32)
+        total_exact[...] = jnp.zeros_like(total_exact)
+        total_exact[0:count] = inputs[-1][...]
+        pl.semaphore_wait(barrier, stages)
+
+        start = [first for _, first, _, _ in streams]
         copies = {}
 
-        def rows_at(first, count):
-            return pl.ds(pl.multiple_of(first, 8), count)
-
-        def send_half(s, k):
-            half = size >> (k + 1)
-            bit, there = partner(*orders[s][k])
+        def rows_at(first, size):
+            return pl.ds(pl.multiple_of(first, min(size, 16)), size)
+
+        def remote(source, target, there, sent, received):
             copy = pltpu.make_async_remote_copy(
-                src_ref=total.at[rows_at(start[s] + (1 - bit) * half, half)],
-                dst_ref=landing.at[pl.ds(s * size + size - 2 * half, half)],
-                send_sem=send.at[s, k],
-                recv_sem=recv.at[s, k],
+                src_ref=source,
+                dst_ref=target,
+                send_sem=sent,
+                recv_sem=received,
                 device_id=there,
                 device_id_type=pl.DeviceIdType.MESH,
             )
             copy.start()
-            copies[s, k] = copy
-
-        for s in range(streams):
+            return copy
+
+        def send_half(s, k):
+            order, first, size, low = streams[s]
+            half = size >> (k + 1)
+            bit, there = partner(*order[k])
+            away = rows_at(start[s] + (1 - bit) * half, half)
+            landed = pl.ds(first + size - 2 * half, half)
+            if low:
+                going[away] = total[away].astype(jnp.bfloat16)
+                source, target = going.at[away], landing.at[landed]
+            else:
+                source, target = total_exact.at[away], landing_exact.at[landed]
+            copies[s, k] = remote(source, target, there, send.at[s, k], recv.at[s, k])
+
+        for s in range(len(streams)):
             send_half(s, 0)
         for k in range(stages):
-            for s in range(streams):
+            for s, (order, first, size, low) in enumerate(streams):
                 half = size >> (k + 1)
-                bit, _ = partner(*orders[s][k])
+                bit, _ = partner(*order[k])
                 copies[s, k].wait()
                 keep = rows_at(start[s] + bit * half, half)
-                target = out_ref if k == stages - 1 else total
-                target[keep] = total[keep] + landing[pl.ds(s * size + size - 2 * half, half)]
+                landed = pl.ds(first + size - 2 * half, half)
+                if low:
+                    value = total[keep] + landing[landed].astype(jnp.float32)
+                    if k == stages - 1:
+                        out_low[keep] = value.astype(jnp.bfloat16)
+                    else:
+                        total[keep] = value
+                else:
+                    target = out_exact if k == stages - 1 else total_exact
+                    target[keep] = total_exact[keep] + landing_exact[landed]
                 start[s] = start[s] + bit * half
                 if k + 1 < stages:
                     send_half(s, k + 1)
 
         def send_back_half(s, k):
+            order, _, size, low = streams[s]
             half = size >> (k + 1)
-            _, there = partner(*orders[s][k])
+            _, there = partner(*order[k])
             at = rows_at(start[s], half)
-            copy = pltpu.make_async_remote_copy(
-                src_ref=out_ref.at[at],
-                dst_ref=out_ref.at[at],
-                send_sem=send_back.at[s, k],
-                recv_sem=recv_back.at[s, k],
-                device_id=there,
-                device_id_type=pl.DeviceIdType.MESH,
+            out = out_low if low else out_exact
+            copies[s, k] = remote(
+                out.at[at], out.at[at], there, send_back.at[s, k], recv_back.at[s, k]
             )
-            copy.start()
-            copies[s, k] = copy
-
-        for s in range(streams):
+
+        for s in range(len(streams)):
             send_back_half(s, stages - 1)
         for k in reversed(range(stages)):
-            for s in range(streams):
+            for s, (order, _, size, _) in enumerate(streams):
                 half = size >> (k + 1)
-                bit, _ = partner(*orders[s][k])
+                bit, _ = partner(*order[k])
                 copies[s, k].wait()
                 start[s] = start[s] - bit * half
                 if k > 0:
                     send_back_half(s, k - 1)
 
     whole = pl.BlockSpec(memory_space=pltpu.VMEM)
-    result = pl.pallas_call(
+    low, high = pl.pallas_call(
         body,
         in_specs=[whole] * number + [pl.BlockSpec(memory_space=pl.ANY)],
-        out_specs=whole,
-        out_shape=jax.ShapeDtypeStruct((streams * size, lanes), jnp.float32),
+        out_specs=[whole, whole],
+        out_shape=[
+            jax.ShapeDtypeStruct((filled, lanes), jnp.bfloat16),
+            jax.ShapeDtypeStruct((small, lanes), jnp.float32),
+        ],
         scratch_shapes=[
-            pltpu.VMEM((streams * size, lanes), jnp.float32),
-            pltpu.VMEM((streams * size, lanes), jnp.float32),
+            pltpu.VMEM((filled, lanes), jnp.float32),
+            pltpu.VMEM((filled, lanes), jnp.bfloat16),
+            pltpu.VMEM((filled, lanes), jnp.bfloat16),
+            pltpu.VMEM((small, lanes), jnp.float32),
+            pltpu.VMEM((small, lanes), jnp.float32),
         ]
-        + [pltpu.SemaphoreType.DMA((streams, stages))] * 4,
+        + [pltpu.SemaphoreType.DMA((len(streams), stages))] * 4,
         compiler_params=pltpu.CompilerParams(
             collective_id=0, has_side_effects=True, vmem_limit_bytes=VMEM_LIMIT
         ),
@@ -647,15 +663,90 @@
     )(*operands, after)
     results, at = [], 0
     for array in wide:
-        count = array.shape[0]
+        size = array.shape[0]
         results.append(
-            jnp.concatenate([result[at : at + count], result[at + count : at + 2 * count]], axis=1)
-        )
-        at += 2 * count
+            jnp.concatenate([low[at : at + size], low[at + size : at + 2 * size]], axis=1).astype(
+                jnp.float32
+            )
+        )
+        at += 2 * size
     for array in narrow:
-        results.append(result[at : at + array.shape[0], : array.shape[1]])
+        results.append(low[at : at + array.shape[0], : array.shape[1]].astype(jnp.float32))
         at += array.shape[0]
-    return results
+    return results + [high[:count]]
+
+
+def edge_rows(grad_flat, from_last, from_next, images, height, breadth, rim, after):
+    channels = grad_flat.shape[1]
+    padded = height + 2 * rim
+    low, high = from_last.astype(jnp.bfloat16), from_next.astype(jnp.bfloat16)
+
+    def body(own_ref, last_ref, next_ref, after_ref, out_ref):
+        del after_ref
+        for i in range(images):
+            for r in range(height + 2):
+                line = r + rim - 1
+                at = (i * padded + line) * breadth
+                value = own_ref[at : at + breadth]
+                if r < rim + 1:
+                    value = value + last_ref[i, r].astype(jnp.float32)
+                if r >= height + 1 - rim:
+                    value = value + next_ref[i, r - (height + 1 - rim)].astype(jnp.float32)
+                out_ref[i, r] = value.astype(jnp.bfloat16)
+
+    whole = pl.BlockSpec(memory_space=pltpu.VMEM)
+    return pl.pallas_call(
+        body,
+        in_specs=[whole] * 3 + [pl.BlockSpec(memory_space=pl.ANY)],
+        out_specs=whole,
+        out_shape=jax.ShapeDtypeStruct((images, height + 2, breadth, channels), jnp.bfloat16),
+        compiler_params=pltpu.CompilerParams(vmem_limit_bytes=VMEM_LIMIT),
+        name="edge_rows",
+    )(grad_flat, low, high, after)
+
+
+def finish_blocks(terms, start, share, masters, firsts, seconds, held, scale, old):
+    slots, block_rows, hidden = masters.shape
+    count = len(terms)
+    correct_one = 1.0 - BETA_ONE ** float(STEP)
+    correct_two = 1.0 - BETA_TWO ** float(STEP)
+
+    def body(held_ref, scale_ref, *refs):
+        total = None
+        for ref in refs[:count]:
+            value = ref[...].astype(jnp.float32)
+            total = value if total is None else total + value
+        w_ref, m_ref, v_ref = refs[count : count + 3]
+        outs = refs[-3:]
+        mine = held_ref[start + pl.program_id(0)] >= 0
+        grad = jnp.where(mine, total * scale_ref[0], 0.0)
+        first_new = BETA_ONE * m_ref[...] + (1.0 - BETA_ONE) * grad
+        second_new = BETA_TWO * v_ref[...] + (1.0 - BETA_TWO) * grad * grad
+        rooted = jnp.sqrt(second_new * (1.0 / correct_two)) + EPSILON
+        outs[0][...] = w_ref[...] - RATE * (
+            first_new * (1.0 / correct_one) / rooted + DECAY * w_ref[...]
+        )
+        outs[1][...] = first_new
+        outs[2][...] = second_new
+
+    term = pl.BlockSpec((1, block_rows, hidden), lambda i: (i, 0, 0))
+    slot = pl.BlockSpec((1, block_rows, hidden), lambda i: (start + i, 0, 0))
+    smem = pl.BlockSpec(memory_space=pltpu.SMEM)
+    kept = [] if old is None else list(old)
+    inputs = [held, scale] + list(terms) + [masters, firsts, seconds] + kept
+    return pl.pallas_call(
+        body,
+        grid=(share,),
+        in_specs=[smem, smem]
+        + [term] * count
+        + [slot] * 3
+        + [pl.BlockSpec(memory_space=pl.ANY)] * len(kept),
+        out_specs=[slot] * 3,
+        out_shape=[jax.ShapeDtypeStruct(masters.shape, jnp.float32)] * 3,
+        input_output_aliases={len(inputs) - 3 + j: j for j in range(len(kept))},
+        compiler_params=pltpu.CompilerParams(vmem_limit_bytes=VMEM_LIMIT),
+        name="finish_blocks",
+    )(*inputs)
 
 
 def on_device(
@@ -842,23 +933,23 @@
 
         return work
 
+    def edges(after):
+        grad_padded_map = found["map"].reshape(images, padded_rows, breadth, channels)
+        to_next = grad_padded_map[:, height + rim - 1 :].astype(jnp.bfloat16)
+        to_last = grad_padded_map[:, : rim + 1].astype(jnp.bfloat16)
+        ends = n_tile - 1
+        from_last = lax.ppermute(to_next, "tile", [(i, i + 1) for i in range(ends)])
+        from_next = lax.ppermute(to_last, "tile", [(i + 1, i) for i in range(ends)])
+        found["rows"] = edge_rows(
+            found["map"], from_last, from_next, images, height, breadth, rim, after
+        )
+        return found["rows"]
+
     def rest(after):
-        grad_flat = found["map"]
-        grad_padded_map = grad_flat.reshape(images, padded_rows, breadth, channels)
-        outer_rims = jnp.concatenate(
-            [grad_padded_map[:, :rim], grad_padded_map[:, rim + height :]], axis=1
-        )
-        returned = padded_2(outer_rims, (("tile", 1),), rim)
-        grad_own = grad_padded_map[:, rim : rim + height]
-        grad_own = (
-            grad_own.at[:, :rim]
-            .add(returned[:, :rim])
-            .at[:, height - rim :]
-            .add(returned[:, 3 * rim :])
-        )
-        grad_map = grad_own.astype(jnp.bfloat16)
+        grad_rows = found["rows"]
+        grad_map = grad_rows[:, 1 : height + 1]
         grad_conv_bias = jnp.sum(grad_map.astype(jnp.float32), axis=(0, 1, 2))
-        grad_map_padded = jnp.pad(padded_2(grad_map, (("tile", 1),), 1), column_pad)
+        grad_map_padded = jnp.pad(grad_rows, column_pad)
         grad_taps, grad_lateral_full = convolve_back(
             grad_map_padded, lateral_padded, grad_map, kernel_taps, height, breadth
         )
@@ -876,7 +967,7 @@
         misc = jnp.pad(misc, (0, filled - misc.size)).reshape(-1, 128)
         heads = jnp.stack(head_grads).reshape(-1, out_width)
         found["sums"] = sum_everywhere(
-            [grad_lateral_w, grad_taps], [heads, misc], after, n_img, n_tile
+            [grad_lateral_w, grad_taps], [heads], misc, after, n_img, n_tile
         )
         return found["sums"][-1]
 
@@ -884,8 +975,9 @@
     for at, count in TURNS_AT.items():
         events[at] = turns_of(start, start + count)
         start += count
+    events[EDGES_AT] = edges
     events[REST_AT] = rest
-    block_parts = sum_parts(parts[0::2], parts[1::2], orders, events)
+    block_terms = sum_parts(parts[0::2], parts[1::2], orders, events)
 
     conv_sum = jnp.concatenate(found["sums"][:2], axis=0)
     head_sum = found["sums"][2].reshape(section_count, hidden, out_width)
@@ -894,9 +986,13 @@
     bias_sum, loss_total, valid_sum = misc_sum[:biases], misc_sum[biases], misc_sum[biases + 1]
     scale = 1.0 / valid_sum
     mine = lax.dynamic_slice_in_dim(slot_block, (at_img * n_tile + at_tile) * slots, slots)
-    block_grad = jnp.where(
-        (mine >= 0)[:, None, None], jnp.concatenate(block_parts, axis=0) * scale, 0.0
-    )
+    held, old, start = mine, None, 0
+    for part, share in zip(block_terms, shares):
+        old = finish_blocks(
+            part, start, share, block_master, block_first, block_second, held, scale[None], old
+        )
+        start += share
+    block_new, block_first_new, block_second_new = old
     step = float(STEP)
     conv_new, conv_first_new, conv_second_new = adamw(
         conv_weight, conv_first, conv_second, conv_sum * scale, step
@@ -906,9 +1002,6 @@
     )
     bias_new, bias_first_new, bias_second_new = adamw(
         bias_vector, bias_first, bias_second, bias_sum * scale, step
-    )
-    block_new, block_first_new, block_second_new = adamw(
-        block_master, block_first, block_second, block_grad, step
     )
     loss = (loss_total * scale).reshape(1)
     return (

time: 1290 us -> 1190 us (0.922)
  starting transfers between devices: 108 us -> 42.9 us
  other arithmetic: 67.9 us -> 43.5 us
  waiting for transfers between devices: 408 us -> 390 us
    pallas_call x0 -> x6, Pallas kernels: none -> 40.2 us  [the longest x5 36.5 us: finish_blocks(): pl.pallas_call(body, grid=(share,), in_specs=[smem, smem] + [term] * coun...]
    ppermute x4 -> x2, starting transfers between devices: 43 us -> 9.4 us  [padded_2(): lax.ppermute(tail, axis, [(i, (i + 1) % count) for i in range(ends)])]
    ppermute x25, starting transfers between devices: 59.7 us -> 26.1 us  [swap(): return lax.ppermute(values, axis, [(i, i ^ 1 << bit) for i in range(count)])]
    pallas_call x5 -> x4, Pallas kernels: 172 us -> 148 us  [map_grads(): pl.pallas_call(body, grid_spec=pltpu.PrefetchScalarGridSpec(num_scalar_pr...]
    pallas_call x1, Pallas kernels: 79.4 us -> 102 us  [sum_everywhere(): pl.pallas_call(body, in_specs=[whole] * number + [pl.BlockSpec(memory_spa...]
    pallas_call x1, Pallas kernels: 66.5 us -> 46.5 us  [weight_grads(): pl.pallas_call(body, grid_spec=pltpu.PrefetchScalarGridSpec(num_scalar_pr...]
    pallas_call x1, Pallas kernels: 58.1 us -> 40.8 us  [first_layer(): pl.pallas_call(body, grid_spec=pltpu.PrefetchScalarGridSpec(num_scalar_pr...]
  transfers between devices with their start and end apart: 34 -> 32, of which waited for: 11 -> 11; matrix products, arithmetic and copies ran while one was open for 8% -> 7% of each run, Pallas kernels for 35% -> 41%
where the time goes in v3:
time: 1190 us; the launch traced here: 1180 us
  Pallas kernels  572 us (48%)
  waiting for transfers between devices  390 us (33%)
  local copies, waits for them, and re-layouts  59.2 us (5%)
  matrix products  47.9 us (4%)
  other arithmetic  43.5 us (4%)
  starting transfers between devices  42.9 us (4%)
  between operations  20.2 us (2%)
    all_gather x1, waiting for transfers between devices, on_device(): lax.all_gather(block_master.astype(jnp.bfloat16), AXES, axis=0, tiled=True)  281 us
    pallas_call x4, Pallas kernels, map_grads(): pl.pallas_call(body, grid_spec=pltpu.PrefetchScalarGridSpec(num_scalar_pr...  148 us
    pallas_call x1, Pallas kernels, pool_regions(): pl.pallas_call(body, grid=(section_count, bins // group), in_specs=[pl.Bl...  109 us
    pallas_call x1, Pallas kernels, sum_everywhere(): pl.pallas_call(body, in_specs=[whole] * number + [pl.BlockSpec(memory_spa...  102 us
    ppermute x25, waiting for transfers between devices, swap(): return lax.ppermute(values, axis, [(i, i ^ 1 << bit) for i in range(count)])  99.9 us
    pallas_call x20, Pallas kernels, sum_blocks(): pl.pallas_call(body, grid=(half // batch,), in_specs=[pl.BlockSpec((batch...  86.4 us
    pallas_call x1, Pallas kernels, weight_grads(): pl.pallas_call(body, grid_spec=pltpu.PrefetchScalarGridSpec(num_scalar_pr...  46.5 us
    pallas_call x1, Pallas kernels, first_layer(): pl.pallas_call(body, grid_spec=pltpu.PrefetchScalarGridSpec(num_scalar_pr...  40.8 us
  transfers between devices with their start and end apart: 32, of which 11 were waited for; matrix products, arithmetic and copies ran while one was open for 7% of the time, Pallas kernels for 41%

profile of v3, /device:TPU:0, one launch (start us, length us, event | category | flops | bytes accessed | tf_op | source)
XLA Modules:
  0.0 1175.8 jit_solution(1978314458917941270)
XLA Ops:
  7.2 4.5 convert_element_type.135
  15.7 4.8 collective-permute-start
  21.9 5.2 scatter_custom_fusion.table_ref
  31.6 3.0 fusion.138
  36.0 5.2 sort.31
  50.3 4.6 collective-permute-start.2
  57.2 4.8 collective-permute-done.2
  62.0 4.1 collective-permute-done.3
  68.6 108.7 %pool_regions.1.x_ref = bf16[3,49,256,256]{3,2,1,0:T(8,128)(2,1)} custom-call(bf16[256,3840]{1,0:T(8,128)(2,1)} %bitcast.298, s32[3,49,256]{2,1,0:T(8,128)} %get-tuple-element.120.row_ref, s32[3,49,256]{2,1,0:T(8,128)} %get-tuple-element.119.col_ref, f32[3,49,256]{2,1,0:T(8,128)} %get-tuple-element.177.fr_ref, f32[3,49,256]{2,1,0:T(8,128)} %get-tuple-element.176.fc_ref), custom_call_target="tpu_custom_call" | custom-call | flops 73987522560 | bytes 19267584 | tf_op jit(solution)/shard_map/pool_regions/pallas_call | solution.py:136
  177.3 280.8 %all-gather.2.cloned.1.call-done.blocks_ref = bf16[1280,32,1024]{2,1,0:T(8,128)(2,1)} async-done(((bf16[40,32,1024]{2,1,0:T(8,128)(2,1)}), bf16[1280,32,1024]{2,1,0:T(8,128)(2,1)}) %all-gather.2.cloned.1.call-update) | async-done | bytes 83886096 | tf_op jit(solution)/shard_map/all_gather | solution.py:789
  458.1 40.8 %first_layer.1 = f32[3,256,1024]{2,1,0:T(8,128)} custom-call(s32[1272]{0:T(1024)} %copy-done.61, bf16[1280,32,1024]{2,1,0:T(8,128)(2,1)} %all-gather.2.cloned.1.call-done.blocks_ref, bf16[3,49,256,256]{3,2,1,0:T(8,128)(2,1)} %pool_regions.1.x_ref), custom_call_target="tpu_custom_call" | custom-call | flops 19730006016 | bytes 96337920 | tf_op jit(solution)/shard_map/first_layer/pallas_call | solution.py:202
  499.0 3.6 gather_fusion.2
  502.6 3.7 multiply_convert_fusion.3
  508.0 3.5 gather_fusion.1
  511.6 3.8 multiply_convert_fusion.5
  519.6 3.5 gather_fusion
  523.2 3.8 multiply_convert_fusion.7
  533.4 2.5 convert_reduce_fusion.7
  546.8 46.5 %weight_grads.1 = (bf16[112,32,1024]{2,1,0:T(8,128)(2,1)}, bf16[112,32,1024]{2,1,0:T(8,128)(2,1)}, bf16[112,32,1024]{2,1,0:T(8,128)(2,1)}, bf16[112,32,1024]{2,1...) custom-call(s32[1272]{0:T(1024)} %get-tuple-element.45.order_ref, ...), custom_call_target="tpu_custom_call" | custom-call | flops 21340618752 | bytes 104202240 | tf_op jit(solution)/shard_map/weight_grads/pallas_call | solution.py:291
  596.9 35.5 %map_grads.4.refs_2_.old_ref = f32[3840,256]{1,0:T(8,128)} custom-call(s32[1272]{0:T(1024)} %copy-done.61, bf16[1280,32,1024]{2,1,0:T(8,128)(2,1)} %all-gather.2.cloned.1.call-done.blocks_ref, bf16[3,256,1024]{2,1,0:T(8,128)(2,1)} %pad_maximum_fusion.1.gf_ref.g_ref, s32[3,49,256]{2,1,0:T(8,128)} %get-tuple-element.120.row_ref, ...), custom_call_target="tpu_custom_call" | custom-call | flops 22313697280 | bytes 18350080 | tf_op jit(solution)/shard_map/map_grads/pallas_call | solution.py:393
  632.4 2.9 collective-permute-done.8.refs_1_
  635.4 5.6 sum_blocks.20.refs_2_
  640.9 4.9 collective-permute-done.7.refs_1_
  645.8 5.6 sum_blocks.21.refs_2_
  651.4 8.2 sum_blocks.22.refs_2_
  665.2 4.0 fusion.214
  669.2 8.0 sum_blocks.23.refs_2_
  678.7 5.4 sum_blocks.24.after_ref
  686.1 47.2 %map_grads.5.refs_3_.old_ref = f32[3840,256]{1,0:T(8,128)} custom-call(s32[1272]{0:T(1024)} %copy-done.61, bf16[1280,32,1024]{2,1,0:T(8,128)(2,1)} %all-gather.2.cloned.1.call-done.blocks_ref, bf16[3,256,1024]{2,1,0:T(8,128)(2,1)} %pad_maximum_fusion.1.gf_ref.g_ref, s32[3,49,256]{2,1,0:T(8,128)} %get-tuple-element.120.row_ref, ...), custom_call_target="tpu_custom_call" | custom-call | flops 31239176192 | bytes 25690112 | tf_op jit(solution)/shard_map/map_grads/pallas_call | solution.py:393
  733.3 10.2 collective-permute-done.10.refs_2_
  743.6 3.8 sum_blocks.25.refs_3_
  748.8 3.8 sum_blocks.26.after_ref
  752.7 23.8 %map_grads.6.refs_3_.old_ref = f32[3840,256]{1,0:T(8,128)} custom-call(s32[1272]{0:T(1024)} %copy-done.61, bf16[1280,32,1024]{2,1,0:T(8,128)(2,1)} %all-gather.2.cloned.1.call-done.blocks_ref, bf16[3,256,1024]{2,1,0:T(8,128)(2,1)} %pad_maximum_fusion.1.gf_ref.g_ref, s32[3,49,256]{2,1,0:T(8,128)} %get-tuple-element.120.row_ref, ...), custom_call_target="tpu_custom_call" | custom-call | flops 13388218368 | bytes 11010048 | tf_op jit(solution)/shard_map/map_grads/pallas_call | solution.py:393
  776.5 5.5 sum_blocks.27.after_ref
  782.0 41.2 %map_grads.7.refs_3_.own_ref = f32[3840,256]{1,0:T(8,128)} custom-call(s32[1272]{0:T(1024)} %copy-done.61, bf16[1280,32,1024]{2,1,0:T(8,128)(2,1)} %all-gather.2.cloned.1.call-done.blocks_ref, bf16[3,256,1024]{2,1,0:T(8,128)(2,1)} %pad_maximum_fusion.1.gf_ref.g_ref, s32[3,49,256]{2,1,0:T(8,128)} %get-tuple-element.120.row_ref, ...), custom_call_target="tpu_custom_call" | custom-call | flops 26776436736 | bytes 22020096 | tf_op jit(solution)/shard_map/map_grads/pallas_call | solution.py:393
  826.5 3.3 collective-permute-start.12
  833.0 2.9 copy.160
  838.1 16.9 %collective-permute-done.16.refs_2_ = bf16[80,32,1024]{2,1,0:T(8,128)(2,1)} collective-permute-done((bf16[80,32,1024]{2,1,0:T(8,128)(2,1)}, bf16[80,32,1024]{2,1,0:T(8,128)(2,1)}, u32[]{:S(2)}, u32[]{:S(2)}) %collective-permute-start.16) | collective-permute-done | bytes 5242912 | tf_op jit(solution)/shard_map/ppermute | solution.py:488
  855.6 5.5 sum_blocks.28.refs_3_
  862.8 3.7 sum_blocks.29.refs_4_
  868.0 3.4 sum_blocks.30.after_ref
  874.0 3.7 edge_rows.1.refs_4_
  883.6 2.6 convert_reduce_fusion.1
  894.5 3.8 collective-permute-done.17.refs_3_
  898.3 3.4 sum_blocks.31.refs_4_
  911.2 102.2 %sum_everywhere.1 = (bf16[8192,128]{1,0:T(8,128)(2,1)}, f32[256,128]{1,0:T(8,128)}) custom-call(f32[256,256]{1,0:T(8,128)} %fusion.56.refs_0_, f32[2304,256]{1,0:T(8,128)} %copy-done.22, f32[3072,85]{1,0:T(8,128)} %bitcast.290, f32[56,128]{1,0:T(8,128)} %pad_bitcast_fusion.refs_3_, bf16[14,32,1024]{2,1,0:T(8,128)(2,1)} %sum_blocks.31.refs_4_), custom_call_target="tpu_custom_call" | custom-call | tf_op jit(solution)/shard_map/sum_everywhere/pallas_call | solution.py:643
  1018.3 3.7 sum_blocks.32.refs_4_
  1023.0 3.8 sum_blocks.33.refs_4_
  1028.0 6.0 multiply_subtract_fusion
  1034.0 3.1 sum_blocks.34.refs_5_
  1038.7 2.6 sum_blocks.35.refs_5_
  1042.3 2.6 sum_blocks.36.refs_5_
  1044.9 8.3 collective-permute-done.23.refs_4_
  1054.3 3.1 sum_blocks.37.refs_5_
  1060.1 3.1 sum_blocks.38.refs_5_
  1070.7 2.6 sum_blocks.39
  1075.0 2.4 multiply_subtract_fusion.1
  1077.4 2.3 collective-permute-done.30.refs_5_
  1079.7 6.6 finish_blocks.5
  1086.4 50.3 %collective-permute-done.29.refs_5_ = bf16[7,32,1024]{2,1,0:T(8,128)(2,1)} collective-permute-done((bf16[7,32,1024]{2,1,0:T(8,128)(2,1)S(1)}, bf16[7,32,1024]{2,1,0:T(8,128)(2,1)}, u32[]{:S(2)}, u32[]{:S(2)}) %collective-permute-start.29) | collective-permute-done | bytes 458784 | tf_op jit(solution)/shard_map/ppermute | solution.py:488
  1136.7 6.6 finish_blocks.6
  1143.4 8.7 finish_blocks.7
  1152.1 8.7 finish_blocks.8
  1161.6 5.8 finish_blocks.9
  (365 shorter events, 120.5 us)
Async XLA Ops:
  7.2 7.1 copy-start
  7.2 450.9 %all-gather.2.cloned.1.call-start = ((), (), s32[]{:S(2)}) async-start(), calls=%async_computation | async-start | bytes 86507520 | tf_op jit(solution)/shard_map/all_gather | solution.py:789
  14.3 7.5 copy-start.91
  14.3 12.8 %copy-start.106 = (s32[256]{0:T(256)S(1)}, s32[256]{0:T(256)}, u32[]{:S(2)}) copy-start(s32[256]{0:T(256)} %param.37) | copy-start | bytes 3076
  14.3 14.1 %copy-start.101 = (s32[3,256]{1,0:T(4,128)S(1)}, s32[3,256]{1,0:T(4,128)}, u32[]{:S(2)}) copy-start(s32[3,256]{1,0:T(4,128)} %param.40) | copy-start | bytes 9220
  14.3 14.1 %copy-start.89 = (s32[256]{0:T(256)S(1)}, s32[256]{0:T(256)}, u32[]{:S(2)}) copy-start(s32[256]{0:T(256)} %param.41) | copy-start | bytes 3076
  14.3 16.1 %copy-start.62 = (s32[3,49,256]{2,1,0:T(8,128)S(1)}, s32[3,49,256]{2,1,0:T(8,128)}, u32[]{:S(2)}) copy-start(s32[3,49,256]{2,1,0:T(8,128)} %param.38) | copy-start | bytes 451588
  14.3 17.0 %copy-start.60 = (f32[3,2,49,256]{3,1,2,0:T(2,128)S(1)}, f32[3,2,49,256]{3,1,2,0:T(2,128)}, u32[]{:S(2)}) copy-start(f32[3,2,49,256]{3,1,2,0:T(2,128)} %param.39) | copy-start | bytes 903172
  14.8 29.2 %copy-start.5 = (bf16[2,8,160,256]{3,2,1,0:T(8,128)(2,1)}, bf16[2,8,160,256]{3,2,1,0:T(8,128)(2,1)S(1)}, u32[]{:S(2)}) copy-start(bf16[2,8,160,256]{3,2,1,0:T(8,128)(2,1)S(1)} %add_convert_fusion.2) | copy-start | bytes 3932164
  15.7 26.3 %collective-permute-start = (bf16[2,1,160,256]{3,2,1,0:T(8,128)(2,1)}, bf16[2,1,160,256]{3,2,1,0:T(8,128)(2,1)S(1)}, u32[]{:S(2)}, u32[]{:S(2)}) collective-permute-start(bf16[2,1,160,256]{3,2,1,0:T(8,128)(2,1)} %get-tuple-element.115), channel_id=1, source_target_pairs={{0,1},{1,2},{2,3},{3,4},{4,5},{5,6},{6,7},{8,9},{9,10},{10,11},{11... | collective-permute-start | bytes 491528 | tf_op jit(solution)/shard_map/ppermute | solution.py:31
  20.5 23.0 %collective-permute-start.1 = (bf16[2,1,160,256]{3,2,1,0:T(8,128)(2,1)}, bf16[2,1,160,256]{3,2,1,0:T(8,128)(2,1)S(1)}, u32[]{:S(2)}, u32[]{:S(2)}) collective-permute-start(bf16[2,1,160,256]{3,2,1,0:T(8,128)(2,1)} %get-tuple-element.116), channel_id=1, source_target_pairs={{1,0},{2,1},{3,2},{4,3},{5,4},{6,5},{7,6},{9,8},{10,9},{11,10},{12... | collective-permute-start | bytes 491528 | tf_op jit(solution)/shard_map/ppermute | solution.py:33
  48.9 7.4 copy-start.102
  50.3 11.7 collective-permute-start.2
  54.9 11.2 collective-permute-start.3
  502.5 4.9 copy-start.73
  511.6 5.6 copy-start.75
  511.6 6.2 copy-start.9
  511.6 6.2 copy-start.84
  530.9 5.0 copy-start.78
  530.9 7.0 copy-start.80
  530.9 10.1 copy-start.76
  533.3 7.7 copy-start.53
  593.3 58.1 %collective-permute-start.6 = (bf16[160,32,1024]{2,1,0:T(8,128)(2,1)}, bf16[160,32,1024]{2,1,0:T(8,128)(2,1)}, u32[]{:S(2)}, u32[]{:S(2)}) collective-permute-start(bf16[160,32,1024]{2,1,0:T(8,128)(2,1)} %get-tuple-element.53), channel_id=1, source_target_pairs={{0,8},{8,0},{16,24},{24,16},{1,9},{9,1},{17,25},{25,17},{2,10},{10... | collective-permute-start | bytes 31457288 | tf_op jit(solution)/shard_map/ppermute | solution.py:488
  593.7 75.5 %collective-permute-start.5 = (bf16[160,32,1024]{2,1,0:T(8,128)(2,1)}, bf16[160,32,1024]{2,1,0:T(8,128)(2,1)}, u32[]{:S(2)}, u32[]{:S(2)}) collective-permute-start(bf16[160,32,1024]{2,1,0:T(8,128)(2,1)} %get-tuple-element.51), channel_id=1, source_target_pairs={{0,8},{8,0},{16,24},{24,16},{1,9},{9,1},{17,25},{25,17},{2,10},{10... | collective-permute-start | bytes 31457288 | tf_op jit(solution)/shard_map/ppermute | solution.py:488
  593.9 41.5 %collective-permute-start.8 = (bf16[112,32,1024]{2,1,0:T(8,128)(2,1)}, bf16[112,32,1024]{2,1,0:T(8,128)(2,1)}, u32[]{:S(2)}, u32[]{:S(2)}) collective-permute-start(bf16[112,32,1024]{2,1,0:T(8,128)(2,1)} %get-tuple-element.56), channel_id=1, source_target_pairs={{0,8},{8,0},{16,24},{24,16},{1,9},{9,1},{17,25},{25,17},{2,10},{10... | collective-permute-start | bytes 22020104 | tf_op jit(solution)/shard_map/ppermute | solution.py:488
  594.2 51.6 %collective-permute-start.7 = (bf16[112,32,1024]{2,1,0:T(8,128)(2,1)}, bf16[112,32,1024]{2,1,0:T(8,128)(2,1)}, u32[]{:S(2)}, u32[]{:S(2)}) collective-permute-start(bf16[112,32,1024]{2,1,0:T(8,128)(2,1)} %get-tuple-element.55), channel_id=1, source_target_pairs={{0,8},{8,0},{16,24},{24,16},{1,9},{9,1},{17,25},{25,17},{2,10},{10... | collective-permute-start | bytes 22020104 | tf_op jit(solution)/shard_map/ppermute | solution.py:488
  594.4 84.3 %collective-permute-start.4 = (bf16[96,32,1024]{2,1,0:T(8,128)(2,1)}, bf16[96,32,1024]{2,1,0:T(8,128)(2,1)}, u32[]{:S(2)}, u32[]{:S(2)}) collective-permute-start(bf16[96,32,1024]{2,1,0:T(8,128)(2,1)} %get-tuple-element.49), channel_id=1, source_target_pairs={{0,8},{8,0},{16,24},{24,16},{1,9},{9,1},{17,25},{25,17},{2,10},{10... | collective-permute-start | bytes 18874376 | tf_op jit(solution)/shard_map/ppermute | solution.py:488
  651.4 11.5 copy-start.6
  651.4 11.5 copy-start.40
  651.4 11.5 copy-start.42
  659.6 116.9 %collective-permute-start.11 = (bf16[80,32,1024]{2,1,0:T(8,128)(2,1)}, bf16[80,32,1024]{2,1,0:T(8,128)(2,1)}, u32[]{:S(2)}, u32[]{:S(2)}) collective-permute-start(bf16[80,32,1024]{2,1,0:T(8,128)(2,1)} %sum_blocks.22.refs_2_), channel_id=1, source_target_pairs={{0,1},{1,0},{2,3},{3,2},{4,5},{5,4},{6,7},{7,6},{8,9},{9,8},{10,11... | collective-permute-start | bytes 15728648 | tf_op jit(solution)/shard_map/ppermute | solution.py:488
  661.1 82.5 %collective-permute-start.10 = (bf16[56,32,1024]{2,1,0:T(8,128)(2,1)}, bf16[56,32,1024]{2,1,0:T(8,128)(2,1)}, u32[]{:S(2)}, u32[]{:S(2)}) collective-permute-start(bf16[56,32,1024]{2,1,0:T(8,128)(2,1)} %sum_blocks.20.refs_2_), channel_id=1, source_target_pairs={{0,2},{1,3},{2,0},{3,1},{4,6},{5,7},{6,4},{7,5},{8,10},{9,11},{10,... | collective-permute-start | bytes 11010056 | tf_op jit(solution)/shard_map/ppermute | solution.py:488
  661.1 87.8 %collective-permute-start.9 = (bf16[56,32,1024]{2,1,0:T(8,128)(2,1)}, bf16[56,32,1024]{2,1,0:T(8,128)(2,1)}, u32[]{:S(2)}, u32[]{:S(2)}) collective-permute-start(bf16[56,32,1024]{2,1,0:T(8,128)(2,1)} %sum_blocks.21.refs_2_), channel_id=1, source_target_pairs={{0,16},{8,24},{16,0},{24,8},{1,17},{9,25},{17,1},{25,9},{2,18},{10... | collective-permute-start | bytes 11010056 | tf_op jit(solution)/shard_map/ppermute | solution.py:488
  677.2 177.8 %collective-permute-start.16 = (bf16[80,32,1024]{2,1,0:T(8,128)(2,1)}, bf16[80,32,1024]{2,1,0:T(8,128)(2,1)}, u32[]{:S(2)}, u32[]{:S(2)}) collective-permute-start(bf16[80,32,1024]{2,1,0:T(8,128)(2,1)} %sum_blocks.23.refs_2_), channel_id=1, source_target_pairs={{0,16},{8,24},{16,0},{24,8},{1,17},{9,25},{17,1},{25,9},{2,18},{10... | collective-permute-start | bytes 15728648 | tf_op jit(solution)/shard_map/ppermute | solution.py:488
  684.1 177.0 %collective-permute-start.15 = (bf16[48,32,1024]{2,1,0:T(8,128)(2,1)}, bf16[48,32,1024]{2,1,0:T(8,128)(2,1)}, u32[]{:S(2)}, u32[]{:S(2)}) collective-permute-start(bf16[48,32,1024]{2,1,0:T(8,128)(2,1)} %sum_blocks.24.after_ref), channel_id=1, source_target_pairs={{0,2},{1,3},{2,0},{3,1},{4,6},{5,7},{6,4},{7,5},{8,10},{9,11},{10,... | collective-permute-start | bytes 9437192 | tf_op jit(solution)/shard_map/ppermute | solution.py:488
  747.4 119.1 %collective-permute-start.14 = (bf16[28,32,1024]{2,1,0:T(8,128)(2,1)}, bf16[28,32,1024]{2,1,0:T(8,128)(2,1)S(1)}, u32[]{:S(2)}, u32[]{:S(2)}) collective-permute-start(bf16[28,32,1024]{2,1,0:T(8,128)(2,1)} %sum_blocks.25.refs_3_), channel_id=1, source_target_pairs={{0,4},{1,5},{2,6},{3,7},{4,0},{5,1},{6,2},{7,3},{8,12},{9,13},{10,... | collective-permute-start | bytes 5505032 | tf_op jit(solution)/shard_map/ppermute | solution.py:488
  825.4 5.7 copy-start.27
  825.4 5.7 copy-start.58
  825.5 5.7 copy-start.81
  825.5 6.0 copy-start.29
  825.5 6.0 copy-start.56
  825.5 6.0 copy-start.79
  825.5 6.2 copy-start.25
  825.5 6.2 copy-start.54
  825.5 6.2 copy-start.77
  826.5 44.9 %collective-permute-start.12 = (bf16[2,3,160,256]{3,2,1,0:T(8,128)(2,1)}, bf16[2,3,160,256]{3,2,1,0:T(8,128)(2,1)}, u32[]{:S(2)}, u32[]{:S(2)}) collective-permute-start(bf16[2,3,160,256]{3,2,1,0:T(8,128)(2,1)} %get-tuple-element.104), channel_id=1, source_target_pairs={{0,1},{1,2},{2,3},{3,4},{4,5},{5,6},{6,7},{8,9},{9,10},{10,11},{11... | collective-permute-start | bytes 1474568 | tf_op jit(solution)/shard_map/ppermute | solution.py:941
  829.9 42.9 %collective-permute-start.13 = (bf16[2,3,160,256]{3,2,1,0:T(8,128)(2,1)}, bf16[2,3,160,256]{3,2,1,0:T(8,128)(2,1)}, u32[]{:S(2)}, u32[]{:S(2)}) collective-permute-start(bf16[2,3,160,256]{3,2,1,0:T(8,128)(2,1)} %get-tuple-element.103), channel_id=1, source_target_pairs={{1,0},{2,1},{3,2},{4,3},{5,4},{6,5},{7,6},{9,8},{10,9},{11,10},{12... | collective-permute-start | bytes 1474568 | tf_op jit(solution)/shard_map/ppermute | solution.py:942
  855.0 43.3 %collective-permute-start.17 = (bf16[28,32,1024]{2,1,0:T(8,128)(2,1)}, bf16[28,32,1024]{2,1,0:T(8,128)(2,1)}, u32[]{:S(2)}, u32[]{:S(2)}) collective-permute-start(bf16[28,32,1024]{2,1,0:T(8,128)(2,1)} %sum_blocks.26.after_ref), channel_id=1, source_target_pairs={{0,1},{1,0},{2,3},{3,2},{4,5},{5,4},{6,7},{7,6},{8,9},{9,8},{10,11... | collective-permute-start | bytes 5505032 | tf_op jit(solution)/shard_map/ppermute | solution.py:488
  861.1 157.3 %collective-permute-start.20 = (bf16[40,32,1024]{2,1,0:T(8,128)(2,1)}, bf16[40,32,1024]{2,1,0:T(8,128)(2,1)}, u32[]{:S(2)}, u32[]{:S(2)}) collective-permute-start(bf16[40,32,1024]{2,1,0:T(8,128)(2,1)} %sum_blocks.27.after_ref), channel_id=1, source_target_pairs={{0,2},{1,3},{2,0},{3,1},{4,6},{5,7},{6,4},{7,5},{8,10},{9,11},{10,... | collective-permute-start | bytes 7864328 | tf_op jit(solution)/shard_map/ppermute | solution.py:488
  866.5 156.5 %collective-permute-start.19 = (bf16[40,32,1024]{2,1,0:T(8,128)(2,1)}, bf16[40,32,1024]{2,1,0:T(8,128)(2,1)}, u32[]{:S(2)}, u32[]{:S(2)}) collective-permute-start(bf16[40,32,1024]{2,1,0:T(8,128)(2,1)} %sum_blocks.28.refs_3_), channel_id=1, source_target_pairs={{0,1},{1,0},{2,3},{3,2},{4,5},{5,4},{6,7},{7,6},{8,9},{9,8},{10,11... | collective-permute-start | bytes 7864328 | tf_op jit(solution)/shard_map/ppermute | solution.py:488
  871.4 6.3 copy-start.13
  871.4 162.6 %collective-permute-start.18 = (bf16[24,32,1024]{2,1,0:T(8,128)(2,1)}, bf16[24,32,1024]{2,1,0:T(8,128)(2,1)}, u32[]{:S(2)}, u32[]{:S(2)}) collective-permute-start(bf16[24,32,1024]{2,1,0:T(8,128)(2,1)} %sum_blocks.29.refs_4_), channel_id=1, source_target_pairs={{0,4},{1,5},{2,6},{3,7},{4,0},{5,1},{6,2},{7,3},{8,12},{9,13},{10,... | collective-permute-start | bytes 4718600 | tf_op jit(solution)/shard_map/ppermute | solution.py:488
  872.8 165.9 %collective-permute-start.25 = (bf16[14,32,1024]{2,1,0:T(8,128)(2,1)}, bf16[14,32,1024]{2,1,0:T(8,128)(2,1)}, u32[]{:S(2)}, u32[]{:S(2)}) collective-permute-start(bf16[14,32,1024]{2,1,0:T(8,128)(2,1)} %sum_blocks.30.after_ref), channel_id=1, source_target_pairs={{0,1},{1,0},{2,3},{3,2},{4,5},{5,4},{6,7},{7,6},{8,9},{9,8},{10,11... | collective-permute-start | bytes 2752520 | tf_op jit(solution)/shard_map/ppermute | solution.py:488
  894.5 8.9 copy-start.43
  901.7 139.6 %collective-permute-start.24 = (bf16[14,32,1024]{2,1,0:T(8,128)(2,1)}, bf16[14,32,1024]{2,1,0:T(8,128)(2,1)S(1)}, u32[]{:S(2)}, u32[]{:S(2)}) collective-permute-start(bf16[14,32,1024]{2,1,0:T(8,128)(2,1)} %sum_blocks.31.refs_4_), channel_id=1, source_target_pairs={{0,2},{1,3},{2,0},{3,1},{4,6},{5,7},{6,4},{7,5},{8,10},{9,11},{10,... | collective-permute-start | bytes 2752520 | tf_op jit(solution)/shard_map/ppermute | solution.py:488
  1022.0 31.3 %collective-permute-start.23 = (bf16[20,32,1024]{2,1,0:T(8,128)(2,1)}, bf16[20,32,1024]{2,1,0:T(8,128)(2,1)S(1)}, u32[]{:S(2)}, u32[]{:S(2)}) collective-permute-start(bf16[20,32,1024]{2,1,0:T(8,128)(2,1)} %sum_blocks.32.refs_4_), channel_id=1, source_target_pairs={{0,16},{8,24},{16,0},{24,8},{1,17},{9,25},{17,1},{25,9},{2,18},{10... | collective-permute-start | bytes 3932168 | tf_op jit(solution)/shard_map/ppermute | solution.py:488
  1023.0 5.0 copy-start.14
  1026.8 32.2 %collective-permute-start.22 = (bf16[20,32,1024]{2,1,0:T(8,128)(2,1)}, bf16[20,32,1024]{2,1,0:T(8,128)(2,1)S(1)}, u32[]{:S(2)}, u32[]{:S(2)}) collective-permute-start(bf16[20,32,1024]{2,1,0:T(8,128)(2,1)} %sum_blocks.33.refs_4_), channel_id=1, source_target_pairs={{0,2},{1,3},{2,0},{3,1},{4,6},{5,7},{6,4},{7,5},{8,10},{9,11},{10,... | collective-permute-start | bytes 3932168 | tf_op jit(solution)/shard_map/ppermute | solution.py:488
  1037.1 33.5 %collective-permute-start.21 = (bf16[12,32,1024]{2,1,0:T(8,128)(2,1)}, bf16[12,32,1024]{2,1,0:T(8,128)(2,1)}, u32[]{:S(2)}, u32[]{:S(2)}) collective-permute-start(bf16[12,32,1024]{2,1,0:T(8,128)(2,1)} %sum_blocks.34.refs_5_), channel_id=1, source_target_pairs={{0,1},{1,0},{2,3},{3,2},{4,5},{5,4},{6,7},{7,6},{8,9},{9,8},{10,11... | collective-permute-start | bytes 2359304 | tf_op jit(solution)/shard_map/ppermute | solution.py:488
  1057.4 85.9 %collective-permute-start.28 = (bf16[10,32,1024]{2,1,0:T(8,128)(2,1)}, bf16[10,32,1024]{2,1,0:T(8,128)(2,1)}, u32[]{:S(2)}, u32[]{:S(2)}) collective-permute-start(bf16[10,32,1024]{2,1,0:T(8,128)(2,1)} %sum_blocks.37.refs_5_), channel_id=1, source_target_pairs={{0,4},{1,5},{2,6},{3,7},{4,0},{5,1},{6,2},{7,3},{8,12},{9,13},{10,... | collective-permute-start | bytes 1966088 | tf_op jit(solution)/shard_map/ppermute | solution.py:488
  1063.2 88.9 %collective-permute-start.27 = (bf16[10,32,1024]{2,1,0:T(8,128)(2,1)}, bf16[10,32,1024]{2,1,0:T(8,128)(2,1)}, u32[]{:S(2)}, u32[]{:S(2)}) collective-permute-start(bf16[10,32,1024]{2,1,0:T(8,128)(2,1)} %sum_blocks.38.refs_5_), channel_id=1, source_target_pairs={{0,4},{1,5},{2,6},{3,7},{4,0},{5,1},{6,2},{7,3},{8,12},{9,13},{10,... | collective-permute-start | bytes 1966088 | tf_op jit(solution)/shard_map/ppermute | solution.py:488
  1065.9 13.8 %collective-permute-start.30 = (bf16[7,32,1024]{2,1,0:T(8,128)(2,1)}, bf16[7,32,1024]{2,1,0:T(8,128)(2,1)}, u32[]{:S(2)}, u32[]{:S(2)}) collective-permute-start(bf16[7,32,1024]{2,1,0:T(8,128)(2,1)} %sum_blocks.35.refs_5_), channel_id=1, source_target_pairs={{0,16},{8,24},{16,0},{24,8},{1,17},{9,25},{17,1},{25,9},{2,18},{10... | collective-permute-start | bytes 1376264 | tf_op jit(solution)/shard_map/ppermute | solution.py:488
  1067.0 69.7 %collective-permute-start.29 = (bf16[7,32,1024]{2,1,0:T(8,128)(2,1)S(1)}, bf16[7,32,1024]{2,1,0:T(8,128)(2,1)}, u32[]{:S(2)}, u32[]{:S(2)}) collective-permute-start(bf16[7,32,1024]{2,1,0:T(8,128)(2,1)S(1)} %copy-done.36), channel_id=1, source_target_pairs={{0,4},{1,5},{2,6},{3,7},{4,0},{5,1},{6,2},{7,3},{8,12},{9,13},{10,... | collective-permute-start | bytes 1376264 | tf_op jit(solution)/shard_map/ppermute | solution.py:488
  1073.3 87.5 %collective-permute-start.26 = (bf16[6,32,1024]{2,1,0:T(8,128)(2,1)}, bf16[6,32,1024]{2,1,0:T(8,128)(2,1)S(1)}, u32[]{:S(2)}, u32[]{:S(2)}) collective-permute-start(bf16[6,32,1024]{2,1,0:T(8,128)(2,1)} %sum_blocks.39), channel_id=1, source_target_pairs={{0,16},{8,24},{16,0},{24,8},{1,17},{9,25},{17,1},{25,9},{2,18},{10... | collective-permute-start | bytes 1179656 | tf_op jit(solution)/shard_map/ppermute | solution.py:488
  (77 other events, 193.7 us)
Sparse Core Ops, SparseCore 0:
  11.9 446.2 all-gather.1

commit v4 on v3

--- a/solution.py
+++ b/solution.py
@@ -1,3 +1,5 @@
+import math
+
 import jax
 import jax.numpy as jnp
 from jax import lax
@@ -458,10 +460,9 @@
     return list(range(count.bit_length() - 1))
 
 
-PARTS = ((7, "zwxy"), (7, "yxzw"), (10, "xzyw"), (10, "yxzw"), (6, "zwxy"))
+PARTS = ((6, "zwxy"), (8, "yxzw"), (10, "xzyw"), (10, "yxzw"), (6, "zwxy"))
 TURNS_AT = {0: 5, 5: 7, 7: 3, 8: 6}
-EDGES_AT = 11
-REST_AT = 12
+EDGES_AT = 12
 
 
 def part_orders(n_img, n_tile):
@@ -486,6 +487,151 @@
 def swap(values, axis, bit):
     count = lax.axis_size(axis)
     return lax.ppermute(values, axis, [(i, i ^ (1 << bit)) for i in range(count)])
+
+
+GATHER_FIRST = 12
+STREAMS = ((11, "wzyx"), (10, "wzxy"), (7, "xywz"))
+
+
+def gather_plan(slots, n_img, n_tile):
+    if n_img * n_tile > 64:
+        return slots, []
+    first = GATHER_FIRST * slots // 40
+    bits = {
+        "x": [("tile", b) for b in bits_of(n_tile)[:1]],
+        "y": [("img", b) for b in bits_of(n_img)[1:]],
+        "z": [("tile", b) for b in bits_of(n_tile)[1:2]],
+        "w": [("tile", b) for b in bits_of(n_tile)[2:]],
+    }
+    total = sum(share for share, _ in STREAMS)
+    streams, done, start = [], 0, first
+    for share, order in STREAMS:
+        done += share
+        end = first + ((slots - first) * done + total // 2) // total
+        places = [place for letter in order for place in bits[letter]] + [("img", 0)]
+        if end > start:
+            streams.append((start, end - start, places))
+        start = end
+    return first, streams
+
+
+def gather_blocks(own, gathered, first, streams, n_img, n_tile, after):
+    slots, block_rows, hidden = own.shape
+    devices = n_img * n_tile
+    stages = len(streams[0][2])
+    pieces = devices - 1
+
+    def body(own_ref, part_ref, after_ref, out_ref, held, send, recv, local, taken, given):
+        del after_ref
+        place = {"img": lax.axis_index("img"), "tile": lax.axis_index("tile")}
+
+        def partner(axis, step):
+            here = place[axis]
+            there = dict(place)
+            there[axis] = here + step - 2 * step * ((here // step) % 2)
+            return (there["img"], there["tile"])
+
+        barrier = pltpu.get_barrier_semaphore()
+        for axis, bit in streams[0][2]:
+            pl.semaphore_signal(
+                barrier,
+                inc=1,
+                device_id=partner(axis, 1 << bit),
+                device_id_type=pl.DeviceIdType.MESH,
+            )
+        pl.semaphore_wait(barrier, stages)
+        copies = {}
+
+        def send_piece(s, k, p):
+            start, share, places = streams[s]
+            base = start * devices
+            source = (
+                own_ref.at[pl.ds(start, share)]
+                if p == 0
+                else out_ref.at[pl.ds(base + p * share, share)]
+            )
+            q = (1 << k) + p
+            axis, bit = places[k]
+            copy = pltpu.make_async_remote_copy(
+                src_ref=source,
+                dst_ref=out_ref.at[pl.ds(base + q * share, share)],
+                send_sem=send.at[s, q - 1],
+                recv_sem=recv.at[s, q - 1],
+                device_id=partner(axis, 1 << bit),
+                device_id_type=pl.DeviceIdType.MESH,
+            )
+            copy.start()
+            copies[s, q] = copy
+
+        for k in range(stages):
+            for s in range(len(streams)):
+                send_piece(s, k, 0)
+        moves = []
+        for s, (start, share, _) in enumerate(streams):
+            moves.append(
+                pltpu.make_async_copy(
+                    own_ref.at[pl.ds(start, share)],
+                    out_ref.at[pl.ds(start * devices, share)],
+                    local.at[s],
+                )
+            )
+        for move in moves:
+            move.start()
+
+        def chunk(ref, c):
+            return ref.at[pl.ds(c * devices, devices)]
+
+        depth = held.shape[0]
+        take = [
+            pltpu.make_async_copy(chunk(part_ref, c), held.at[c % depth], taken.at[c % depth])
+            for c in range(first)
+        ]
+        give = [
+            pltpu.make_async_copy(held.at[c % depth], chunk(out_ref, c), given.at[c % depth])
+            for c in range(first)
+        ]
+        for c in range(min(depth, first)):
+            take[c].start()
+        for c in range(first):
+            take[c].wait()
+            give[c].start()
+            if c >= 2 and c - 2 + depth < first:
+                give[c - 2].wait()
+                take[c - 2 + depth].start()
+        for c in range(first):
+            if c + depth >= first:
+                give[c].wait()
+
+        for q in range(1, devices):
+            for s in range(len(streams)):
+                copies[s, q].wait_recv()
+                for k in range(q.bit_length(), stages):
+                    send_piece(s, k, q)
+        for q in range(1, devices):
+            for s in range(len(streams)):
+                copies[s, q].wait_send()
+        for move in moves:
+            move.wait()
+
+    anywhere = pl.BlockSpec(memory_space=pl.ANY)
+    return pl.pallas_call(
+        body,
+        in_specs=[anywhere] * 3,
+        out_specs=anywhere,
+        out_shape=jax.ShapeDtypeStruct((slots * devices, block_rows, hidden), jnp.bfloat16),
+        scratch_shapes=[
+            pltpu.VMEM((4, devices, block_rows, hidden), jnp.bfloat16),
+            pltpu.SemaphoreType.DMA((len(streams), pieces)),
+            pltpu.SemaphoreType.DMA((len(streams), pieces)),
+            pltpu.SemaphoreType.DMA((len(streams),)),
+            pltpu.SemaphoreType.DMA((4,)),
+            pltpu.SemaphoreType.DMA((4,)),
+        ],
+        compiler_params=pltpu.CompilerParams(
+            collective_id=1, has_side_effects=True, vmem_limit_bytes=VMEM_LIMIT
+        ),
+        name="gather_blocks",
+    )(own, gathered, after)
 
 
 def sum_parts(kept, sent, orders, events):
@@ -498,6 +644,7 @@
         half = terms[i][-1].shape[0] // 2
         last = sum_blocks(terms[i], half, last)
         terms[i].append(swap(last, *orders[i][stage]))
+    events["end"](last)
     return terms
 
 
@@ -708,6 +855,7 @@
 def finish_blocks(terms, start, share, masters, firsts, seconds, held, scale, old):
     slots, block_rows, hidden = masters.shape
     count = len(terms)
+    batch = math.gcd(math.gcd(start, share), 2)
     correct_one = 1.0 - BETA_ONE ** float(STEP)
     correct_two = 1.0 - BETA_TWO ** float(STEP)
 
@@ -718,8 +866,12 @@
             total = value if total is None else total + value
         w_ref, m_ref, v_ref = refs[count : count + 3]
         outs = refs[-3:]
-        mine = held_ref[start + pl.program_id(0)] >= 0
-        grad = jnp.where(mine, total * scale_ref[0], 0.0)
+        place = start + pl.program_id(0) * batch
+        total = total * scale_ref[0]
+        grad = jnp.concatenate(
+            [jnp.where(held_ref[place + i] >= 0, total[i : i + 1], 0.0) for i in range(batch)],
+            axis=0,
+        )
         first_new = BETA_ONE * m_ref[...] + (1.0 - BETA_ONE) * grad
         second_new = BETA_TWO * v_ref[...] + (1.0 - BETA_TWO) * grad * grad
         rooted = jnp.sqrt(second_new * (1.0 / correct_two)) + EPSILON
@@ -729,14 +881,14 @@
         outs[1][...] = first_new
         outs[2][...] = second_new
 
-    term = pl.BlockSpec((1, block_rows, hidden), lambda i: (i, 0, 0))
-    slot = pl.BlockSpec((1, block_rows, hidden), lambda i: (start + i, 0, 0))
+    term = pl.BlockSpec((batch, block_rows, hidden), lambda i: (i, 0, 0))
+    slot = pl.BlockSpec((batch, block_rows, hidden), lambda i: (start // batch + i, 0, 0))
     smem = pl.BlockSpec(memory_space=pltpu.SMEM)
     kept = [] if old is None else list(old)
     inputs = [held, scale] + list(terms) + [masters, firsts, seconds] + kept
     return pl.pallas_call(
         body,
-        grid=(share,),
+        grid=(share // batch,),
         in_specs=[smem, smem]
         + [term] * count
         + [slot] * 3
@@ -786,7 +938,9 @@
     n_img, n_tile = lax.axis_size("img"), lax.axis_size("tile")
     at_img, at_tile = lax.axis_index("img"), lax.axis_index("tile")
 
-    gathered = lax.all_gather(block_master.astype(jnp.bfloat16), AXES, axis=0, tiled=True)
+    own_blocks = block_master.astype(jnp.bfloat16)
+    go_first, streams = gather_plan(slots, n_img, n_tile)
+    gathered = lax.all_gather(own_blocks[:go_first], AXES, axis=0, tiled=True)
     position = jnp.arange(all_slots, dtype=jnp.int32)
     owner_slot = (
         jnp.zeros((block_total,), jnp.int32)
@@ -797,9 +951,18 @@
     orders = part_orders(n_img, n_tile)
     shares = part_sizes(slots)
     groups = n_img * n_tile // 2
+    row_of = (owner_slot // slots) * go_first + owner_slot % slots
     owner = owner_slot // slots
     within = owner_slot % slots
     relative = {"img": (owner // n_tile) ^ at_img, "tile": (owner % n_tile) ^ at_tile}
+    for begin, share, places in streams:
+        rank = jnp.zeros((block_total,), jnp.int32)
+        for k, (axis, bit) in enumerate(places):
+            rank = rank + (((relative[axis] >> bit) & 1) << k)
+        inside = (within >= begin) & (within < begin + share)
+        row_of = jnp.where(
+            inside, begin * n_img * n_tile + rank * share + within - begin, row_of
+        )
     kind = jnp.zeros((block_total,), jnp.int32)
     place = jnp.zeros((block_total,), jnp.int32)
     start = 0
@@ -848,7 +1011,9 @@
     fracs_row = corner_frac[:, 0]
     fracs_col = corner_frac[:, 1]
     feats_t = pool_regions(map_t, sample_rows, sample_cols, fracs_row, fracs_col, breadth)
-    first_pres = first_layer(owner_slot, gathered, feats_t, section_blocks)
+    if streams:
+        gathered = gather_blocks(own_blocks, gathered, go_first, streams, n_img, n_tile, feats_t)
+    first_pres = first_layer(row_of, gathered, feats_t, section_blocks)
 
     loss_part = jnp.zeros((), jnp.float32)
     head_grads = []
@@ -856,7 +1021,7 @@
     acts_t, grads_first, grads_second = [], [], []
     for section in range(section_count):
         second_slots = lax.slice_in_dim(
-            owner_slot, section * section_blocks + first_blocks, (section + 1) * section_blocks
+            row_of, section * section_blocks + first_blocks, (section + 1) * section_blocks
         )
         second_matrix = gathered[second_slots].reshape(hidden, hidden)
         head_low = head_all[section]
@@ -926,7 +1091,7 @@
     def turns_of(start, stop):
         def work(after):
             found["map"] = map_grads(
-                found["map"], (start, stop), owner_slot, gathered, grads_first, sample_rows,
+                found["map"], (start, stop), row_of, gathered, grads_first, sample_rows,
                 sample_cols, fracs_row, fracs_col, section_blocks, lines, breadth, after,
             )
             return found["map"]
@@ -976,7 +1141,7 @@
         events[at] = turns_of(start, start + count)
         start += count
     events[EDGES_AT] = edges
-    events[REST_AT] = rest
+    events["end"] = rest
     block_terms = sum_parts(parts[0::2], parts[1::2], orders, events)
 
     conv_sum = jnp.concatenate(found["sums"][:2], axis=0)

time: 1190 us -> 1140 us (0.958)
  waiting for transfers between devices: 390 us -> 137 us
  Pallas kernels: 572 us -> 761 us
    all_gather x1, waiting for transfers between devices: 281 us -> 0.01 us  [on_device(): gathered = lax.all_gather(own_blocks[:go_first], AXES, axis=0, tiled=True)]
    pallas_call x5 -> x6, Pallas kernels: 36.5 us -> 256 us  [the longest x1 226 us: gather_blocks(): pl.pallas_call(body, in_specs=[anywhere] * 3, out_specs=anywhere, out_sha...]
    pallas_call x1, Pallas kernels: 102 us -> 70.3 us  [sum_everywhere(): pl.pallas_call(body, in_specs=[whole] * number + [pl.BlockSpec(memory_spa...]
    ppermute x25, waiting for transfers between devices: 99.9 us -> 118 us  [swap(): return lax.ppermute(values, axis, [(i, i ^ 1 << bit) for i in range(count)])]
    ppermute x2, waiting for transfers between devices: 4.84 us -> 18.7 us  [padded_2(): lax.ppermute(tail, axis, [(i, (i + 1) % count) for i in range(ends)])]
  transfers between devices with their start and end apart: 32 -> 32, of which waited for: 11 -> 9; matrix products, arithmetic and copies ran while one was open for 7% -> 9% of each run, Pallas kernels for 41% -> 39%
where the time goes in v4:
time: 1140 us; the launch traced here: 1120 us
  Pallas kernels  761 us (67%)
  waiting for transfers between devices  137 us (12%)
  local copies, waits for them, and re-layouts  61.1 us (5%)
  matrix products  58.9 us (5%)
  starting transfers between devices  44 us (4%)
  other arithmetic  43.1 us (4%)
  between operations  20.1 us (2%)
    pallas_call x1, Pallas kernels, gather_blocks(): pl.pallas_call(body, in_specs=[anywhere] * 3, out_specs=anywhere, out_sha...  226 us
    pallas_call x4, Pallas kernels, map_grads(): pl.pallas_call(body, grid_spec=pltpu.PrefetchScalarGridSpec(num_scalar_pr...  148 us
    ppermute x25, waiting for transfers between devices, swap(): return lax.ppermute(values, axis, [(i, i ^ 1 << bit) for i in range(count)])  118 us
    pallas_call x1, Pallas kernels, pool_regions(): pl.pallas_call(body, grid=(section_count, bins // group), in_specs=[pl.Bl...  109 us
    pallas_call x20, Pallas kernels, sum_blocks(): pl.pallas_call(body, grid=(half // batch,), in_specs=[pl.BlockSpec((batch...  86.8 us
    pallas_call x1, Pallas kernels, sum_everywhere(): pl.pallas_call(body, in_specs=[whole] * number + [pl.BlockSpec(memory_spa...  70.3 us
    pallas_call x1, Pallas kernels, weight_grads(): pl.pallas_call(body, grid_spec=pltpu.PrefetchScalarGridSpec(num_scalar_pr...  46.6 us
    pallas_call x1, Pallas kernels, first_layer(): pl.pallas_call(body, grid_spec=pltpu.PrefetchScalarGridSpec(num_scalar_pr...  40.8 us
  transfers between devices with their start and end apart: 32, of which 9 were waited for; matrix products, arithmetic and copies ran while one was open for 9% of the time, Pallas kernels for 39%

profile of v4, /device:TPU:0, one launch (start us, length us, event | category | flops | bytes accessed | tf_op | source)
XLA Modules:
  0.0 1124.9 jit_solution(15902046778141811582)
XLA Ops:
  7.2 3.0 convert_element_type.135.own_ref
  16.6 4.8 collective-permute-start
  22.8 5.2 scatter_custom_fusion
  33.1 3.0 fusion.138
  38.1 5.2 sort.31
  52.4 4.6 collective-permute-start.2
  59.8 18.7 %collective-permute-done.2 = bf16[2,2,160,256]{3,2,1,0:T(8,128)(2,1)S(1)} collective-permute-done((bf16[2,2,160,256]{3,2,1,0:T(8,128)(2,1)S(1)}, bf16[2,2,160,256]{3,2,1,0:T(8,128)(2,1)S(1)}, u32[]{:S(2)}, u32[]{:S(2)}) %collective-permute-start.2) | collective-permute-done | bytes 327712 | tf_op jit(solution)/shard_map/ppermute | solution.py:33
  81.0 108.7 %pool_regions.1.after_ref.x_ref = bf16[3,49,256,256]{3,2,1,0:T(8,128)(2,1)} custom-call(bf16[256,3840]{1,0:T(8,128)(2,1)} %bitcast.298, s32[3,49,256]{2,1,0:T(8,128)} %get-tuple-element.120.row_ref, s32[3,49,256]{2,1,0:T(8,128)} %get-tuple-element.119.col_ref, f32[3,49,256]{2,1,0:T(8,128)} %get-tuple-element.176.fr_ref, f32[3,49,256]{2,1,0:T(8,128)} %get-tuple-element.175.fc_ref), custom_call_target="tpu_custom_call" | custom-call | flops 73987522560 | bytes 19267584 | tf_op jit(solution)/shard_map/pool_regions/pallas_call | solution.py:138
  189.7 226.4 %gather_blocks.1.blocks_ref = bf16[1280,32,1024]{2,1,0:T(8,128)(2,1)} custom-call(bf16[40,32,1024]{2,1,0:T(8,128)(2,1)} %copy-done.13, bf16[384,32,1024]{2,1,0:T(8,128)(2,1)} %all-gather.2.cloned.1.call-done.part_ref, bf16[3,49,256,256]{3,2,1,0:T(8,128)(2,1)} %pool_regions.1.after_ref.x_ref), custom_call_target="tpu_custom_call" | custom-call | tf_op jit(solution)/shard_map/gather_blocks/pallas_call | solution.py:617
  416.1 40.8 %first_layer.1 = f32[3,256,1024]{2,1,0:T(8,128)} custom-call(s32[1272]{0:T(1024)} %copy-done.61, bf16[1280,32,1024]{2,1,0:T(8,128)(2,1)} %gather_blocks.1.blocks_ref, bf16[3,49,256,256]{3,2,1,0:T(8,128)(2,1)} %pool_regions.1.after_ref.x_ref), custom_call_target="tpu_custom_call" | custom-call | flops 19730006016 | bytes 96337920 | tf_op jit(solution)/shard_map/first_layer/pallas_call | solution.py:204
  456.9 3.7 gather_fusion.2
  460.6 3.7 multiply_convert_fusion.3
  466.1 3.8 gather_fusion.1
  469.9 3.7 multiply_convert_fusion.5
  476.0 3.8 gather_fusion
  479.8 2.8 fusion.128
  482.7 3.0 multiply_convert_fusion.7
  492.1 2.5 convert_reduce_fusion.7
  505.6 46.6 %weight_grads.1 = (bf16[96,32,1024]{2,1,0:T(8,128)(2,1)}, bf16[96,32,1024]{2,1,0:T(8,128)(2,1)}, bf16[128,32,1024]{2,1,0:T(8,128)(2,1)}, bf16[128,32,1024]{2,1,0...) custom-call(s32[1272]{0:T(1024)} %get-tuple-element.45.order_ref, ...), custom_call_target="tpu_custom_call" | custom-call | flops 21340618752 | bytes 104202240 | tf_op jit(solution)/shard_map/weight_grads/pallas_call | solution.py:293
  555.9 35.4 %map_grads.4.refs_2_.old_ref = f32[3840,256]{1,0:T(8,128)} custom-call(s32[1272]{0:T(1024)} %copy-done.61, bf16[1280,32,1024]{2,1,0:T(8,128)(2,1)} %gather_blocks.1.blocks_ref, bf16[3,256,1024]{2,1,0:T(8,128)(2,1)} %pad_maximum_fusion.1.gf_ref.g_ref, s32[3,49,256]{2,1,0:T(8,128)} %get-tuple-element.120.row_ref, s32[3,49,256]{2,1,0:T(8,128)} %get-tuple-element.119.col_ref, ...), custom_call_target="tpu_custom_call" | custom-call | flops 22313697280 | bytes 18350080 | tf_op jit(solution)/shard_map/map_grads/pallas_call | solution.py:395
  591.3 2.6 copy-done.5
  594.0 5.4 sum_blocks.20.refs_2_
  599.4 5.4 collective-permute-done.7.refs_1_
  604.8 6.0 sum_blocks.21.refs_2_
  612.2 8.2 sum_blocks.22.refs_2_
  623.6 4.0 fusion.214
  629.3 8.0 sum_blocks.23.refs_2_
  638.1 5.4 sum_blocks.24.after_ref
  643.5 47.2 %map_grads.5.refs_3_.old_ref = f32[3840,256]{1,0:T(8,128)} custom-call(s32[1272]{0:T(1024)} %copy-done.61, bf16[1280,32,1024]{2,1,0:T(8,128)(2,1)} %gather_blocks.1.blocks_ref, bf16[3,256,1024]{2,1,0:T(8,128)(2,1)} %pad_maximum_fusion.1.gf_ref.g_ref, s32[3,49,256]{2,1,0:T(8,128)} %get-tuple-element.120.row_ref, s32[3,49,256]{2,1,0:T(8,128)} %get-tuple-element.119.col_ref, ...), custom_call_target="tpu_custom_call" | custom-call | flops 31239176192 | bytes 25690112 | tf_op jit(solution)/shard_map/map_grads/pallas_call | solution.py:395
  695.8 3.5 sum_blocks.25.refs_3_
  701.0 3.5 collective-permute-done.9.refs_2_
  704.5 4.1 sum_blocks.26.after_ref
  710.7 23.8 %map_grads.6.refs_3_.old_ref = f32[3840,256]{1,0:T(8,128)} custom-call(s32[1272]{0:T(1024)} %copy-done.61, bf16[1280,32,1024]{2,1,0:T(8,128)(2,1)} %gather_blocks.1.blocks_ref, bf16[3,256,1024]{2,1,0:T(8,128)(2,1)} %pad_maximum_fusion.1.gf_ref.g_ref, s32[3,49,256]{2,1,0:T(8,128)} %get-tuple-element.120.row_ref, s32[3,49,256]{2,1,0:T(8,128)} %get-tuple-element.119.col_ref, ...), custom_call_target="tpu_custom_call" | custom-call | flops 13388218368 | bytes 11010048 | tf_op jit(solution)/shard_map/map_grads/pallas_call | solution.py:395
  736.5 5.5 sum_blocks.27.after_ref
  742.0 41.2 %map_grads.7.refs_3_.own_ref = f32[3840,256]{1,0:T(8,128)} custom-call(s32[1272]{0:T(1024)} %copy-done.61, bf16[1280,32,1024]{2,1,0:T(8,128)(2,1)} %gather_blocks.1.blocks_ref, bf16[3,256,1024]{2,1,0:T(8,128)(2,1)} %pad_maximum_fusion.1.gf_ref.g_ref, s32[3,49,256]{2,1,0:T(8,128)} %get-tuple-element.120.row_ref, s32[3,49,256]{2,1,0:T(8,128)} %get-tuple-element.119.col_ref, ...), custom_call_target="tpu_custom_call" | custom-call | flops 26776436736 | bytes 22020096 | tf_op jit(solution)/shard_map/map_grads/pallas_call | solution.py:395
  786.5 4.7 collective-permute-start.12
  791.2 25.1 %collective-permute-done.17.refs_2_ = bf16[80,32,1024]{2,1,0:T(8,128)(2,1)} collective-permute-done((bf16[80,32,1024]{2,1,0:T(8,128)(2,1)}, bf16[80,32,1024]{2,1,0:T(8,128)(2,1)}, u32[]{:S(2)}, u32[]{:S(2)}) %collective-permute-start.17) | collective-permute-done | bytes 5242912 | tf_op jit(solution)/shard_map/ppermute | solution.py:489
  819.5 2.9 copy.160
  824.5 5.7 sum_blocks.28.refs_3_
  830.2 4.1 collective-permute-start.20
  834.3 3.5 sum_blocks.29.refs_4_
  839.1 3.1 sum_blocks.30.refs_4_
  842.9 3.6 sum_blocks.31.after_ref
  847.7 3.7 edge_rows.1.refs_4_
  869.5 5.2 convert_reduce_fusion.1
  874.8 51.2 %collective-permute-done.20.refs_3_ = bf16[40,32,1024]{2,1,0:T(8,128)(2,1)S(1)} collective-permute-done((bf16[40,32,1024]{2,1,0:T(8,128)(2,1)}, bf16[40,32,1024]{2,1,0:T(8,128)(2,1)S(1)}, u32[]{:S(2)}, u32[]{:S(2)}) %collective-permute-start.20) | collective-permute-done | bytes 2621472 | tf_op jit(solution)/shard_map/ppermute | solution.py:489
  927.5 3.6 sum_blocks.32.refs_4_
  934.0 3.9 sum_blocks.33.refs_4_
  940.7 3.1 sum_blocks.34.refs_5_
  946.1 2.7 fusion.106
  953.2 2.8 sum_blocks.36.refs_5_
  956.0 3.3 collective-permute-start.29
  959.3 4.0 collective-permute-done.23.refs_4_
  963.3 3.1 sum_blocks.37.refs_5_
  966.4 25.4 %collective-permute-done.22.refs_4_ = bf16[20,32,1024]{2,1,0:T(8,128)(2,1)} collective-permute-done((bf16[20,32,1024]{2,1,0:T(8,128)(2,1)}, bf16[20,32,1024]{2,1,0:T(8,128)(2,1)}, u32[]{:S(2)}, u32[]{:S(2)}) %collective-permute-start.22) | collective-permute-done | bytes 1310752 | tf_op jit(solution)/shard_map/ppermute | solution.py:489
  991.8 3.1 sum_blocks.38.refs_5_
  995.9 2.6 sum_blocks.39.refs_4_
  1000.0 70.3 %sum_everywhere.1 = (bf16[8192,128]{1,0:T(8,128)(2,1)}, f32[256,128]{1,0:T(8,128)}) custom-call(f32[256,256]{1,0:T(8,128)} %fusion.56.refs_0_, f32[2304,256]{1,0:T(8,128)} %fusion.112.refs_1_, f32[3072,85]{1,0:T(8,128)} %bitcast.290, f32[56,128]{1,0:T(8,128)} %pad_bitcast_fusion.refs_3_, bf16[6,32,1024]{2,1,0:T(8,128)(2,1)} %sum_blocks.39.refs_4_), custom_call_target="tpu_custom_call" | custom-call | tf_op jit(solution)/shard_map/sum_everywhere/pallas_call | solution.py:790
  1074.7 4.3 multiply_subtract_fusion
  1082.4 4.9 finish_blocks.5
  1087.4 5.9 finish_blocks.6
  1096.4 7.2 finish_blocks.7
  1104.4 7.2 finish_blocks.8
  1111.6 4.9 finish_blocks.9
  (370 shorter events, 126.2 us)
Async XLA Ops:
  7.2 8.0 copy-start
  7.2 182.5 %all-gather.2.cloned.1.call-start = ((), (), s32[]{:S(2)}) async-start(), calls=%async_computation | async-start | bytes 25952256 | tf_op jit(solution)/shard_map/all_gather | solution.py:943
  15.2 7.5 copy-start.92
  15.2 13.4 %copy-start.107 = (s32[256]{0:T(256)S(1)}, s32[256]{0:T(256)}, u32[]{:S(2)}) copy-start(s32[256]{0:T(256)} %param.37) | copy-start | bytes 3076
  15.2 15.3 %copy-start.102 = (s32[3,256]{1,0:T(4,128)S(1)}, s32[3,256]{1,0:T(4,128)}, u32[]{:S(2)}) copy-start(s32[3,256]{1,0:T(4,128)} %param.40) | copy-start | bytes 9220
  15.2 15.4 %copy-start.90 = (s32[256]{0:T(256)S(1)}, s32[256]{0:T(256)}, u32[]{:S(2)}) copy-start(s32[256]{0:T(256)} %param.41) | copy-start | bytes 3076
  15.2 16.7 %copy-start.60 = (s32[3,49,256]{2,1,0:T(8,128)S(1)}, s32[3,49,256]{2,1,0:T(8,128)}, u32[]{:S(2)}) copy-start(s32[3,49,256]{2,1,0:T(8,128)} %param.38) | copy-start | bytes 451588
  15.2 17.6 %copy-start.59 = (f32[3,2,49,256]{3,1,2,0:T(2,128)S(1)}, f32[3,2,49,256]{3,1,2,0:T(2,128)}, u32[]{:S(2)}) copy-start(f32[3,2,49,256]{3,1,2,0:T(2,128)} %param.39) | copy-start | bytes 903172
  15.8 30.4 %copy-start.6 = (bf16[2,8,160,256]{3,2,1,0:T(8,128)(2,1)}, bf16[2,8,160,256]{3,2,1,0:T(8,128)(2,1)S(1)}, u32[]{:S(2)}) copy-start(bf16[2,8,160,256]{3,2,1,0:T(8,128)(2,1)S(1)} %add_convert_fusion.2) | copy-start | bytes 3932164
  16.6 27.5 %collective-permute-start = (bf16[2,1,160,256]{3,2,1,0:T(8,128)(2,1)}, bf16[2,1,160,256]{3,2,1,0:T(8,128)(2,1)S(1)}, u32[]{:S(2)}, u32[]{:S(2)}) collective-permute-start(bf16[2,1,160,256]{3,2,1,0:T(8,128)(2,1)} %get-tuple-element.115), channel_id=1, source_target_pairs={{0,1},{1,2},{2,3},{3,4},{4,5},{5,6},{6,7},{8,9},{9,10},{10,11},{11... | collective-permute-start | bytes 491528 | tf_op jit(solution)/shard_map/ppermute | solution.py:33
  21.4 24.2 %collective-permute-start.1 = (bf16[2,1,160,256]{3,2,1,0:T(8,128)(2,1)}, bf16[2,1,160,256]{3,2,1,0:T(8,128)(2,1)S(1)}, u32[]{:S(2)}, u32[]{:S(2)}) collective-permute-start(bf16[2,1,160,256]{3,2,1,0:T(8,128)(2,1)} %get-tuple-element.116), channel_id=1, source_target_pairs={{1,0},{2,1},{3,2},{4,3},{5,4},{6,5},{7,6},{9,8},{10,9},{11,10},{12... | collective-permute-start | bytes 491528 | tf_op jit(solution)/shard_map/ppermute | solution.py:35
  51.0 7.4 copy-start.103
  52.4 26.1 %collective-permute-start.2 = (bf16[2,2,160,256]{3,2,1,0:T(8,128)(2,1)S(1)}, bf16[2,2,160,256]{3,2,1,0:T(8,128)(2,1)S(1)}, u32[]{:S(2)}, u32[]{:S(2)}) collective-permute-start(bf16[2,2,160,256]{3,2,1,0:T(8,128)(2,1)S(1)} %get-tuple-element.113), channel_id=1, source_target_pairs={{0,1},{1,2},{2,3},{3,4},{4,5},{5,6},{6,7},{8,9},{9,10},{10,11},{11... | collective-permute-start | bytes 983048 | tf_op jit(solution)/shard_map/ppermute | solution.py:33
  56.9 21.5 %collective-permute-start.3 = (bf16[2,2,160,256]{3,2,1,0:T(8,128)(2,1)S(1)}, bf16[2,2,160,256]{3,2,1,0:T(8,128)(2,1)S(1)}, u32[]{:S(2)}, u32[]{:S(2)}) collective-permute-start(bf16[2,2,160,256]{3,2,1,0:T(8,128)(2,1)S(1)} %get-tuple-element.114), channel_id=1, source_target_pairs={{1,0},{2,1},{3,2},{4,3},{5,4},{6,5},{7,6},{9,8},{10,9},{11,10},{12... | collective-permute-start | bytes 983048 | tf_op jit(solution)/shard_map/ppermute | solution.py:35
  489.6 7.0 copy-start.81
  489.6 10.2 copy-start.77
  492.1 7.7 copy-start.53
  552.2 60.0 %collective-permute-start.6 = (bf16[160,32,1024]{2,1,0:T(8,128)(2,1)}, bf16[160,32,1024]{2,1,0:T(8,128)(2,1)}, u32[]{:S(2)}, u32[]{:S(2)}) collective-permute-start(bf16[160,32,1024]{2,1,0:T(8,128)(2,1)} %get-tuple-element.53), channel_id=1, source_target_pairs={{0,8},{8,0},{16,24},{24,16},{1,9},{9,1},{17,25},{25,17},{2,10},{10... | collective-permute-start | bytes 31457288 | tf_op jit(solution)/shard_map/ppermute | solution.py:489
  552.7 76.6 %collective-permute-start.5 = (bf16[160,32,1024]{2,1,0:T(8,128)(2,1)}, bf16[160,32,1024]{2,1,0:T(8,128)(2,1)}, u32[]{:S(2)}, u32[]{:S(2)}) collective-permute-start(bf16[160,32,1024]{2,1,0:T(8,128)(2,1)} %get-tuple-element.51), channel_id=1, source_target_pairs={{0,8},{8,0},{16,24},{24,16},{1,9},{9,1},{17,25},{25,17},{2,10},{10... | collective-permute-start | bytes 31457288 | tf_op jit(solution)/shard_map/ppermute | solution.py:489
  552.8 52.0 %collective-permute-start.7 = (bf16[128,32,1024]{2,1,0:T(8,128)(2,1)}, bf16[128,32,1024]{2,1,0:T(8,128)(2,1)}, u32[]{:S(2)}, u32[]{:S(2)}) collective-permute-start(bf16[128,32,1024]{2,1,0:T(8,128)(2,1)} %get-tuple-element.55), channel_id=1, source_target_pairs={{0,8},{8,0},{16,24},{24,16},{1,9},{9,1},{17,25},{25,17},{2,10},{10... | collective-permute-start | bytes 25165832 | tf_op jit(solution)/shard_map/ppermute | solution.py:489
  553.2 38.1 %collective-permute-start.8 = (bf16[96,32,1024]{2,1,0:T(8,128)(2,1)}, bf16[96,32,1024]{2,1,0:T(8,128)(2,1)S(1)}, u32[]{:S(2)}, u32[]{:S(2)}) collective-permute-start(bf16[96,32,1024]{2,1,0:T(8,128)(2,1)} %get-tuple-element.56), channel_id=1, source_target_pairs={{0,8},{8,0},{16,24},{24,16},{1,9},{9,1},{17,25},{25,17},{2,10},{10... | collective-permute-start | bytes 18874376 | tf_op jit(solution)/shard_map/ppermute | solution.py:489
  553.3 84.8 %collective-permute-start.4 = (bf16[96,32,1024]{2,1,0:T(8,128)(2,1)}, bf16[96,32,1024]{2,1,0:T(8,128)(2,1)}, u32[]{:S(2)}, u32[]{:S(2)}) collective-permute-start(bf16[96,32,1024]{2,1,0:T(8,128)(2,1)} %get-tuple-element.49), channel_id=1, source_target_pairs={{0,8},{8,0},{16,24},{24,16},{1,9},{9,1},{17,25},{25,17},{2,10},{10... | collective-permute-start | bytes 18874376 | tf_op jit(solution)/shard_map/ppermute | solution.py:489
  610.8 93.7 %collective-permute-start.9 = (bf16[64,32,1024]{2,1,0:T(8,128)(2,1)}, bf16[64,32,1024]{2,1,0:T(8,128)(2,1)}, u32[]{:S(2)}, u32[]{:S(2)}) collective-permute-start(bf16[64,32,1024]{2,1,0:T(8,128)(2,1)} %sum_blocks.21.refs_2_), channel_id=1, source_target_pairs={{0,16},{8,24},{16,0},{24,8},{1,17},{9,25},{17,1},{25,9},{2,18},{10... | collective-permute-start | bytes 12582920 | tf_op jit(solution)/shard_map/ppermute | solution.py:489
  612.2 11.5 %copy-start.4 = (bf16[2,10,162,256]{3,2,1,0:T(8,128)(2,1)S(1)}, bf16[2,10,162,256]{3,2,1,0:T(8,128)(2,1)}, u32[]{:S(2)}) copy-start(bf16[2,10,162,256]{3,2,1,0:T(8,128)(2,1)} %copy-done.3) | copy-start | bytes 4976644
  620.3 116.2 %collective-permute-start.11 = (bf16[80,32,1024]{2,1,0:T(8,128)(2,1)}, bf16[80,32,1024]{2,1,0:T(8,128)(2,1)}, u32[]{:S(2)}, u32[]{:S(2)}) collective-permute-start(bf16[80,32,1024]{2,1,0:T(8,128)(2,1)} %sum_blocks.22.refs_2_), channel_id=1, source_target_pairs={{0,1},{1,0},{2,3},{3,2},{4,5},{5,4},{6,7},{7,6},{8,9},{9,8},{10,11... | collective-permute-start | bytes 15728648 | tf_op jit(solution)/shard_map/ppermute | solution.py:489
  623.6 70.4 %collective-permute-start.10 = (bf16[48,32,1024]{2,1,0:T(8,128)(2,1)}, bf16[48,32,1024]{2,1,0:T(8,128)(2,1)S(1)}, u32[]{:S(2)}, u32[]{:S(2)}) collective-permute-start(bf16[48,32,1024]{2,1,0:T(8,128)(2,1)} %sum_blocks.20.refs_2_), channel_id=1, source_target_pairs={{0,2},{1,3},{2,0},{3,1},{4,6},{5,7},{6,4},{7,5},{8,10},{9,11},{10,... | collective-permute-start | bytes 9437192 | tf_op jit(solution)/shard_map/ppermute | solution.py:489
  637.3 179.0 %collective-permute-start.17 = (bf16[80,32,1024]{2,1,0:T(8,128)(2,1)}, bf16[80,32,1024]{2,1,0:T(8,128)(2,1)}, u32[]{:S(2)}, u32[]{:S(2)}) collective-permute-start(bf16[80,32,1024]{2,1,0:T(8,128)(2,1)} %sum_blocks.23.refs_2_), channel_id=1, source_target_pairs={{0,16},{8,24},{16,0},{24,8},{1,17},{9,25},{17,1},{25,9},{2,18},{10... | collective-permute-start | bytes 15728648 | tf_op jit(solution)/shard_map/ppermute | solution.py:489
  690.7 139.5 %collective-permute-start.16 = (bf16[48,32,1024]{2,1,0:T(8,128)(2,1)}, bf16[48,32,1024]{2,1,0:T(8,128)(2,1)}, u32[]{:S(2)}, u32[]{:S(2)}) collective-permute-start(bf16[48,32,1024]{2,1,0:T(8,128)(2,1)} %sum_blocks.24.after_ref), channel_id=1, source_target_pairs={{0,2},{1,3},{2,0},{3,1},{4,6},{5,7},{6,4},{7,5},{8,10},{9,11},{10,... | collective-permute-start | bytes 9437192 | tf_op jit(solution)/shard_map/ppermute | solution.py:489
  699.3 138.5 %collective-permute-start.15 = (bf16[24,32,1024]{2,1,0:T(8,128)(2,1)}, bf16[24,32,1024]{2,1,0:T(8,128)(2,1)S(1)}, u32[]{:S(2)}, u32[]{:S(2)}) collective-permute-start(bf16[24,32,1024]{2,1,0:T(8,128)(2,1)} %sum_blocks.25.refs_3_), channel_id=1, source_target_pairs={{0,4},{1,5},{2,6},{3,7},{4,0},{5,1},{6,2},{7,3},{8,12},{9,13},{10,... | collective-permute-start | bytes 4718600 | tf_op jit(solution)/shard_map/ppermute | solution.py:489
  708.7 133.5 %collective-permute-start.14 = (bf16[32,32,1024]{2,1,0:T(8,128)(2,1)}, bf16[32,32,1024]{2,1,0:T(8,128)(2,1)}, u32[]{:S(2)}, u32[]{:S(2)}) collective-permute-start(bf16[32,32,1024]{2,1,0:T(8,128)(2,1)} %sum_blocks.26.after_ref), channel_id=1, source_target_pairs={{0,1},{1,0},{2,3},{3,2},{4,5},{5,4},{6,7},{7,6},{8,9},{9,8},{10,11... | collective-permute-start | bytes 6291464 | tf_op jit(solution)/shard_map/ppermute | solution.py:489
  785.4 32.2 %copy-start.31 = (bf16[256,1024]{1,0:T(8,128)(2,1)S(1)}, bf16[256,1024]{1,0:T(8,128)(2,1)}, u32[]{:S(2)}) copy-start(bf16[256,1024]{1,0:T(8,128)(2,1)} %copy-done.30) | copy-start | bytes 1572868
  785.4 32.2 %copy-start.56 = (bf16[256,81]{0,1:T(8,128)(2,1)S(1)}, bf16[256,81]{0,1:T(8,128)(2,1)}, u32[]{:S(2)}) copy-start(bf16[256,81]{0,1:T(8,128)(2,1)} %copy-done.55) | copy-start | bytes 124420
  785.5 32.2 %copy-start.80 = (bf16[256,4]{0,1:T(4,128)(2,1)S(1)}, bf16[256,4]{0,1:T(4,128)(2,1)}, u32[]{:S(2)}) copy-start(bf16[256,4]{0,1:T(4,128)(2,1)} %copy-done.79) | copy-start | bytes 6148
  785.5 32.4 %copy-start.29 = (bf16[256,1024]{1,0:T(8,128)(2,1)S(1)}, bf16[256,1024]{1,0:T(8,128)(2,1)}, u32[]{:S(2)}) copy-start(bf16[256,1024]{1,0:T(8,128)(2,1)} %copy-done.28) | copy-start | bytes 1572868
  785.5 32.4 %copy-start.58 = (bf16[256,81]{0,1:T(8,128)(2,1)S(1)}, bf16[256,81]{0,1:T(8,128)(2,1)}, u32[]{:S(2)}) copy-start(bf16[256,81]{0,1:T(8,128)(2,1)} %copy-done.57) | copy-start | bytes 124420
  785.5 32.4 %copy-start.82 = (bf16[256,4]{0,1:T(4,128)(2,1)S(1)}, bf16[256,4]{0,1:T(4,128)(2,1)}, u32[]{:S(2)}) copy-start(bf16[256,4]{0,1:T(4,128)(2,1)} %copy-done.81) | copy-start | bytes 6148
  785.5 32.6 %copy-start.27 = (bf16[256,1024]{1,0:T(8,128)(2,1)S(1)}, bf16[256,1024]{1,0:T(8,128)(2,1)}, u32[]{:S(2)}) copy-start(bf16[256,1024]{1,0:T(8,128)(2,1)} %copy-done.26) | copy-start | bytes 1572868
  785.5 32.6 %copy-start.54 = (bf16[256,81]{0,1:T(8,128)(2,1)S(1)}, bf16[256,81]{0,1:T(8,128)(2,1)}, u32[]{:S(2)}) copy-start(bf16[256,81]{0,1:T(8,128)(2,1)} %copy-done.53) | copy-start | bytes 124420
  785.5 32.6 %copy-start.78 = (bf16[256,4]{0,1:T(4,128)(2,1)S(1)}, bf16[256,4]{0,1:T(4,128)(2,1)}, u32[]{:S(2)}) copy-start(bf16[256,4]{0,1:T(4,128)(2,1)} %copy-done.77) | copy-start | bytes 6148
  786.5 60.0 %collective-permute-start.12 = (bf16[2,3,160,256]{3,2,1,0:T(8,128)(2,1)}, bf16[2,3,160,256]{3,2,1,0:T(8,128)(2,1)}, u32[]{:S(2)}, u32[]{:S(2)}) collective-permute-start(bf16[2,3,160,256]{3,2,1,0:T(8,128)(2,1)} %get-tuple-element.104), channel_id=1, source_target_pairs={{0,1},{1,2},{2,3},{3,4},{4,5},{5,6},{6,7},{8,9},{9,10},{10,11},{11... | collective-permute-start | bytes 1474568 | tf_op jit(solution)/shard_map/ppermute | solution.py:1106
  816.3 31.4 %collective-permute-start.13 = (bf16[2,3,160,256]{3,2,1,0:T(8,128)(2,1)}, bf16[2,3,160,256]{3,2,1,0:T(8,128)(2,1)}, u32[]{:S(2)}, u32[]{:S(2)}) collective-permute-start(bf16[2,3,160,256]{3,2,1,0:T(8,128)(2,1)} %get-tuple-element.103), channel_id=1, source_target_pairs={{1,0},{2,1},{3,2},{4,3},{5,4},{6,5},{7,6},{9,8},{10,9},{11,10},{12... | collective-permute-start | bytes 1474568 | tf_op jit(solution)/shard_map/ppermute | solution.py:1107
  830.2 95.8 %collective-permute-start.20 = (bf16[40,32,1024]{2,1,0:T(8,128)(2,1)}, bf16[40,32,1024]{2,1,0:T(8,128)(2,1)S(1)}, u32[]{:S(2)}, u32[]{:S(2)}) collective-permute-start(bf16[40,32,1024]{2,1,0:T(8,128)(2,1)} %sum_blocks.27.after_ref), channel_id=1, source_target_pairs={{0,2},{1,3},{2,0},{3,1},{4,6},{5,7},{6,4},{7,5},{8,10},{9,11},{10,... | collective-permute-start | bytes 7864328 | tf_op jit(solution)/shard_map/ppermute | solution.py:489
  837.8 94.7 %collective-permute-start.19 = (bf16[40,32,1024]{2,1,0:T(8,128)(2,1)}, bf16[40,32,1024]{2,1,0:T(8,128)(2,1)S(1)}, u32[]{:S(2)}, u32[]{:S(2)}) collective-permute-start(bf16[40,32,1024]{2,1,0:T(8,128)(2,1)} %sum_blocks.28.refs_3_), channel_id=1, source_target_pairs={{0,1},{1,0},{2,3},{3,2},{4,5},{5,4},{6,7},{7,6},{8,9},{9,8},{10,11... | collective-permute-start | bytes 7864328 | tf_op jit(solution)/shard_map/ppermute | solution.py:489
  842.2 98.5 %collective-permute-start.18 = (bf16[24,32,1024]{2,1,0:T(8,128)(2,1)}, bf16[24,32,1024]{2,1,0:T(8,128)(2,1)}, u32[]{:S(2)}, u32[]{:S(2)}) collective-permute-start(bf16[24,32,1024]{2,1,0:T(8,128)(2,1)} %sum_blocks.29.refs_4_), channel_id=1, source_target_pairs={{0,4},{1,5},{2,6},{3,7},{4,0},{5,1},{6,2},{7,3},{8,12},{9,13},{10,... | collective-permute-start | bytes 4718600 | tf_op jit(solution)/shard_map/ppermute | solution.py:489
  846.5 103.5 %collective-permute-start.25 = (bf16[12,32,1024]{2,1,0:T(8,128)(2,1)}, bf16[12,32,1024]{2,1,0:T(8,128)(2,1)}, u32[]{:S(2)}, u32[]{:S(2)}) collective-permute-start(bf16[12,32,1024]{2,1,0:T(8,128)(2,1)} %sum_blocks.30.refs_4_), channel_id=1, source_target_pairs={{0,1},{1,0},{2,3},{3,2},{4,5},{5,4},{6,7},{7,6},{8,9},{9,8},{10,11... | collective-permute-start | bytes 2359304 | tf_op jit(solution)/shard_map/ppermute | solution.py:489
  847.7 105.5 %collective-permute-start.24 = (bf16[16,32,1024]{2,1,0:T(8,128)(2,1)}, bf16[16,32,1024]{2,1,0:T(8,128)(2,1)}, u32[]{:S(2)}, u32[]{:S(2)}) collective-permute-start(bf16[16,32,1024]{2,1,0:T(8,128)(2,1)} %sum_blocks.31.after_ref), channel_id=1, source_target_pairs={{0,2},{1,3},{2,0},{3,1},{4,6},{5,7},{6,4},{7,5},{8,10},{9,11},{10,... | collective-permute-start | bytes 3145736 | tf_op jit(solution)/shard_map/ppermute | solution.py:489
  931.2 6.8 copy-start.2
  931.2 6.8 copy-start.45
  931.2 32.1 %collective-permute-start.23 = (bf16[20,32,1024]{2,1,0:T(8,128)(2,1)}, bf16[20,32,1024]{2,1,0:T(8,128)(2,1)}, u32[]{:S(2)}, u32[]{:S(2)}) collective-permute-start(bf16[20,32,1024]{2,1,0:T(8,128)(2,1)} %sum_blocks.32.refs_4_), channel_id=1, source_target_pairs={{0,16},{8,24},{16,0},{24,8},{1,17},{9,25},{17,1},{25,9},{2,18},{10... | collective-permute-start | bytes 3932168 | tf_op jit(solution)/shard_map/ppermute | solution.py:489
  937.8 54.0 %collective-permute-start.22 = (bf16[20,32,1024]{2,1,0:T(8,128)(2,1)}, bf16[20,32,1024]{2,1,0:T(8,128)(2,1)}, u32[]{:S(2)}, u32[]{:S(2)}) collective-permute-start(bf16[20,32,1024]{2,1,0:T(8,128)(2,1)} %sum_blocks.33.refs_4_), channel_id=1, source_target_pairs={{0,2},{1,3},{2,0},{3,1},{4,6},{5,7},{6,4},{7,5},{8,10},{9,11},{10,... | collective-permute-start | bytes 3932168 | tf_op jit(solution)/shard_map/ppermute | solution.py:489
  943.8 52.2 %collective-permute-start.21 = (bf16[12,32,1024]{2,1,0:T(8,128)(2,1)}, bf16[12,32,1024]{2,1,0:T(8,128)(2,1)}, u32[]{:S(2)}, u32[]{:S(2)}) collective-permute-start(bf16[12,32,1024]{2,1,0:T(8,128)(2,1)} %sum_blocks.34.refs_5_), channel_id=1, source_target_pairs={{0,1},{1,0},{2,3},{3,2},{4,5},{5,4},{6,7},{7,6},{8,9},{9,8},{10,11... | collective-permute-start | bytes 2359304 | tf_op jit(solution)/shard_map/ppermute | solution.py:489
  952.5 129.9 %collective-permute-start.30 = (bf16[6,32,1024]{2,1,0:T(8,128)(2,1)}, bf16[6,32,1024]{2,1,0:T(8,128)(2,1)}, u32[]{:S(2)}, u32[]{:S(2)}) collective-permute-start(bf16[6,32,1024]{2,1,0:T(8,128)(2,1)} %sum_blocks.35.refs_5_), channel_id=1, source_target_pairs={{0,16},{8,24},{16,0},{24,8},{1,17},{9,25},{17,1},{25,9},{2,18},{10... | collective-permute-start | bytes 1179656 | tf_op jit(solution)/shard_map/ppermute | solution.py:489
  956.0 131.3 %collective-permute-start.29 = (bf16[8,32,1024]{2,1,0:T(8,128)(2,1)}, bf16[8,32,1024]{2,1,0:T(8,128)(2,1)}, u32[]{:S(2)}, u32[]{:S(2)}) collective-permute-start(bf16[8,32,1024]{2,1,0:T(8,128)(2,1)} %sum_blocks.36.refs_5_), channel_id=1, source_target_pairs={{0,4},{1,5},{2,6},{3,7},{4,0},{5,1},{6,2},{7,3},{8,12},{9,13},{10,... | collective-permute-start | bytes 1572872 | tf_op jit(solution)/shard_map/ppermute | solution.py:489
  966.4 130.0 %collective-permute-start.28 = (bf16[10,32,1024]{2,1,0:T(8,128)(2,1)}, bf16[10,32,1024]{2,1,0:T(8,128)(2,1)}, u32[]{:S(2)}, u32[]{:S(2)}) collective-permute-start(bf16[10,32,1024]{2,1,0:T(8,128)(2,1)} %sum_blocks.37.refs_5_), channel_id=1, source_target_pairs={{0,4},{1,5},{2,6},{3,7},{4,0},{5,1},{6,2},{7,3},{8,12},{9,13},{10,... | collective-permute-start | bytes 1966088 | tf_op jit(solution)/shard_map/ppermute | solution.py:489
  995.0 108.6 %collective-permute-start.27 = (bf16[10,32,1024]{2,1,0:T(8,128)(2,1)}, bf16[10,32,1024]{2,1,0:T(8,128)(2,1)S(1)}, u32[]{:S(2)}, u32[]{:S(2)}) collective-permute-start(bf16[10,32,1024]{2,1,0:T(8,128)(2,1)} %sum_blocks.38.refs_5_), channel_id=1, source_target_pairs={{0,4},{1,5},{2,6},{3,7},{4,0},{5,1},{6,2},{7,3},{8,12},{9,13},{10,... | collective-permute-start | bytes 1966088 | tf_op jit(solution)/shard_map/ppermute | solution.py:489
  995.9 78.8 %copy-start.24 = (f32[2560,256]{1,0:T(8,128)S(1)}, f32[2560,256]{1,0:T(8,128)}, u32[]{:S(2)}) copy-start(f32[2560,256]{1,0:T(8,128)} %param.26) | copy-start | bytes 7864324
  998.6 113.0 %collective-permute-start.26 = (bf16[6,32,1024]{2,1,0:T(8,128)(2,1)}, bf16[6,32,1024]{2,1,0:T(8,128)(2,1)}, u32[]{:S(2)}, u32[]{:S(2)}) collective-permute-start(bf16[6,32,1024]{2,1,0:T(8,128)(2,1)} %sum_blocks.39.refs_4_), channel_id=1, source_target_pairs={{0,16},{8,24},{16,0},{24,8},{1,17},{9,25},{17,1},{25,9},{2,18},{10... | collective-permute-start | bytes 1179656 | tf_op jit(solution)/shard_map/ppermute | solution.py:489
  1000.0 74.8 %copy-start.23 = (f32[2560,256]{1,0:T(8,128)S(1)}, f32[2560,256]{1,0:T(8,128)}, u32[]{:S(2)}) copy-start(f32[2560,256]{1,0:T(8,128)} %param.25) | copy-start | bytes 7864324
  1087.3 6.0 copy-start.63
  1087.3 6.0 copy-start.65
  1087.4 6.6 copy-start.21
  1087.4 6.6 copy-start.22
  1087.4 6.6 copy-start.50
  1087.4 6.6 copy-start.51
  (78 other events, 207.6 us)
Sparse Core Ops, SparseCore 0:
  12.8 173.4 all-gather.1

commit v5 on v4

--- a/solution.py
+++ b/solution.py
@@ -460,7 +460,7 @@
     return list(range(count.bit_length() - 1))
 
 
-PARTS = ((6, "zwxy"), (8, "yxzw"), (10, "xzyw"), (10, "yxzw"), (6, "zwxy"))
+PARTS = ((6, "zwyx"), (6, "yxzw"), (10, "xzyw"), (12, "yxzw"), (6, "zwxy"))
 TURNS_AT = {0: 5, 5: 7, 7: 3, 8: 6}
 EDGES_AT = 12
 

time: 1140 us -> 1140 us (level)
  transfers between devices with their start and end apart: 32 -> 32, of which waited for: 9 -> 8; matrix products, arithmetic and copies ran while one was open for 9% -> 9% of each run, Pallas kernels for 39% -> 40%
where the time goes in v5:
time: 1140 us; the launch traced here: 1130 us
  Pallas kernels  765 us (67%)
  waiting for transfers between devices  128 us (11%)
  matrix products  63.2 us (6%)
  local copies, waits for them, and re-layouts  59.6 us (5%)
  starting transfers between devices  50.5 us (4%)
  other arithmetic  43.2 us (4%)
  between operations  20.2 us (2%)
    pallas_call x1, Pallas kernels, gather_blocks(): pl.pallas_call(body, in_specs=[anywhere] * 3, out_specs=anywhere, out_sha...  226 us
    pallas_call x4, Pallas kernels, map_grads(): pl.pallas_call(body, grid_spec=pltpu.PrefetchScalarGridSpec(num_scalar_pr...  148 us
    ppermute x25, waiting for transfers between devices, swap(): return lax.ppermute(values, axis, [(i, i ^ 1 << bit) for i in range(count)])  109 us
    pallas_call x1, Pallas kernels, pool_regions(): pl.pallas_call(body, grid=(section_count, bins // group), in_specs=[pl.Bl...  109 us
    pallas_call x20, Pallas kernels, sum_blocks(): pl.pallas_call(body, grid=(half // batch,), in_specs=[pl.BlockSpec((batch...  87.1 us
    pallas_call x1, Pallas kernels, sum_everywhere(): pl.pallas_call(body, in_specs=[whole] * number + [pl.BlockSpec(memory_spa...  74 us
    pallas_call x1, Pallas kernels, weight_grads(): pl.pallas_call(body, grid_spec=pltpu.PrefetchScalarGridSpec(num_scalar_pr...  46.4 us
    pallas_call x1, Pallas kernels, first_layer(): pl.pallas_call(body, grid_spec=pltpu.PrefetchScalarGridSpec(num_scalar_pr...  40.7 us
  transfers between devices with their start and end apart: 32, of which 8 were waited for; matrix products, arithmetic and copies ran while one was open for 9% of the time, Pallas kernels for 40%

profile of v5, /device:TPU:0, one launch (start us, length us, event | category | flops | bytes accessed | tf_op | source)
XLA Modules:
  0.0 1129.2 jit_solution(11735345242471573667)
XLA Ops:
  7.2 3.0 convert_element_type.135.own_ref
  16.6 4.8 collective-permute-start
  22.8 5.2 scatter_custom_fusion
  33.1 3.0 fusion.138
  38.2 5.2 sort.31
  52.5 4.6 collective-permute-start.2
  59.9 18.7 %collective-permute-done.2 = bf16[2,2,160,256]{3,2,1,0:T(8,128)(2,1)S(1)} collective-permute-done((bf16[2,2,160,256]{3,2,1,0:T(8,128)(2,1)S(1)}, bf16[2,2,160,256]{3,2,1,0:T(8,128)(2,1)S(1)}, u32[]{:S(2)}, u32[]{:S(2)}) %collective-permute-start.2) | collective-permute-done | bytes 327712 | tf_op jit(solution)/shard_map/ppermute | solution.py:33
  81.0 108.7 %pool_regions.1.after_ref.x_ref = bf16[3,49,256,256]{3,2,1,0:T(8,128)(2,1)} custom-call(bf16[256,3840]{1,0:T(8,128)(2,1)} %bitcast.298, s32[3,49,256]{2,1,0:T(8,128)} %get-tuple-element.120.row_ref, s32[3,49,256]{2,1,0:T(8,128)} %get-tuple-element.119.col_ref, f32[3,49,256]{2,1,0:T(8,128)} %get-tuple-element.176.fr_ref, f32[3,49,256]{2,1,0:T(8,128)} %get-tuple-element.175.fc_ref), custom_call_target="tpu_custom_call" | custom-call | flops 73987522560 | bytes 19267584 | tf_op jit(solution)/shard_map/pool_regions/pallas_call | solution.py:138
  189.8 226.3 %gather_blocks.1.blocks_ref = bf16[1280,32,1024]{2,1,0:T(8,128)(2,1)} custom-call(bf16[40,32,1024]{2,1,0:T(8,128)(2,1)} %copy-done.12, bf16[384,32,1024]{2,1,0:T(8,128)(2,1)} %all-gather.2.cloned.1.call-done.part_ref, bf16[3,49,256,256]{3,2,1,0:T(8,128)(2,1)} %pool_regions.1.after_ref.x_ref), custom_call_target="tpu_custom_call" | custom-call | tf_op jit(solution)/shard_map/gather_blocks/pallas_call | solution.py:617
  416.1 40.7 %first_layer.1 = f32[3,256,1024]{2,1,0:T(8,128)} custom-call(s32[1272]{0:T(1024)} %copy-done.62, bf16[1280,32,1024]{2,1,0:T(8,128)(2,1)} %gather_blocks.1.blocks_ref, bf16[3,49,256,256]{3,2,1,0:T(8,128)(2,1)} %pool_regions.1.after_ref.x_ref), custom_call_target="tpu_custom_call" | custom-call | flops 19730006016 | bytes 96337920 | tf_op jit(solution)/shard_map/first_layer/pallas_call | solution.py:204
  456.8 3.7 gather_fusion.2
  460.5 3.7 multiply_convert_fusion.3
  466.0 3.8 gather_fusion.1
  469.9 3.7 multiply_convert_fusion.5
  475.9 3.8 gather_fusion
  479.8 2.8 fusion.128
  482.7 3.0 multiply_convert_fusion.7
  505.5 46.4 %weight_grads.1 = (bf16[96,32,1024]{2,1,0:T(8,128)(2,1)}, bf16[96,32,1024]{2,1,0:T(8,128)(2,1)}, bf16[96,32,1024]{2,1,0:T(8,128)(2,1)}, bf16[96,32,1024]{2,1,0:T...) custom-call(s32[1272]{0:T(1024)} %get-tuple-element.45.order_ref, ...), custom_call_target="tpu_custom_call" | custom-call | flops 21340618752 | bytes 104202240 | tf_op jit(solution)/shard_map/weight_grads/pallas_call | solution.py:293
  555.8 35.5 %map_grads.4.refs_2_.old_ref = f32[3840,256]{1,0:T(8,128)} custom-call(s32[1272]{0:T(1024)} %copy-done.62, bf16[1280,32,1024]{2,1,0:T(8,128)(2,1)} %gather_blocks.1.blocks_ref, bf16[3,256,1024]{2,1,0:T(8,128)(2,1)} %pad_maximum_fusion.1.gf_ref.g_ref, s32[3,49,256]{2,1,0:T(8,128)} %get-tuple-element.120.row_ref, s32[3,49,256]{2,1,0:T(8,128)} %get-tuple-element.119.col_ref, ...), custom_call_target="tpu_custom_call" | custom-call | flops 22313697280 | bytes 18350080 | tf_op jit(solution)/shard_map/map_grads/pallas_call | solution.py:395
  591.3 13.4 %collective-permute-done.8.refs_1_ = bf16[96,32,1024]{2,1,0:T(8,128)(2,1)} collective-permute-done((bf16[96,32,1024]{2,1,0:T(8,128)(2,1)}, bf16[96,32,1024]{2,1,0:T(8,128)(2,1)}, u32[]{:S(2)}, u32[]{:S(2)}) %collective-permute-start.8) | collective-permute-done | bytes 6291488 | tf_op jit(solution)/shard_map/ppermute | solution.py:489
  604.8 5.4 sum_blocks.20.refs_2_
  612.8 5.4 sum_blocks.21.refs_2_
  618.2 8.2 sum_blocks.22.refs_2_
  631.3 4.0 fusion.214
  637.0 8.7 sum_blocks.23.refs_2_
  646.2 5.4 sum_blocks.24.after_ref
  653.6 47.2 %map_grads.5.refs_3_.old_ref = f32[3840,256]{1,0:T(8,128)} custom-call(s32[1272]{0:T(1024)} %copy-done.62, bf16[1280,32,1024]{2,1,0:T(8,128)(2,1)} %gather_blocks.1.blocks_ref, bf16[3,256,1024]{2,1,0:T(8,128)(2,1)} %pad_maximum_fusion.1.gf_ref.g_ref, s32[3,49,256]{2,1,0:T(8,128)} %get-tuple-element.120.row_ref, s32[3,49,256]{2,1,0:T(8,128)} %get-tuple-element.119.col_ref, ...), custom_call_target="tpu_custom_call" | custom-call | flops 31239176192 | bytes 25690112 | tf_op jit(solution)/shard_map/map_grads/pallas_call | solution.py:395
  702.6 3.5 sum_blocks.25.refs_3_
  707.3 3.5 sum_blocks.26.after_ref
  710.8 23.8 %map_grads.6.refs_3_.old_ref = f32[3840,256]{1,0:T(8,128)} custom-call(s32[1272]{0:T(1024)} %copy-done.62, bf16[1280,32,1024]{2,1,0:T(8,128)(2,1)} %gather_blocks.1.blocks_ref, bf16[3,256,1024]{2,1,0:T(8,128)(2,1)} %pad_maximum_fusion.1.gf_ref.g_ref, s32[3,49,256]{2,1,0:T(8,128)} %get-tuple-element.120.row_ref, s32[3,49,256]{2,1,0:T(8,128)} %get-tuple-element.119.col_ref, ...), custom_call_target="tpu_custom_call" | custom-call | flops 13388218368 | bytes 11010048 | tf_op jit(solution)/shard_map/map_grads/pallas_call | solution.py:395
  734.6 7.9 collective-permute-done.11.refs_2_
  742.5 5.5 sum_blocks.27.after_ref
  748.0 41.2 %map_grads.7.refs_3_.own_ref = f32[3840,256]{1,0:T(8,128)} custom-call(s32[1272]{0:T(1024)} %copy-done.62, bf16[1280,32,1024]{2,1,0:T(8,128)(2,1)} %gather_blocks.1.blocks_ref, bf16[3,256,1024]{2,1,0:T(8,128)(2,1)} %pad_maximum_fusion.1.gf_ref.g_ref, s32[3,49,256]{2,1,0:T(8,128)} %get-tuple-element.120.row_ref, s32[3,49,256]{2,1,0:T(8,128)} %get-tuple-element.119.col_ref, ...), custom_call_target="tpu_custom_call" | custom-call | flops 26776436736 | bytes 22020096 | tf_op jit(solution)/shard_map/map_grads/pallas_call | solution.py:395
  792.5 9.5 collective-permute-done.16.refs_2_
  804.0 31.0 %collective-permute-done.17.refs_2_ = bf16[96,32,1024]{2,1,0:T(8,128)(2,1)} collective-permute-done((bf16[96,32,1024]{2,1,0:T(8,128)(2,1)}, bf16[96,32,1024]{2,1,0:T(8,128)(2,1)}, u32[]{:S(2)}, u32[]{:S(2)}) %collective-permute-start.17) | collective-permute-done | bytes 6291488 | tf_op jit(solution)/shard_map/ppermute | solution.py:489
  838.2 2.9 copy.160
  843.3 6.6 sum_blocks.28.refs_3_
  849.9 3.5 sum_blocks.29.refs_4_
  856.1 3.1 sum_blocks.30.refs_4_
  859.2 3.2 collective-permute-start.18
  862.4 3.1 sum_blocks.31.after_ref
  867.2 6.9 collective-permute-start.24
  874.1 3.7 edge_rows.1.refs_4_
  877.8 3.5 fusion.40
  881.3 2.9 fusion.42
  884.3 2.9 fusion.44
  887.2 3.8 sum_blocks.32.refs_4_
  893.3 2.7 fusion.64
  909.3 3.3 convert_reduce_fusion.1
  912.6 20.8 %collective-permute-done.19.refs_3_ = bf16[48,32,1024]{2,1,0:T(8,128)(2,1)S(1)} collective-permute-done((bf16[48,32,1024]{2,1,0:T(8,128)(2,1)}, bf16[48,32,1024]{2,1,0:T(8,128)(2,1)S(1)}, u32[]{:S(2)}, u32[]{:S(2)}) %collective-permute-start.19) | collective-permute-done | bytes 3145760 | tf_op jit(solution)/shard_map/ppermute | solution.py:489
  935.1 4.3 sum_blocks.33.refs_4_
  943.9 3.1 sum_blocks.34.refs_5_
  949.3 2.7 fusion.106
  959.6 2.8 collective-permute-start.29
  962.4 3.1 sum_blocks.37.refs_5_
  965.7 26.1 %collective-permute-done.22.refs_4_ = bf16[24,32,1024]{2,1,0:T(8,128)(2,1)} collective-permute-done((bf16[24,32,1024]{2,1,0:T(8,128)(2,1)}, bf16[24,32,1024]{2,1,0:T(8,128)(2,1)}, u32[]{:S(2)}, u32[]{:S(2)}) %collective-permute-start.22) | collective-permute-done | bytes 1572896 | tf_op jit(solution)/shard_map/ppermute | solution.py:489
  991.8 3.5 sum_blocks.38.refs_5_
  1000.4 74.0 %sum_everywhere.1 = (bf16[8192,128]{1,0:T(8,128)(2,1)}, f32[256,128]{1,0:T(8,128)}) custom-call(f32[256,256]{1,0:T(8,128)} %fusion.56.refs_0_, f32[2304,256]{1,0:T(8,128)} %fusion.112.refs_1_, f32[3072,85]{1,0:T(8,128)} %bitcast.290, f32[56,128]{1,0:T(8,128)} %pad_bitcast_fusion.refs_3_, bf16[6,32,1024]{2,1,0:T(8,128)(2,1)} %sum_blocks.39.refs_4_), custom_call_target="tpu_custom_call" | custom-call | tf_op jit(solution)/shard_map/sum_everywhere/pallas_call | solution.py:790
  1078.9 4.3 multiply_subtract_fusion
  1086.6 4.9 finish_blocks.5
  1091.5 4.9 finish_blocks.6
  1097.3 7.7 finish_blocks.7
  1108.2 7.7 finish_blocks.8
  1115.9 4.9 finish_blocks.9
  (372 shorter events, 131.9 us)
Async XLA Ops:
  7.2 8.0 copy-start
  7.2 182.6 %all-gather.2.cloned.1.call-start = ((), (), s32[]{:S(2)}) async-start(), calls=%async_computation | async-start | bytes 25952256 | tf_op jit(solution)/shard_map/all_gather | solution.py:943
  15.2 7.5 copy-start.93
  15.2 13.5 %copy-start.108 = (s32[256]{0:T(256)S(1)}, s32[256]{0:T(256)}, u32[]{:S(2)}) copy-start(s32[256]{0:T(256)} %param.37) | copy-start | bytes 3076
  15.2 15.4 %copy-start.103 = (s32[3,256]{1,0:T(4,128)S(1)}, s32[3,256]{1,0:T(4,128)}, u32[]{:S(2)}) copy-start(s32[3,256]{1,0:T(4,128)} %param.40) | copy-start | bytes 9220
  15.2 15.4 %copy-start.91 = (s32[256]{0:T(256)S(1)}, s32[256]{0:T(256)}, u32[]{:S(2)}) copy-start(s32[256]{0:T(256)} %param.41) | copy-start | bytes 3076
  15.2 16.7 %copy-start.61 = (s32[3,49,256]{2,1,0:T(8,128)S(1)}, s32[3,49,256]{2,1,0:T(8,128)}, u32[]{:S(2)}) copy-start(s32[3,49,256]{2,1,0:T(8,128)} %param.38) | copy-start | bytes 451588
  15.3 17.6 %copy-start.60 = (f32[3,2,49,256]{3,1,2,0:T(2,128)S(1)}, f32[3,2,49,256]{3,1,2,0:T(2,128)}, u32[]{:S(2)}) copy-start(f32[3,2,49,256]{3,1,2,0:T(2,128)} %param.39) | copy-start | bytes 903172
  15.8 30.5 %copy-start.6 = (bf16[2,8,160,256]{3,2,1,0:T(8,128)(2,1)}, bf16[2,8,160,256]{3,2,1,0:T(8,128)(2,1)S(1)}, u32[]{:S(2)}) copy-start(bf16[2,8,160,256]{3,2,1,0:T(8,128)(2,1)S(1)} %add_convert_fusion.2) | copy-start | bytes 3932164
  16.6 27.6 %collective-permute-start = (bf16[2,1,160,256]{3,2,1,0:T(8,128)(2,1)}, bf16[2,1,160,256]{3,2,1,0:T(8,128)(2,1)S(1)}, u32[]{:S(2)}, u32[]{:S(2)}) collective-permute-start(bf16[2,1,160,256]{3,2,1,0:T(8,128)(2,1)} %get-tuple-element.115), channel_id=1, source_target_pairs={{0,1},{1,2},{2,3},{3,4},{4,5},{5,6},{6,7},{8,9},{9,10},{10,11},{11... | collective-permute-start | bytes 491528 | tf_op jit(solution)/shard_map/ppermute | solution.py:33
  21.5 24.2 %collective-permute-start.1 = (bf16[2,1,160,256]{3,2,1,0:T(8,128)(2,1)}, bf16[2,1,160,256]{3,2,1,0:T(8,128)(2,1)S(1)}, u32[]{:S(2)}, u32[]{:S(2)}) collective-permute-start(bf16[2,1,160,256]{3,2,1,0:T(8,128)(2,1)} %get-tuple-element.116), channel_id=1, source_target_pairs={{1,0},{2,1},{3,2},{4,3},{5,4},{6,5},{7,6},{9,8},{10,9},{11,10},{12... | collective-permute-start | bytes 491528 | tf_op jit(solution)/shard_map/ppermute | solution.py:35
  51.1 7.4 copy-start.104
  52.5 26.1 %collective-permute-start.2 = (bf16[2,2,160,256]{3,2,1,0:T(8,128)(2,1)S(1)}, bf16[2,2,160,256]{3,2,1,0:T(8,128)(2,1)S(1)}, u32[]{:S(2)}, u32[]{:S(2)}) collective-permute-start(bf16[2,2,160,256]{3,2,1,0:T(8,128)(2,1)S(1)} %get-tuple-element.113), channel_id=1, source_target_pairs={{0,1},{1,2},{2,3},{3,4},{4,5},{5,6},{6,7},{8,9},{9,10},{10,11},{11... | collective-permute-start | bytes 983048 | tf_op jit(solution)/shard_map/ppermute | solution.py:33
  57.0 21.5 %collective-permute-start.3 = (bf16[2,2,160,256]{3,2,1,0:T(8,128)(2,1)S(1)}, bf16[2,2,160,256]{3,2,1,0:T(8,128)(2,1)S(1)}, u32[]{:S(2)}, u32[]{:S(2)}) collective-permute-start(bf16[2,2,160,256]{3,2,1,0:T(8,128)(2,1)S(1)} %get-tuple-element.114), channel_id=1, source_target_pairs={{1,0},{2,1},{3,2},{4,3},{5,4},{6,5},{7,6},{9,8},{10,9},{11,10},{12... | collective-permute-start | bytes 983048 | tf_op jit(solution)/shard_map/ppermute | solution.py:35
  489.5 10.2 copy-start.78
  492.0 7.7 copy-start.54
  552.0 85.0 %collective-permute-start.5 = (bf16[192,32,1024]{2,1,0:T(8,128)(2,1)}, bf16[192,32,1024]{2,1,0:T(8,128)(2,1)}, u32[]{:S(2)}, u32[]{:S(2)}) collective-permute-start(bf16[192,32,1024]{2,1,0:T(8,128)(2,1)} %get-tuple-element.51), channel_id=1, source_target_pairs={{0,8},{8,0},{16,24},{24,16},{1,9},{9,1},{17,25},{25,17},{2,10},{10... | collective-permute-start | bytes 37748744 | tf_op jit(solution)/shard_map/ppermute | solution.py:489
  552.6 65.6 %collective-permute-start.6 = (bf16[160,32,1024]{2,1,0:T(8,128)(2,1)}, bf16[160,32,1024]{2,1,0:T(8,128)(2,1)}, u32[]{:S(2)}, u32[]{:S(2)}) collective-permute-start(bf16[160,32,1024]{2,1,0:T(8,128)(2,1)} %get-tuple-element.53), channel_id=1, source_target_pairs={{0,8},{8,0},{16,24},{24,16},{1,9},{9,1},{17,25},{25,17},{2,10},{10... | collective-permute-start | bytes 31457288 | tf_op jit(solution)/shard_map/ppermute | solution.py:489
  552.7 52.0 %collective-permute-start.8 = (bf16[96,32,1024]{2,1,0:T(8,128)(2,1)}, bf16[96,32,1024]{2,1,0:T(8,128)(2,1)}, u32[]{:S(2)}, u32[]{:S(2)}) collective-permute-start(bf16[96,32,1024]{2,1,0:T(8,128)(2,1)} %get-tuple-element.56), channel_id=1, source_target_pairs={{0,8},{8,0},{16,24},{24,16},{1,9},{9,1},{17,25},{25,17},{2,10},{10... | collective-permute-start | bytes 18874376 | tf_op jit(solution)/shard_map/ppermute | solution.py:489
  553.2 57.0 %collective-permute-start.7 = (bf16[96,32,1024]{2,1,0:T(8,128)(2,1)}, bf16[96,32,1024]{2,1,0:T(8,128)(2,1)S(1)}, u32[]{:S(2)}, u32[]{:S(2)}) collective-permute-start(bf16[96,32,1024]{2,1,0:T(8,128)(2,1)} %get-tuple-element.55), channel_id=1, source_target_pairs={{0,8},{8,0},{16,24},{24,16},{1,9},{9,1},{17,25},{25,17},{2,10},{10... | collective-permute-start | bytes 18874376 | tf_op jit(solution)/shard_map/ppermute | solution.py:489
  553.2 92.9 %collective-permute-start.4 = (bf16[96,32,1024]{2,1,0:T(8,128)(2,1)}, bf16[96,32,1024]{2,1,0:T(8,128)(2,1)}, u32[]{:S(2)}, u32[]{:S(2)}) collective-permute-start(bf16[96,32,1024]{2,1,0:T(8,128)(2,1)} %get-tuple-element.49), channel_id=1, source_target_pairs={{0,8},{8,0},{16,24},{24,16},{1,9},{9,1},{17,25},{25,17},{2,10},{10... | collective-permute-start | bytes 18874376 | tf_op jit(solution)/shard_map/ppermute | solution.py:489
  618.2 13.1 %copy-start.4 = (bf16[2,10,162,256]{3,2,1,0:T(8,128)(2,1)S(1)}, bf16[2,10,162,256]{3,2,1,0:T(8,128)(2,1)}, u32[]{:S(2)}) copy-start(bf16[2,10,162,256]{3,2,1,0:T(8,128)(2,1)} %copy-done.3) | copy-start | bytes 4976644
  626.4 116.2 %collective-permute-start.11 = (bf16[80,32,1024]{2,1,0:T(8,128)(2,1)}, bf16[80,32,1024]{2,1,0:T(8,128)(2,1)}, u32[]{:S(2)}, u32[]{:S(2)}) collective-permute-start(bf16[80,32,1024]{2,1,0:T(8,128)(2,1)} %sum_blocks.22.refs_2_), channel_id=1, source_target_pairs={{0,1},{1,0},{2,3},{3,2},{4,5},{5,4},{6,7},{7,6},{8,9},{9,8},{10,11... | collective-permute-start | bytes 15728648 | tf_op jit(solution)/shard_map/ppermute | solution.py:489
  629.7 71.2 %collective-permute-start.10 = (bf16[48,32,1024]{2,1,0:T(8,128)(2,1)}, bf16[48,32,1024]{2,1,0:T(8,128)(2,1)S(1)}, u32[]{:S(2)}, u32[]{:S(2)}) collective-permute-start(bf16[48,32,1024]{2,1,0:T(8,128)(2,1)} %sum_blocks.20.refs_2_), channel_id=1, source_target_pairs={{0,2},{1,3},{2,0},{3,1},{4,6},{5,7},{6,4},{7,5},{8,10},{9,11},{10,... | collective-permute-start | bytes 9437192 | tf_op jit(solution)/shard_map/ppermute | solution.py:489
  629.7 77.6 %collective-permute-start.9 = (bf16[48,32,1024]{2,1,0:T(8,128)(2,1)}, bf16[48,32,1024]{2,1,0:T(8,128)(2,1)}, u32[]{:S(2)}, u32[]{:S(2)}) collective-permute-start(bf16[48,32,1024]{2,1,0:T(8,128)(2,1)} %sum_blocks.21.refs_2_), channel_id=1, source_target_pairs={{0,16},{8,24},{16,0},{24,8},{1,17},{9,25},{17,1},{25,9},{2,18},{10... | collective-permute-start | bytes 9437192 | tf_op jit(solution)/shard_map/ppermute | solution.py:489
  645.6 189.4 %collective-permute-start.17 = (bf16[96,32,1024]{2,1,0:T(8,128)(2,1)}, bf16[96,32,1024]{2,1,0:T(8,128)(2,1)}, u32[]{:S(2)}, u32[]{:S(2)}) collective-permute-start(bf16[96,32,1024]{2,1,0:T(8,128)(2,1)} %sum_blocks.23.refs_2_), channel_id=1, source_target_pairs={{0,16},{8,24},{16,0},{24,8},{1,17},{9,25},{17,1},{25,9},{2,18},{10... | collective-permute-start | bytes 18874376 | tf_op jit(solution)/shard_map/ppermute | solution.py:489
  651.6 150.5 %collective-permute-start.16 = (bf16[48,32,1024]{2,1,0:T(8,128)(2,1)}, bf16[48,32,1024]{2,1,0:T(8,128)(2,1)}, u32[]{:S(2)}, u32[]{:S(2)}) collective-permute-start(bf16[48,32,1024]{2,1,0:T(8,128)(2,1)} %sum_blocks.24.after_ref), channel_id=1, source_target_pairs={{0,2},{1,3},{2,0},{3,1},{4,6},{5,7},{6,4},{7,5},{8,10},{9,11},{10,... | collective-permute-start | bytes 9437192 | tf_op jit(solution)/shard_map/ppermute | solution.py:489
  706.0 147.4 %collective-permute-start.15 = (bf16[24,32,1024]{2,1,0:T(8,128)(2,1)}, bf16[24,32,1024]{2,1,0:T(8,128)(2,1)}, u32[]{:S(2)}, u32[]{:S(2)}) collective-permute-start(bf16[24,32,1024]{2,1,0:T(8,128)(2,1)} %sum_blocks.25.refs_3_), channel_id=1, source_target_pairs={{0,4},{1,5},{2,6},{3,7},{4,0},{5,1},{6,2},{7,3},{8,12},{9,13},{10,... | collective-permute-start | bytes 4718600 | tf_op jit(solution)/shard_map/ppermute | solution.py:489
  734.6 124.6 %collective-permute-start.14 = (bf16[24,32,1024]{2,1,0:T(8,128)(2,1)}, bf16[24,32,1024]{2,1,0:T(8,128)(2,1)S(1)}, u32[]{:S(2)}, u32[]{:S(2)}) collective-permute-start(bf16[24,32,1024]{2,1,0:T(8,128)(2,1)} %sum_blocks.26.after_ref), channel_id=1, source_target_pairs={{0,1},{1,0},{2,3},{3,2},{4,5},{5,4},{6,7},{7,6},{8,9},{9,8},{10,11... | collective-permute-start | bytes 4718600 | tf_op jit(solution)/shard_map/ppermute | solution.py:489
  748.0 139.3 %collective-permute-start.20 = (bf16[40,32,1024]{2,1,0:T(8,128)(2,1)}, bf16[40,32,1024]{2,1,0:T(8,128)(2,1)}, u32[]{:S(2)}, u32[]{:S(2)}) collective-permute-start(bf16[40,32,1024]{2,1,0:T(8,128)(2,1)} %sum_blocks.27.after_ref), channel_id=1, source_target_pairs={{0,2},{1,3},{2,0},{3,1},{4,6},{5,7},{6,4},{7,5},{8,10},{9,11},{10,... | collective-permute-start | bytes 7864328 | tf_op jit(solution)/shard_map/ppermute | solution.py:489
  791.5 44.8 %copy-start.33 = (bf16[256,1024]{1,0:T(8,128)(2,1)S(1)}, bf16[256,1024]{1,0:T(8,128)(2,1)}, u32[]{:S(2)}) copy-start(bf16[256,1024]{1,0:T(8,128)(2,1)} %copy-done.32) | copy-start | bytes 1572868
  791.5 44.8 %copy-start.57 = (bf16[256,81]{0,1:T(8,128)(2,1)S(1)}, bf16[256,81]{0,1:T(8,128)(2,1)}, u32[]{:S(2)}) copy-start(bf16[256,81]{0,1:T(8,128)(2,1)} %copy-done.56) | copy-start | bytes 124420
  791.5 44.8 %copy-start.81 = (bf16[256,4]{0,1:T(4,128)(2,1)S(1)}, bf16[256,4]{0,1:T(4,128)(2,1)}, u32[]{:S(2)}) copy-start(bf16[256,4]{0,1:T(4,128)(2,1)} %copy-done.80) | copy-start | bytes 6148
  791.5 45.1 %copy-start.31 = (bf16[256,1024]{1,0:T(8,128)(2,1)S(1)}, bf16[256,1024]{1,0:T(8,128)(2,1)}, u32[]{:S(2)}) copy-start(bf16[256,1024]{1,0:T(8,128)(2,1)} %copy-done.30) | copy-start | bytes 1572868
  791.5 45.1 %copy-start.59 = (bf16[256,81]{0,1:T(8,128)(2,1)S(1)}, bf16[256,81]{0,1:T(8,128)(2,1)}, u32[]{:S(2)}) copy-start(bf16[256,81]{0,1:T(8,128)(2,1)} %copy-done.58) | copy-start | bytes 124420
  791.5 45.1 %copy-start.83 = (bf16[256,4]{0,1:T(4,128)(2,1)S(1)}, bf16[256,4]{0,1:T(4,128)(2,1)}, u32[]{:S(2)}) copy-start(bf16[256,4]{0,1:T(4,128)(2,1)} %copy-done.82) | copy-start | bytes 6148
  791.5 45.3 %copy-start.29 = (bf16[256,1024]{1,0:T(8,128)(2,1)S(1)}, bf16[256,1024]{1,0:T(8,128)(2,1)}, u32[]{:S(2)}) copy-start(bf16[256,1024]{1,0:T(8,128)(2,1)} %copy-done.28) | copy-start | bytes 1572868
  791.5 45.3 %copy-start.55 = (bf16[256,81]{0,1:T(8,128)(2,1)S(1)}, bf16[256,81]{0,1:T(8,128)(2,1)}, u32[]{:S(2)}) copy-start(bf16[256,81]{0,1:T(8,128)(2,1)} %copy-done.54) | copy-start | bytes 124420
  791.5 45.3 %copy-start.79 = (bf16[256,4]{0,1:T(4,128)(2,1)S(1)}, bf16[256,4]{0,1:T(4,128)(2,1)}, u32[]{:S(2)}) copy-start(bf16[256,4]{0,1:T(4,128)(2,1)} %copy-done.78) | copy-start | bytes 6148
  802.1 63.4 %collective-permute-start.12 = (bf16[2,3,160,256]{3,2,1,0:T(8,128)(2,1)}, bf16[2,3,160,256]{3,2,1,0:T(8,128)(2,1)S(1)}, u32[]{:S(2)}, u32[]{:S(2)}) collective-permute-start(bf16[2,3,160,256]{3,2,1,0:T(8,128)(2,1)} %get-tuple-element.104), channel_id=1, source_target_pairs={{0,1},{1,2},{2,3},{3,4},{4,5},{5,6},{6,7},{8,9},{9,10},{10,11},{11... | collective-permute-start | bytes 1474568 | tf_op jit(solution)/shard_map/ppermute | solution.py:1106
  835.0 32.2 %collective-permute-start.13 = (bf16[2,3,160,256]{3,2,1,0:T(8,128)(2,1)}, bf16[2,3,160,256]{3,2,1,0:T(8,128)(2,1)}, u32[]{:S(2)}, u32[]{:S(2)}) collective-permute-start(bf16[2,3,160,256]{3,2,1,0:T(8,128)(2,1)} %get-tuple-element.103), channel_id=1, source_target_pairs={{1,0},{2,1},{3,2},{4,3},{5,4},{6,5},{7,6},{9,8},{10,9},{11,10},{12... | collective-permute-start | bytes 1474568 | tf_op jit(solution)/shard_map/ppermute | solution.py:1107
  853.5 80.0 %collective-permute-start.19 = (bf16[48,32,1024]{2,1,0:T(8,128)(2,1)}, bf16[48,32,1024]{2,1,0:T(8,128)(2,1)S(1)}, u32[]{:S(2)}, u32[]{:S(2)}) collective-permute-start(bf16[48,32,1024]{2,1,0:T(8,128)(2,1)} %sum_blocks.28.refs_3_), channel_id=1, source_target_pairs={{0,1},{1,0},{2,3},{3,2},{4,5},{5,4},{6,7},{7,6},{8,9},{9,8},{10,11... | collective-permute-start | bytes 9437192 | tf_op jit(solution)/shard_map/ppermute | solution.py:489
  859.2 84.7 %collective-permute-start.18 = (bf16[24,32,1024]{2,1,0:T(8,128)(2,1)}, bf16[24,32,1024]{2,1,0:T(8,128)(2,1)}, u32[]{:S(2)}, u32[]{:S(2)}) collective-permute-start(bf16[24,32,1024]{2,1,0:T(8,128)(2,1)} %sum_blocks.29.refs_4_), channel_id=1, source_target_pairs={{0,4},{1,5},{2,6},{3,7},{4,0},{5,1},{6,2},{7,3},{8,12},{9,13},{10,... | collective-permute-start | bytes 4718600 | tf_op jit(solution)/shard_map/ppermute | solution.py:489
  865.5 8.6 copy-start.53
  865.5 87.7 %collective-permute-start.25 = (bf16[12,32,1024]{2,1,0:T(8,128)(2,1)}, bf16[12,32,1024]{2,1,0:T(8,128)(2,1)}, u32[]{:S(2)}, u32[]{:S(2)}) collective-permute-start(bf16[12,32,1024]{2,1,0:T(8,128)(2,1)} %sum_blocks.30.refs_4_), channel_id=1, source_target_pairs={{0,16},{8,24},{16,0},{24,8},{1,17},{9,25},{17,1},{25,9},{2,18},{10... | collective-permute-start | bytes 2359304 | tf_op jit(solution)/shard_map/ppermute | solution.py:489
  867.2 89.9 %collective-permute-start.24 = (bf16[12,32,1024]{2,1,0:T(8,128)(2,1)}, bf16[12,32,1024]{2,1,0:T(8,128)(2,1)}, u32[]{:S(2)}, u32[]{:S(2)}) collective-permute-start(bf16[12,32,1024]{2,1,0:T(8,128)(2,1)} %sum_blocks.31.after_ref), channel_id=1, source_target_pairs={{0,2},{1,3},{2,0},{3,1},{4,6},{5,7},{6,4},{7,5},{8,10},{9,11},{10,... | collective-permute-start | bytes 2359304 | tf_op jit(solution)/shard_map/ppermute | solution.py:489
  891.0 71.4 %collective-permute-start.23 = (bf16[20,32,1024]{2,1,0:T(8,128)(2,1)}, bf16[20,32,1024]{2,1,0:T(8,128)(2,1)}, u32[]{:S(2)}, u32[]{:S(2)}) collective-permute-start(bf16[20,32,1024]{2,1,0:T(8,128)(2,1)} %sum_blocks.32.refs_4_), channel_id=1, source_target_pairs={{0,16},{8,24},{16,0},{24,8},{1,17},{9,25},{17,1},{25,9},{2,18},{10... | collective-permute-start | bytes 3932168 | tf_op jit(solution)/shard_map/ppermute | solution.py:489
  939.4 52.4 %collective-permute-start.22 = (bf16[24,32,1024]{2,1,0:T(8,128)(2,1)}, bf16[24,32,1024]{2,1,0:T(8,128)(2,1)}, u32[]{:S(2)}, u32[]{:S(2)}) collective-permute-start(bf16[24,32,1024]{2,1,0:T(8,128)(2,1)} %sum_blocks.33.refs_4_), channel_id=1, source_target_pairs={{0,2},{1,3},{2,0},{3,1},{4,6},{5,7},{6,4},{7,5},{8,10},{9,11},{10,... | collective-permute-start | bytes 4718600 | tf_op jit(solution)/shard_map/ppermute | solution.py:489
  947.0 49.3 %collective-permute-start.21 = (bf16[12,32,1024]{2,1,0:T(8,128)(2,1)}, bf16[12,32,1024]{2,1,0:T(8,128)(2,1)}, u32[]{:S(2)}, u32[]{:S(2)}) collective-permute-start(bf16[12,32,1024]{2,1,0:T(8,128)(2,1)} %sum_blocks.34.refs_5_), channel_id=1, source_target_pairs={{0,1},{1,0},{2,3},{3,2},{4,5},{5,4},{6,7},{7,6},{8,9},{9,8},{10,11... | collective-permute-start | bytes 2359304 | tf_op jit(solution)/shard_map/ppermute | solution.py:489
  955.7 130.9 %collective-permute-start.30 = (bf16[6,32,1024]{2,1,0:T(8,128)(2,1)}, bf16[6,32,1024]{2,1,0:T(8,128)(2,1)}, u32[]{:S(2)}, u32[]{:S(2)}) collective-permute-start(bf16[6,32,1024]{2,1,0:T(8,128)(2,1)} %sum_blocks.35.refs_5_), channel_id=1, source_target_pairs={{0,1},{1,0},{2,3},{3,2},{4,5},{5,4},{6,7},{7,6},{8,9},{9,8},{10,11... | collective-permute-start | bytes 1179656 | tf_op jit(solution)/shard_map/ppermute | solution.py:489
  959.6 131.9 %collective-permute-start.29 = (bf16[6,32,1024]{2,1,0:T(8,128)(2,1)}, bf16[6,32,1024]{2,1,0:T(8,128)(2,1)}, u32[]{:S(2)}, u32[]{:S(2)}) collective-permute-start(bf16[6,32,1024]{2,1,0:T(8,128)(2,1)} %sum_blocks.36.refs_5_), channel_id=1, source_target_pairs={{0,4},{1,5},{2,6},{3,7},{4,0},{5,1},{6,2},{7,3},{8,12},{9,13},{10,... | collective-permute-start | bytes 1179656 | tf_op jit(solution)/shard_map/ppermute | solution.py:489
  965.5 130.9 %collective-permute-start.28 = (bf16[10,32,1024]{2,1,0:T(8,128)(2,1)}, bf16[10,32,1024]{2,1,0:T(8,128)(2,1)S(1)}, u32[]{:S(2)}, u32[]{:S(2)}) collective-permute-start(bf16[10,32,1024]{2,1,0:T(8,128)(2,1)} %sum_blocks.37.refs_5_), channel_id=1, source_target_pairs={{0,4},{1,5},{2,6},{3,7},{4,0},{5,1},{6,2},{7,3},{8,12},{9,13},{10,... | collective-permute-start | bytes 1966088 | tf_op jit(solution)/shard_map/ppermute | solution.py:489
  995.3 112.8 %collective-permute-start.27 = (bf16[12,32,1024]{2,1,0:T(8,128)(2,1)}, bf16[12,32,1024]{2,1,0:T(8,128)(2,1)}, u32[]{:S(2)}, u32[]{:S(2)}) collective-permute-start(bf16[12,32,1024]{2,1,0:T(8,128)(2,1)} %sum_blocks.38.refs_5_), channel_id=1, source_target_pairs={{0,4},{1,5},{2,6},{3,7},{4,0},{5,1},{6,2},{7,3},{8,12},{9,13},{10,... | collective-permute-start | bytes 2359304 | tf_op jit(solution)/shard_map/ppermute | solution.py:489
  996.3 82.6 %copy-start.26 = (f32[2560,256]{1,0:T(8,128)S(1)}, f32[2560,256]{1,0:T(8,128)}, u32[]{:S(2)}) copy-start(f32[2560,256]{1,0:T(8,128)} %param.26) | copy-start | bytes 7864324
  998.9 116.9 %collective-permute-start.26 = (bf16[6,32,1024]{2,1,0:T(8,128)(2,1)}, bf16[6,32,1024]{2,1,0:T(8,128)(2,1)}, u32[]{:S(2)}, u32[]{:S(2)}) collective-permute-start(bf16[6,32,1024]{2,1,0:T(8,128)(2,1)} %sum_blocks.39.refs_4_), channel_id=1, source_target_pairs={{0,16},{8,24},{16,0},{24,8},{1,17},{9,25},{17,1},{25,9},{2,18},{10... | collective-permute-start | bytes 1179656 | tf_op jit(solution)/shard_map/ppermute | solution.py:489
  1000.4 78.5 %copy-start.25 = (f32[2560,256]{1,0:T(8,128)S(1)}, f32[2560,256]{1,0:T(8,128)}, u32[]{:S(2)}) copy-start(f32[2560,256]{1,0:T(8,128)} %param.25) | copy-start | bytes 7864324
  1097.3 7.8 copy-start.64
  1097.3 7.8 copy-start.66
  1097.3 7.8 copy-start.70
  1097.3 7.8 copy-start.71
  1097.3 8.5 copy-start.23
  1097.3 8.5 copy-start.24
  1097.3 8.5 copy-start.50
  1097.3 8.5 copy-start.51
  (79 other events, 222.1 us)
Sparse Core Ops, SparseCore 0:
  12.8 173.4 all-gather.1
